TPU v7x, 256 devices: a whole 4x4x8 slice. The times are simulated.
256 devices in a mesh: gx: 8 (over z), gy: 32 (over y, x, core).
Axes of the slice: x: 4, y: 4, z: 8, core: 2. Of those that a mesh axis runs over, the one named last changes fastest.
Arguments:
- source: float32 [64, 1024, 256], P('gx', 'gy'), may hold values from -4 to 4
- material: int32 [64, 1024, 256], P('gx', 'gy'), may hold values from 0 to 2
- boundary_flags: int32 [64, 1024, 256], P('gx', 'gy'), may hold values 0 or 1
Outputs:
- pressure: float32 [64, 1024, 256], P('gx', 'gy')
- residual: float32 [64, 1024, 256], P('gx', 'gy')
All inputs are finite; a program needn't handle non-finite values. No bound on the sum of `boundary_flags` on one device may be relied on, other than what follows from the above.
Results may differ from a plain program's by a relative error of at most 0.0003.
Values sent between devices are 32-bit elements; how exact they have to be, the bound alone decides.
No kernel may reach another device: no remote copies, remote signals or barrier semaphores. Data moves between devices by JAX's collectives and lax.ppermute only.
A program may use at most 128 MiB of HBM per device.

v0:
```python
import jax
import jax.numpy as jnp
from jax import lax
from jax.sharding import PartitionSpec as P

FINE_LEVELS = 3
PRE_SWEEPS = 3
POST_SWEEPS = 2
COARSE_SWEEPS = 8


OMEGA = 0.8
SHIFT = 0.001
ROBIN = 2.0
INVERSE_SOLID = 1.0 / 3.0
INVERSE_DENSE = 0.125


def padded_2(block, sides, width):
    for axis, dim in sides:
        count = lax.axis_size(axis)
        forward = [(i, i + 1) for i in range(count - 1)]
        backward = [(target, source) for source, target in forward]
        low = lax.ppermute(
            lax.slice_in_dim(block, block.shape[dim] - width, None, axis=dim), axis, forward
        )
        high = lax.ppermute(lax.slice_in_dim(block, 0, width, axis=dim), axis, backward)
        block = jnp.concatenate([low, block, high], axis=dim)
    return block


def coefficients(material, boundary_flags):
    inverse = jnp.where(
        material == 0, 1.0, jnp.where(material == 1, INVERSE_SOLID, INVERSE_DENSE)
    ).astype(jnp.float32)
    reaction = SHIFT + ROBIN * boundary_flags.astype(jnp.float32)
    return jnp.stack([inverse, reaction])


def harmonic(former, latter):
    summed = former + latter
    return 2.0 * former * latter / jnp.where(summed > 0, summed, 1.0)


def prepare(padded, scaling, rim_width):
    inverse = padded[0]
    reaction = padded[1]
    faces_x = harmonic(inverse[1:], inverse[:-1])
    faces_y = harmonic(inverse[:, 1:], inverse[:, :-1])
    faces_z = harmonic(inverse[:, :, 1:], inverse[:, :, :-1])
    summed = faces_x[1:, 1:-1, 1:-1] + faces_x[:-1, 1:-1, 1:-1]
    summed = summed + faces_y[1:-1, 1:, 1:-1] + faces_y[1:-1, :-1, 1:-1]
    summed = summed + faces_z[1:-1, 1:-1, 1:] + faces_z[1:-1, 1:-1, :-1]
    diagonal = scaling * summed + reaction[1:-1, 1:-1, 1:-1]
    diagonal = jnp.where(diagonal > 0, diagonal, 1.0)
    return (faces_x, faces_y, faces_z, reaction, diagonal, scaling, rim_width)


def operate(padded, stencil):
    faces_x, faces_y, faces_z, reaction, diagonal, scaling, rim_width = stencil
    center = padded[1:-1, 1:-1, 1:-1]
    fluxes = faces_x[1:, 1:-1, 1:-1] * (center - padded[2:, 1:-1, 1:-1])
    fluxes = fluxes + faces_x[:-1, 1:-1, 1:-1] * (center - padded[:-2, 1:-1, 1:-1])
    fluxes = fluxes + faces_y[1:-1, 1:, 1:-1] * (center - padded[1:-1, 2:, 1:-1])
    fluxes = fluxes + faces_y[1:-1, :-1, 1:-1] * (center - padded[1:-1, :-2, 1:-1])
    fluxes = fluxes + faces_z[1:-1, 1:-1, 1:] * (center - padded[1:-1, 1:-1, 2:])
    fluxes = fluxes + faces_z[1:-1, 1:-1, :-1] * (center - padded[1:-1, 1:-1, :-2])
    return scaling * fluxes + reaction[1:-1, 1:-1, 1:-1] * center


def relax(padded, source_now, stencil):
    applied = operate(padded, stencil)
    diagonal = stencil[4]
    return padded[1:-1, 1:-1, 1:-1] + OMEGA * (source_now - applied) / diagonal


def start_field(source_now, stencil):
    return OMEGA * source_now / stencil[4]


def coarsen(array):
    shape = array.shape
    lead = shape[:-3]
    blocks = array.reshape(lead + (shape[-3] // 2, 2, shape[-2] // 2, 2, shape[-1] // 2, 2))
    return jnp.mean(blocks, axis=(-5, -3, -1))


def refine(array):
    return jnp.repeat(jnp.repeat(jnp.repeat(array, 2, axis=0), 2, axis=1), 2, axis=2)


def pad_depth(array, rim_width):
    widths = [(0, 0)] * (array.ndim - 1) + [(rim_width, rim_width)]
    return jnp.pad(array, widths)


def single_rims(pressure):
    return pad_depth(padded_2(pressure, (("gx", 0), ("gy", 1)), 1), 1)


def residual_rims(pressure):
    return pad_depth(padded_2(pressure, (("gx", 0), ("gy", 1)), 1), 1)


def smooth(pressure, source_now, stencil, remaining):
    for repeat in range(remaining):
        pressure = relax(single_rims(pressure), source_now, stencil)
    return pressure


def coarse_solve(current, coef, scaling):
    padded_coef = pad_depth(padded_2(coef, (("gx", 1), ("gy", 2)), 1), 1)
    stencil = prepare(padded_coef, scaling, 1)
    correction = start_field(current, stencil)
    for repeat in range(COARSE_SWEEPS - 1):
        padded = pad_depth(padded_2(correction, (("gx", 0), ("gy", 1)), 1), 1)
        correction = relax(padded, current, stencil)
    return correction


def per_device(source, material, boundary_flags):
    rim_width = 1
    coef = coefficients(material, boundary_flags)
    saved = []
    current = source
    for level_index in range(FINE_LEVELS):
        padded_coef = padded_2(coef, (("gx", 1), ("gy", 2)), rim_width)
        stencil = prepare(pad_depth(padded_coef, rim_width), 0.25**level_index, rim_width)
        source_wide = None
        pressure = start_field(current, stencil)
        pressure = smooth(pressure, current, stencil, PRE_SWEEPS - 1)
        residue = current - operate(residual_rims(pressure), stencil)
        saved.append((pressure, current, source_wide, stencil))
        current = coarsen(residue)
        coef = coarsen(coef)
    correction = coarse_solve(current, coef, 0.25**FINE_LEVELS)
    for level_index in reversed(range(FINE_LEVELS)):
        pressure, current, source_wide, stencil = saved[level_index]
        pressure = pressure + refine(correction)
        pressure = smooth(pressure, current, stencil, POST_SWEEPS)
        correction = pressure
    residual = source - operate(residual_rims(correction), saved[0][3])
    return (correction, residual)


def solution(mesh):
    return jax.shard_map(
        per_device,
        mesh=mesh,
        in_specs=(P("gx", "gy", None), P("gx", "gy", None), P("gx", "gy", None)),
        out_specs=(P("gx", "gy", None), P("gx", "gy", None)),
        check_vma=False,
    )
```

profile of v0, /device:TPU:7, one launch (start us, length us, event | category | flops | bytes accessed | tf_op | source)
XLA Modules:
  0.0 598.1 jit_solution(5693758933715185931)
XLA Ops:
  6.7 18.1 %stack.19 = f32[1,4,2,16,2,128,2]{6,5,4,3,2,1,0:T(8,128)} reshape(f32[8,32,256]{2,1,0:T(8,128)S(1)} %get-tuple-element.40) | data formatting | bytes 524288 | tf_op jit(solution)/shard_map/stack | solution.py:37
  24.8 18.1 %stack.18 = f32[1,4,2,16,2,128,2]{6,5,4,3,2,1,0:T(8,128)} reshape(f32[8,32,256]{2,1,0:T(8,128)S(1)} %get-tuple-element.119) | data formatting | bytes 524288 | tf_op jit(solution)/shard_map/stack | solution.py:37
  42.8 12.8 %maximum_reduce_fusion = f32[2,4,16,128]{3,2,1,0:T(8,128)S(1)} fusion(f32[1,4,2,16,2,128,2]{6,5,4,3,2,1,0:T(8,128)} %stack.19, f32[1,4,2,16,2,128,2]{6,5,4,3,2,1,0:T(8,128)} %stack.18), kind=kLoop, calls=%fused_computation | loop fusion | flops 245760 | bytes 589824 | tf_op jit(solution)/shard_map/reduce_sum | solution.py:85
  61.1 5.5 div.163
  80.7 5.8 collective-permute-start.18
  95.8 6.0 collective-permute-start.48
  132.6 5.1 collective-permute-done.10
  159.3 18.8 %reshape.88 = f32[4,2,16,2,128,2]{5,4,3,2,1,0:T(8,128)} reshape(f32[8,32,256]{2,1,0:T(8,128)} %fusion.66) | data formatting | bytes 524288 | tf_op jit(solution)/shard_map/reshape | solution.py:84
  178.1 7.0 %reduce_sum.68 = f32[4,16,128]{2,1,0:T(8,128)S(1)} reduce(f32[4,2,16,2,128,2]{5,4,3,2,1,0:T(8,128)} %reshape.88, f32[]{:T(128)} %constant.21.clone.1), dimensions={1,3,5}, to_apply=%region_0.1 | reduce | flops 57344 | bytes 294916 | tf_op jit(solution)/shard_map/reduce_sum | solution.py:85
  196.0 5.8 collective-permute-start.23
  266.0 5.6 collective-permute-start.39
  334.8 5.1 collective-permute-done.54
  354.1 5.1 collective-permute-done.58
  372.6 5.1 collective-permute-done.62
  391.1 5.1 collective-permute-done.66
  409.6 5.1 collective-permute-done.70
  428.1 5.1 collective-permute-done.74
  446.7 5.1 collective-permute-done.78
  468.8 5.1 collective-permute-done.82
  487.4 5.1 collective-permute-done.86
  530.3 5.1 collective-permute-done.94
  553.1 5.2 collective-permute-done.98
  572.2 5.2 collective-permute-done.102
  591.2 5.2 collective-permute-done.106
  (359 shorter events, 420.7 us)
Async XLA Ops:
  1.8 69.2 %collective-permute-start = (f32[2,1,32,256]{3,2,1,0:T(8,128)S(1)}, f32[2,1,32,256]{3,2,1,0:T(8,128)S(1)}, u32[]{:S(2)}, u32[]{:S(2)}) collective-permute-start(f32[2,1,32,256]{3,2,1,0:T(8,128)S(1)} %get-tuple-element.16), channel_id=1, source_target_pairs={{0,32},{32,64},{64,96},{96,128},{128,160},{160,192},{192,224},{1,3... | collective-permute-start | bytes 196616 | tf_op jit(solution)/shard_map/ppermute | solution.py:24
  5.4 65.6 %collective-permute-start.1 = (f32[2,1,32,256]{3,2,1,0:T(8,128)S(1)}, f32[2,1,32,256]{3,2,1,0:T(8,128)S(1)}, u32[]{:S(2)}, u32[]{:S(2)}) collective-permute-start(f32[2,1,32,256]{3,2,1,0:T(8,128)S(1)} %get-tuple-element.17), channel_id=1, source_target_pairs={{32,0},{64,32},{96,64},{128,96},{160,128},{192,160},{224,192},{33,... | collective-permute-start | bytes 196616 | tf_op jit(solution)/shard_map/ppermute | solution.py:27
  55.7 23.1 %collective-permute-start.16 = (f32[2,1,16,128]{3,2,1,0:T(8,128)S(1)}, f32[2,1,16,128]{3,2,1,0:T(8,128)S(1)}, u32[]{:S(2)}, u32[]{:S(2)}) collective-permute-start(f32[2,1,16,128]{3,2,1,0:T(8,128)S(1)} %get-tuple-element.52), channel_id=1, source_target_pairs={{0,32},{32,64},{64,96},{96,128},{128,160},{160,192},{192,224},{1,3... | collective-permute-start | bytes 49160 | tf_op jit(solution)/shard_map/ppermute | solution.py:24
  59.8 18.9 %collective-permute-start.17 = (f32[2,1,16,128]{3,2,1,0:T(8,128)S(1)}, f32[2,1,16,128]{3,2,1,0:T(8,128)S(1)}, u32[]{:S(2)}, u32[]{:S(2)}) collective-permute-start(f32[2,1,16,128]{3,2,1,0:T(8,128)S(1)} %get-tuple-element.53), channel_id=1, source_target_pairs={{32,0},{64,32},{96,64},{128,96},{160,128},{192,160},{224,192},{33,... | collective-permute-start | bytes 49160 | tf_op jit(solution)/shard_map/ppermute | solution.py:27
  69.7 191.2 %collective-permute-start.49 = (f32[2,1,4,32]{3,2,1,0:T(4,128)S(1)}, f32[2,1,4,32]{3,2,1,0:T(4,128)}, u32[]{:S(2)}, u32[]{:S(2)}) collective-permute-start(f32[2,1,4,32]{3,2,1,0:T(4,128)S(1)} %multiply_bitcast_fusion), channel_id=1, source_target_pairs={{32,0},{64,32},{96,64},{128,96},{160,128},{192,160},{224,192},{33,... | collective-permute-start | bytes 3080 | tf_op jit(solution)/shard_map/ppermute | solution.py:27
  71.1 15.4 %collective-permute-start.3 = (f32[2,10,1,256]{3,0,2,1:T(2,128)S(1)}, f32[2,10,1,256]{3,0,2,1:T(2,128)S(1)}, u32[]{:S(2)}, u32[]{:S(2)}) collective-permute-start(f32[2,10,1,256]{3,0,2,1:T(2,128)S(1)} %copy.260), channel_id=1, source_target_pairs={{1,0},{2,1},{3,2},{4,3},{5,4},{6,5},{7,6},{8,7},{9,8},{10,9},{11,1... | collective-permute-start | bytes 61448 | tf_op jit(solution)/shard_map/ppermute | solution.py:27
  74.3 12.2 %collective-permute-start.2 = (f32[2,10,1,256]{3,0,2,1:T(2,128)S(1)}, f32[2,10,1,256]{3,0,2,1:T(2,128)S(1)}, u32[]{:S(2)}, u32[]{:S(2)}) collective-permute-start(f32[2,10,1,256]{3,0,2,1:T(2,128)S(1)} %copy.259), channel_id=1, source_target_pairs={{0,1},{1,2},{2,3},{3,4},{4,5},{5,6},{6,7},{7,8},{8,9},{9,10},{10,1... | collective-permute-start | bytes 61448 | tf_op jit(solution)/shard_map/ppermute | solution.py:24
  78.8 17.0 %collective-permute-start.19 = (f32[2,6,1,128]{3,0,2,1:T(2,128)S(1)}, f32[2,6,1,128]{3,0,2,1:T(2,128)S(1)}, u32[]{:S(2)}, u32[]{:S(2)}) collective-permute-start(f32[2,6,1,128]{3,0,2,1:T(2,128)S(1)} %copy.262), channel_id=1, source_target_pairs={{1,0},{2,1},{3,2},{4,3},{5,4},{6,5},{7,6},{8,7},{9,8},{10,9},{11,1... | collective-permute-start | bytes 18440 | tf_op jit(solution)/shard_map/ppermute | solution.py:27
  80.7 21.0 %collective-permute-start.18 = (f32[2,6,1,128]{3,0,2,1:T(2,128)S(1)}, f32[2,6,1,128]{3,0,2,1:T(2,128)S(1)}, u32[]{:S(2)}, u32[]{:S(2)}) collective-permute-start(f32[2,6,1,128]{3,0,2,1:T(2,128)S(1)} %copy.261), channel_id=1, source_target_pairs={{0,1},{1,2},{2,3},{3,4},{4,5},{5,6},{6,7},{7,8},{8,9},{9,10},{10,1... | collective-permute-start | bytes 18440 | tf_op jit(solution)/shard_map/ppermute | solution.py:24
  89.1 17.3 %collective-permute-start.5 = (f32[1,32,256]{2,1,0:T(8,128)S(1)}, f32[1,32,256]{2,1,0:T(8,128)S(1)}, u32[]{:S(2)}, u32[]{:S(2)}) collective-permute-start(f32[1,32,256]{2,1,0:T(8,128)S(1)} %get-tuple-element.46), channel_id=1, source_target_pairs={{0,32},{32,64},{64,96},{96,128},{128,160},{160,192},{192,224},{1,3... | collective-permute-start | bytes 98312 | tf_op jit(solution)/shard_map/ppermute | solution.py:24
  93.9 12.5 %collective-permute-start.4 = (f32[1,32,256]{2,1,0:T(8,128)S(1)}, f32[1,32,256]{2,1,0:T(8,128)S(1)}, u32[]{:S(2)}, u32[]{:S(2)}) collective-permute-start(f32[1,32,256]{2,1,0:T(8,128)S(1)} %get-tuple-element.47), channel_id=1, source_target_pairs={{32,0},{64,32},{96,64},{128,96},{160,128},{192,160},{224,192},{33,... | collective-permute-start | bytes 98312 | tf_op jit(solution)/shard_map/ppermute | solution.py:27
  95.8 165.1 %collective-permute-start.48 = (f32[2,1,4,32]{3,2,1,0:T(4,128)S(1)}, f32[2,1,4,32]{3,2,1,0:T(4,128)}, u32[]{:S(2)}, u32[]{:S(2)}) collective-permute-start(f32[2,1,4,32]{3,2,1,0:T(4,128)S(1)} %multiply_bitcast_fusion), channel_id=1, source_target_pairs={{0,32},{32,64},{64,96},{96,128},{128,160},{160,192},{192,224},{1,3... | collective-permute-start | bytes 3080 | tf_op jit(solution)/shard_map/ppermute | solution.py:24
  101.8 85.6 %collective-permute-start.32 = (f32[2,1,8,64]{3,2,1,0:T(8,128)}, f32[2,1,8,64]{3,2,1,0:T(8,128)}, u32[]{:S(2)}, u32[]{:S(2)}) collective-permute-start(f32[2,1,8,64]{3,2,1,0:T(8,128)} %get-tuple-element.90), channel_id=1, source_target_pairs={{0,32},{32,64},{64,96},{96,128},{128,160},{160,192},{192,224},{1,3... | collective-permute-start | bytes 12296 | tf_op jit(solution)/shard_map/ppermute | solution.py:24
  109.2 7.1 %collective-permute-start.6 = (f32[10,1,256]{2,1,0:T(1,128)S(1)}, f32[10,1,256]{2,1,0:T(1,128)S(1)}, u32[]{:S(2)}, u32[]{:S(2)}) collective-permute-start(f32[10,1,256]{2,1,0:T(1,128)S(1)} %get-tuple-element.29), channel_id=1, source_target_pairs={{1,0},{2,1},{3,2},{4,3},{5,4},{6,5},{7,6},{8,7},{9,8},{10,9},{11,1... | collective-permute-start | bytes 30728 | tf_op jit(solution)/shard_map/ppermute | solution.py:27
  152.5 36.2 %collective-permute-start.33 = (f32[2,1,8,64]{3,2,1,0:T(8,128)}, f32[2,1,8,64]{3,2,1,0:T(8,128)}, u32[]{:S(2)}, u32[]{:S(2)}) collective-permute-start(f32[2,1,8,64]{3,2,1,0:T(8,128)} %get-tuple-element.91), channel_id=1, source_target_pairs={{32,0},{64,32},{96,64},{128,96},{160,128},{192,160},{224,192},{33,... | collective-permute-start | bytes 12296 | tf_op jit(solution)/shard_map/ppermute | solution.py:27
  185.2 8.8 %collective-permute-start.21 = (f32[1,16,128]{2,1,0:T(8,128)S(1)}, f32[1,16,128]{2,1,0:T(8,128)S(1)}, u32[]{:S(2)}, u32[]{:S(2)}) collective-permute-start(f32[1,16,128]{2,1,0:T(8,128)S(1)} %get-tuple-element.74), channel_id=1, source_target_pairs={{0,32},{32,64},{64,96},{96,128},{128,160},{160,192},{192,224},{1,3... | collective-permute-start | bytes 24584 | tf_op jit(solution)/shard_map/ppermute | solution.py:24
  187.4 8.6 %collective-permute-start.20 = (f32[1,16,128]{2,1,0:T(8,128)S(1)}, f32[1,16,128]{2,1,0:T(8,128)S(1)}, u32[]{:S(2)}, u32[]{:S(2)}) collective-permute-start(f32[1,16,128]{2,1,0:T(8,128)S(1)} %get-tuple-element.75), channel_id=1, source_target_pairs={{32,0},{64,32},{96,64},{128,96},{160,128},{192,160},{224,192},{33,... | collective-permute-start | bytes 24584 | tf_op jit(solution)/shard_map/ppermute | solution.py:27
  189.5 12.3 %collective-permute-start.34 = (f32[2,4,1,64]{3,2,1,0:T(1,128)S(1)}, f32[2,4,1,64]{3,2,1,0:T(1,128)S(1)}, u32[]{:S(2)}, u32[]{:S(2)}) collective-permute-start(f32[2,4,1,64]{3,2,1,0:T(1,128)S(1)} %get-tuple-element.68), channel_id=1, source_target_pairs={{0,1},{1,2},{2,3},{3,4},{4,5},{5,6},{6,7},{7,8},{8,9},{9,10},{10,1... | collective-permute-start | bytes 6152 | tf_op jit(solution)/shard_map/ppermute | solution.py:24
  194.1 9.7 %collective-permute-start.35 = (f32[2,4,1,64]{3,2,1,0:T(1,128)S(1)}, f32[2,4,1,64]{3,2,1,0:T(1,128)S(1)}, u32[]{:S(2)}, u32[]{:S(2)}) collective-permute-start(f32[2,4,1,64]{3,2,1,0:T(1,128)S(1)} %get-tuple-element.69), channel_id=1, source_target_pairs={{1,0},{2,1},{3,2},{4,3},{5,4},{6,5},{7,6},{8,7},{9,8},{10,9},{11,1... | collective-permute-start | bytes 6152 | tf_op jit(solution)/shard_map/ppermute | solution.py:27
  196.0 8.6 %collective-permute-start.23 = (f32[6,1,128]{2,1,0:T(1,128)S(1)}, f32[6,1,128]{2,1,0:T(1,128)S(1)}, u32[]{:S(2)}, u32[]{:S(2)}) collective-permute-start(f32[6,1,128]{2,1,0:T(1,128)S(1)} %get-tuple-element.62), channel_id=1, source_target_pairs={{0,1},{1,2},{2,3},{3,4},{4,5},{5,6},{6,7},{7,8},{8,9},{9,10},{10,1... | collective-permute-start | bytes 9224 | tf_op jit(solution)/shard_map/ppermute | solution.py:24
  254.7 11.3 %collective-permute-start.37 = (f32[1,8,64]{2,1,0:T(8,128)S(1)}, f32[1,8,64]{2,1,0:T(8,128)S(1)}, u32[]{:S(2)}, u32[]{:S(2)}) collective-permute-start(f32[1,8,64]{2,1,0:T(8,128)S(1)} %get-tuple-element.102), channel_id=1, source_target_pairs={{0,32},{32,64},{64,96},{96,128},{128,160},{160,192},{192,224},{1,3... | collective-permute-start | bytes 6152 | tf_op jit(solution)/shard_map/ppermute | solution.py:24
  261.7 11.9 %collective-permute-start.50 = (f32[2,3,1,32]{3,2,1,0:T(1,128)S(1)}, f32[2,3,1,32]{3,2,1,0:T(1,128)S(1)}, u32[]{:S(2)}, u32[]{:S(2)}) collective-permute-start(f32[2,3,1,32]{3,2,1,0:T(1,128)S(1)} %get-tuple-element.92), channel_id=1, source_target_pairs={{0,1},{1,2},{2,3},{3,4},{4,5},{5,6},{6,7},{7,8},{8,9},{9,10},{10,1... | collective-permute-start | bytes 2312 | tf_op jit(solution)/shard_map/ppermute | solution.py:24
  263.9 9.7 %collective-permute-start.51 = (f32[2,3,1,32]{3,2,1,0:T(1,128)S(1)}, f32[2,3,1,32]{3,2,1,0:T(1,128)S(1)}, u32[]{:S(2)}, u32[]{:S(2)}) collective-permute-start(f32[2,3,1,32]{3,2,1,0:T(1,128)S(1)} %get-tuple-element.93), channel_id=1, source_target_pairs={{1,0},{2,1},{3,2},{4,3},{5,4},{6,5},{7,6},{8,7},{9,8},{10,9},{11,1... | collective-permute-start | bytes 2312 | tf_op jit(solution)/shard_map/ppermute | solution.py:27
  266.0 8.3 %collective-permute-start.39 = (f32[4,1,64]{2,1,0:T(1,128)S(1)}, f32[4,1,64]{2,1,0:T(1,128)S(1)}, u32[]{:S(2)}, u32[]{:S(2)}) collective-permute-start(f32[4,1,64]{2,1,0:T(1,128)S(1)} %get-tuple-element.88), channel_id=1, source_target_pairs={{0,1},{1,2},{2,3},{3,4},{4,5},{5,6},{6,7},{7,8},{8,9},{9,10},{10,1... | collective-permute-start | bytes 3080 | tf_op jit(solution)/shard_map/ppermute | solution.py:24
  (88 other events, 522.9 us)
where the time goes:
time: 603 us; the launch traced here: 598 us
  starting transfers between devices  279 us (46%)
  waiting for transfers between devices  174 us (29%)
  local copies, waits for them, and re-layouts  81.4 us (13%)
  other arithmetic  60.7 us (10%)
    ppermute x54, starting transfers between devices, padded_2(): lax.ppermute(lax.slice_in_dim(block, block.shape[dim] - width, None, axis...  191 us
    ppermute x54, waiting for transfers between devices, padded_2(): lax.ppermute(lax.slice_in_dim(block, 0, width, axis=dim), axis, backward)  174 us
    ppermute x54, starting transfers between devices, padded_2(): lax.ppermute(lax.slice_in_dim(block, 0, width, axis=dim), axis, backward)  88.6 us
    another operation x2, local copies, waits for them, and re-layouts, coefficients(): return jnp.stack([inverse, reaction])  36.2 us
    reduce_sum x8, other arithmetic, coarsen(): return jnp.mean(blocks, axis=(-5, -3, -1))  26.8 us
    reshape x2, local copies, waits for them, and re-layouts, coarsen(): array.reshape(lead + (shape[-3] // 2, 2, shape[-2] // 2, 2, shape[-1] //...  23 us
    add x19, other arithmetic, relax(): return padded[1:-1, 1:-1, 1:-1] + OMEGA * (source_now - applied) / diagonal  13.1 us
  transfers between devices with their start and end apart: 108, of which 43 were waited for; matrix products, arithmetic and copies ran while one was open for 18% of the time, Pallas kernels for 0%

commit v1 on v0

v1 whole, which is shorter than its diff:
```python
import functools

import jax
import jax.numpy as jnp
from jax import lax
from jax.experimental import pallas as pl
from jax.experimental.pallas import tpu as pltpu
from jax.sharding import PartitionSpec as P

F32 = jnp.float32
OMEGA = 0.8
SHIFT = 0.001
ROBIN = 2.0
INVERSE_SOLID = 1.0 / 3.0
INVERSE_DENSE = 0.125
MIB = 1 << 20


def swap(block, axis, parity):
    count = lax.axis_size(axis)
    pairs = [(i, i + 1) for i in range(parity, count - 1, 2)]
    return lax.ppermute(block, axis, pairs + [(b, a) for a, b in pairs])


def swaps(first, second, axis):
    return swap(first, axis, 0), swap(second, axis, 1)


def iota(shape, dim):
    return lax.broadcasted_iota(jnp.int32, shape, dim)


def dot(a, b):
    return lax.dot_general(
        a,
        b,
        (((1,), (0,)), ((), ())),
        precision=lax.Precision.HIGHEST,
        preferred_element_type=F32,
    )


def inverse_density(material):
    return jnp.where(
        material == 0, F32(1.0), jnp.where(material == 1, F32(INVERSE_SOLID), F32(INVERSE_DENSE))
    )


def reaction_of(flags):
    return F32(SHIFT) + F32(ROBIN) * flags.astype(F32)


def recip(x):
    return 1.0 / x


def harmonic(a, b):
    return (2.0 * a * b) * recip(jnp.maximum(a + b, F32(1e-30)))


def coarsen_z0():
    return jnp.where(iota((256, 128), 0) // 2 == iota((256, 128), 1), F32(0.125), F32(0.0))


def coarsen_z1(half):
    lane = iota((128, 128), 1)
    hit = (iota((128, 128), 0) // 2 == lane % 64) & (lane // 64 == half)
    return jnp.where(hit, F32(0.125), F32(0.0))


def coarsen_z2():
    hit = (iota((128, 128), 0) % 64) // 2 == iota((128, 128), 1) % 32
    return jnp.where(hit, F32(0.125), F32(0.0))


def fold_level2(tiles):
    t = dot(tiles, coarsen_z2())
    keep = (iota((64, 128), 0) % 8) // 2 == iota((64, 128), 1) // 32
    t = jnp.where(keep, t, F32(0.0))
    return jnp.sum(t.reshape(8, 8, 128), axis=1)


def pair_rows(ref, count):
    return ref[:, pl.ds(0, count, stride=2), :] + ref[:, pl.ds(1, count, stride=2), :]


def fold_level1(tmp):
    t = pair_rows(tmp, 8)
    return dot(t[0], coarsen_z1(0)) + dot(t[1], coarsen_z1(1))


def next_y(v):
    return pltpu.roll(v, v.shape[0] - 1, 0)


def last_y(v):
    return pltpu.roll(v, 1, 0)


def next_z(v):
    return pltpu.roll(v, v.shape[1] - 1, 1)


def last_z(v):
    return pltpu.roll(v, 1, 1)


def weights(b, c, g, wx, wy, wz, rd, v, scaling, low, high):
    scale = F32(scaling)
    prev = scale * harmonic(b[low - 1], b[low])
    wx[low - 1] = prev
    shape = prev.shape
    inside = iota(shape, 1) < shape[1] - 1

    def body(x, prev):
        here = b[x]
        cur = scale * harmonic(here, b[x + 1])
        wx[x] = cur
        fy = scale * harmonic(here, next_y(here))
        wy[x] = fy
        fz = jnp.where(inside, scale * harmonic(here, next_z(here)), F32(0.0))
        wz[x] = fz
        d = (prev + cur) + (fy + last_y(fy)) + (fz + last_z(fz)) + c[x]
        r = jnp.where(d > 0, F32(OMEGA) * recip(jnp.where(d > 0, d, F32(1.0))), F32(0.0))
        rd[x] = r
        v[x] = r * g[x]
        return cur

    lax.fori_loop(low, high, body, prev)


def rows(v, g, c, wx, wy, wz, low, high, emit):
    first = wx[low - 1] * (v[low - 1] - v[low])

    def body(x, prev):
        here = v[x]
        cur = wx[x] * (here - v[x + 1])
        fy = wy[x] * (here - next_y(here))
        fz = wz[x] * (here - next_z(here))
        flux = (cur - prev) + (fy - last_y(fy)) + (fz - last_z(fz))
        emit(x, here, g[x] - (flux + c[x] * here))
        return cur

    lax.fori_loop(low, high, body, first)


def sweep(src, dst, g, c, wx, wy, wz, rd, low, high):
    def emit(x, here, res):
        dst[x] = here + rd[x] * res

    rows(src, g, c, wx, wy, wz, low, high, emit)


def k_pack_x0(idx, m, f, g, s0, s1):
    even = lax.rem(idx[0], 2) == 0
    for out, high in ((s0, even), (s1, jnp.logical_not(even))):
        four = jnp.where(high, 4, 0)
        three = jnp.where(high, 5, 0)
        for k in range(4):
            out[k] = inverse_density(m[four + k])
        for k in range(3):
            out[4 + k] = reaction_of(f[three + k])
            out[7 + k] = g[three + k]


def k_coefs(m, f, b1, c1, bc2, tmp0, tmp1):
    z0 = coarsen_z0()
    for k, out in ((0, b1), (1, c1)):
        for x in range(4):
            if k == 0:
                tmp0[x] = inverse_density(m[2 * x]) + inverse_density(m[2 * x + 1])
            else:
                tmp0[x] = reaction_of(f[2 * x]) + reaction_of(f[2 * x + 1])
        for x in range(4):
            out[x] = fold_y0(tmp0, x, z0)
        for x in range(2):
            tmp1[x] = out[2 * x] + out[2 * x + 1]
        bc2[k] = fold_level1(tmp1)


def fold_y0(tmp, x, z0):
    low = tmp[x, :, 0:128]
    high = tmp[x, :, 128:256]
    half = z0[0:128, 0:64]
    del half
    t = dot(low, z0[0:128]) + dot(high, z0[128:256])
    sel = jnp.where(iota((16, 32), 1) // 2 == iota((16, 32), 0), F32(1.0), F32(0.0))
    return dot(sel, t)


def strip_tiles(out, t, value):
    out[t, 0:4, :] = value[:, 0:128]
    out[t, 4:8, :] = value[:, 128:256]


def each_side(odd, low, high, r0, r1, put):
    @pl.when(odd == 0)
    def _():
        put(r0, True)
        put(r1, False)

    @pl.when(odd == 1)
    def _():
        put(r0, False)
        put(r1, True)


def pick_sides(odd, r0, r1):
    def low(k):
        return jnp.where(odd == 0, r1[k], r0[k])

    def high(k):
        return jnp.where(odd == 0, r0[k], r1[k])

    return low, high


def k_pack_y0(idx, m, f, g, r0, r1, s0, s1):
    odd_x = lax.rem(idx[0], 2)
    odd_y = lax.rem(idx[1], 2)

    def fill(out, at):
        cut = pl.ds(at, 4)

        def side(k):
            return r0[k, cut, :], r1[k, cut, :]

        t = 0
        for x in range(-4, 12):
            if 0 <= x < 8:
                val = inverse_density(m[x, cut, :])
            else:
                a, b = side(x + 4 if x < 0 else x - 8)
                val = jnp.where(odd_x == 0, b, a) if x < 0 else jnp.where(odd_x == 0, a, b)
            strip_tiles(out, t, val)
            t += 1
        for base, own in ((4, f), (7, g)):
            for x in range(-3, 11):
                if 0 <= x < 8:
                    val = own[x, cut, :]
                    if base == 4:
                        val = reaction_of(val)
                else:
                    a, b = side(base + (x + 3 if x < 0 else x - 8))
                    val = jnp.where(odd_x == 0, b, a) if x < 0 else jnp.where(odd_x == 0, a, b)
                strip_tiles(out, t, val)
                t += 1

    @pl.when(odd_y == 0)
    def _():
        fill(s0, 28)
        fill(s1, 0)

    @pl.when(odd_y == 1)
    def _():
        fill(s0, 0)
        fill(s1, 28)


def put_strips0(ext, first_row, count, buf, base, high):
    at = 40 if high else 4
    for k in range(count):
        ext[first_row + k, at : at + 4, 0:128] = buf[base + k, 0:4, :]
        ext[first_row + k, at : at + 4, 128:256] = buf[base + k, 4:8, :]


def k_descend0(
    idx, m, f, g, r0x, r1x, r0y, r1y, b1, c1,
    v0, g1, s0, s1, wx, wy, wz, rd, ce, ge,
    be, va, vb, tmp,
):
    odd_x = lax.rem(idx[0], 2)
    odd_y = lax.rem(idx[1], 2)
    zeros = jnp.zeros((16, 8, 256), F32)
    for ext in (be, ce, ge):
        ext[:, 0:8, :] = zeros
        ext[:, 40:48, :] = zeros
    for x in range(8):
        be[4 + x, 8:40, :] = inverse_density(m[x])
        ce[4 + x, 8:40, :] = reaction_of(f[x])
        ge[4 + x, 8:40, :] = g[x]

    def put_x(buf, high):
        for k in range(4):
            be[(12 if high else 0) + k, 8:40, :] = buf[k]
        for k in range(3):
            ce[(12 if high else 1) + k, 8:40, :] = buf[4 + k]
            ge[(12 if high else 1) + k, 8:40, :] = buf[7 + k]

    each_side(odd_x, None, None, r0x, r1x, put_x)

    def put_y(buf, high):
        put_strips0(be, 0, 16, buf, 0, high)
        put_strips0(ce, 1, 14, buf, 16, high)
        put_strips0(ge, 1, 14, buf, 30, high)

    each_side(odd_y, None, None, r0y, r1y, put_y)

    weights(be, ce, ge, wx, wy, wz, rd, va, 1.0, 1, 15)
    sweep(va, vb, ge, ce, wx, wy, wz, rd, 2, 14)
    sweep(vb, va, ge, ce, wx, wy, wz, rd, 3, 13)
    for x in range(8):
        v0[x] = va[4 + x, 8:40, :]

    def emit(x, here, res):
        k = x - 4
        own = res[8:40, :]

        @pl.when(lax.rem(k, 2) == 0)
        def _():
            tmp[k // 2] = own

        @pl.when(lax.rem(k, 2) == 1)
        def _():
            tmp[k // 2] += own

    rows(va, ge, ce, wx, wy, wz, 4, 12, emit)
    z0 = coarsen_z0()
    for x in range(4):
        g1[x] = fold_y0(tmp, x, z0)

    for out, high in ((s0, odd_x == 0), (s1, odd_x == 1)):
        one = jnp.where(high, 1, 0)
        for k in range(4):
            out[k] = b1[k]
        for k in range(3):
            out[4 + k] = c1[one + k]
            out[7 + k] = g1[one + k]


def k_pack_y1(idx, g1, b1, c1, r0, r1, s0, s1):
    odd_x = lax.rem(idx[0], 2)
    odd_y = lax.rem(idx[1], 2)

    def fill(out, at):
        cut = pl.ds(at, 4)
        t = 0
        for own, base, reach in ((b1, 0, 4), (c1, 4, 3), (g1, 7, 3)):
            for x in range(-reach, 4 + reach):
                if 0 <= x < 4:
                    val = own[x, cut, :]
                else:
                    k = base + (x + reach if x < 0 else x - 4)
                    a, b = r0[k, cut, :], r1[k, cut, :]
                    val = jnp.where(odd_x == 0, b, a) if x < 0 else jnp.where(odd_x == 0, a, b)
                half = 4 * (t % 2)
                out[t // 2, half : half + 4, :] = val
                t += 1

    @pl.when(odd_y == 0)
    def _():
        fill(s0, 12)
        fill(s1, 0)

    @pl.when(odd_y == 1)
    def _():
        fill(s0, 0)
        fill(s1, 12)


def k_descend1(
    idx, g1, b1, c1, bc2, v0, r0x, r1x, r0y, r1y,
    v1, pay, sv0, sv1, wx, wy, wz, rd, ce, ge,
    be, va, vb, tmp,
):
    odd_x = lax.rem(idx[0], 2)
    odd_y = lax.rem(idx[1], 2)
    zeros = jnp.zeros((12, 8, 128), F32)
    for ext in (be, ce, ge):
        ext[:, 0:8, :] = zeros
        ext[:, 24:32, :] = zeros
    for x in range(4):
        be[4 + x, 8:24, :] = b1[x]
        ce[4 + x, 8:24, :] = c1[x]
        ge[4 + x, 8:24, :] = g1[x]

    def put_x(buf, high):
        for k in range(4):
            be[(8 if high else 0) + k, 8:24, :] = buf[k]
        for k in range(3):
            ce[(8 if high else 1) + k, 8:24, :] = buf[4 + k]
            ge[(8 if high else 1) + k, 8:24, :] = buf[7 + k]

    each_side(odd_x, None, None, r0x, r1x, put_x)

    def put_y(buf, high):
        at = 24 if high else 4
        t = 0
        for ext, first, count in ((be, 0, 12), (ce, 1, 10), (ge, 1, 10)):
            for k in range(count):
                half = 4 * (t % 2)
                ext[first + k, at : at + 4, :] = buf[t // 2, half : half + 4, :]
                t += 1

    each_side(odd_y, None, None, r0y, r1y, put_y)

    weights(be, ce, ge, wx, wy, wz, rd, va, 0.25, 1, 11)
    sweep(va, vb, ge, ce, wx, wy, wz, rd, 2, 10)
    sweep(vb, va, ge, ce, wx, wy, wz, rd, 3, 9)
    for x in range(4):
        v1[x] = va[4 + x, 8:24, :]

    def emit(x, here, res):
        k = x - 4
        own = res[8:24, :]

        @pl.when(lax.rem(k, 2) == 0)
        def _():
            tmp[k // 2] = own

        @pl.when(lax.rem(k, 2) == 1)
        def _():
            tmp[k // 2] += own

    rows(va, ge, ce, wx, wy, wz, 4, 8, emit)
    g2 = fold_level1(tmp)
    for k in range(8):
        pay[k, 0] = g2
        pay[k, 1] = bc2[0]
        pay[k, 2] = bc2[1]

    for out, high in ((sv0, odd_x == 0), (sv1, odd_x == 1)):
        five = jnp.where(high, 5, 0)
        for k in range(3):
            row = v0[five + k]
            for q in range(2):
                for h in range(2):
                    out[4 * k + 2 * q + h] = row[16 * q : 16 * q + 16, 128 * h : 128 * h + 128]
        for k in range(4):
            out[12 + k] = v1[k]


def k_pack_y2(idx, v0, v1, rv0, rv1, gathered, s0, s1):
    odd_x = lax.rem(idx[0], 2)
    odd_y = lax.rem(idx[1], 2)
    for out in (s0, s1):
        for k in range(3):
            for i in range(8):
                out[8 * k + i] = gathered[i, k]

    def fill(out, high):
        cut = pl.ds(28 if high else 0, 4)
        q = 1 if high else 0
        part = pl.ds(12 if high else 0, 4)
        for t, x in enumerate(range(-3, 11)):
            if 0 <= x < 8:
                strip_tiles(out, 24 + t, v0[x, cut, :])
            else:
                k = 4 * (x + 3 if x < 0 else x - 8) + 2 * q
                for h in range(2):
                    a, b = rv0[k + h, part, :], rv1[k + h, part, :]
                    val = jnp.where(odd_x == 0, b, a) if x < 0 else jnp.where(odd_x == 0, a, b)
                    out[24 + t, 4 * h : 4 * h + 4, :] = val
        for t, x in enumerate(range(-4, 8)):
            if 0 <= x < 4:
                val = v1[x, part, :]
            else:
                k = 12 + (x + 4 if x < 0 else x - 4)
                a, b = rv0[k, part, :], rv1[k, part, :]
                val = jnp.where(odd_x == 0, b, a) if x < 0 else jnp.where(odd_x == 0, a, b)
            half = 4 * (t % 2)
            out[38 + t // 2, half : half + 4, :] = val

    @pl.when(odd_y == 0)
    def _():
        fill(s0, True)
        fill(s1, False)

    @pl.when(odd_y == 1)
    def _():
        fill(s0, False)
        fill(s1, True)


def upper(shape):
    return iota(shape, len(shape) - 1) >= 64


def pair_next(v):
    mask = upper(v[0].shape)
    out = []
    for i in range(8):
        after = v[i + 1] if i < 7 else jnp.zeros_like(v[0])
        out.append(pltpu.roll(jnp.where(mask, v[i], after), 64, 1))
    return out


def pair_last(f):
    mask = upper(f[0].shape)
    out = []
    for i in range(8):
        before = f[i - 1] if i > 0 else jnp.zeros_like(f[0])
        out.append(pltpu.roll(jnp.where(mask, before, f[i]), 64, 1))
    return out


def weights2(b, c, scaling):
    scale = F32(scaling)
    inside = iota(b[0].shape, 1) % 64 < 63
    wx = [scale * harmonic(p, q) for p, q in zip(b, pair_next(b))]
    wy = [scale * harmonic(p, next_y(p)) for p in b]
    wz = [jnp.where(inside, scale * harmonic(p, next_z(p)), F32(0.0)) for p in b]
    back = pair_last(wx)
    rd = []
    for i in range(8):
        d = (wx[i] + back[i]) + (wy[i] + last_y(wy[i])) + (wz[i] + last_z(wz[i])) + c[i]
        rd.append(jnp.where(d > 0, F32(OMEGA) * recip(jnp.where(d > 0, d, F32(1.0))), F32(0.0)))
    return wx, wy, wz, rd


def residual2(v, g, c, wx, wy, wz):
    fx = [w * (p - q) for w, p, q in zip(wx, v, pair_next(v))]
    back = pair_last(fx)
    out = []
    for i in range(8):
        fy = wy[i] * (v[i] - next_y(v[i]))
        fz = wz[i] * (v[i] - next_z(v[i]))
        flux = (fx[i] - back[i]) + (fy - last_y(fy)) + (fz - last_z(fz))
        out.append(g[i] - (flux + c[i] * v[i]))
    return out


def k_descend2(idx, gathered, r0, r1, v2, pay, wx2, wy2, wz2, rd2, ce2, ge2, be2, tmp):
    odd_y = lax.rem(idx[1], 2)
    for k, ext in enumerate((ge2, be2, ce2)):
        for i in range(8):
            ext[i, 8:16, :] = gathered[i, k]

    def put(buf, high):
        at = 16 if high else 0
        for k, ext in enumerate((ge2, be2, ce2)):
            for i in range(8):
                ext[i, at : at + 8, :] = buf[8 * k + i]

    each_side(odd_y, None, None, r0, r1, put)
    b = [be2[i] for i in range(8)]
    c = [ce2[i] for i in range(8)]
    g = [ge2[i] for i in range(8)]
    wx, wy, wz, rd = weights2(b, c, 0.0625)
    for i in range(8):
        wx2[i] = wx[i]
        wy2[i] = wy[i]
        wz2[i] = wz[i]
        rd2[i] = rd[i]
    v = [p * q for p, q in zip(rd, g)]
    for _ in range(2):
        r = residual2(v, g, c, wx, wy, wz)
        v = [p + q * s for p, q, s in zip(v, rd, r)]
    r = residual2(v, g, c, wx, wy, wz)
    for i in range(8):
        v2[i] = v[i]
        tmp[8 * i : 8 * i + 8, :] = r[i][8:16, :]
    folded = [fold_level2(tmp[...])]
    for k in (1, 2):
        for i in range(8):
            tmp[8 * i : 8 * i + 8, :] = gathered[i, k]
        folded.append(fold_level2(tmp[...]))
    for j in range(32):
        for k in range(3):
            pay[j, k] = folded[k]


def block_next(v):
    head = iota(v[0].shape, 1) < 32
    out = []
    for t in range(7):
        after = v[t + 1] if t < 6 else jnp.zeros_like(v[0])
        out.append(pltpu.roll(jnp.where(head, after, v[t]), 96, 1))
    return out


def block_last(f):
    tail = iota(f[0].shape, 1) >= 96
    out = []
    for t in range(7):
        before = f[t - 1] if t > 0 else jnp.zeros_like(f[0])
        out.append(pltpu.roll(jnp.where(tail, before, f[t]), 32, 1))
    return out


def solve3(g, b, c):
    scale = F32(0.015625)
    shape = g[0].shape
    inside_x = iota(shape, 0) < 7
    inside_z = iota(shape, 1) % 32 < 31
    zero = F32(0.0)
    wx = [jnp.where(inside_x, scale * harmonic(p, next_y(p)), zero) for p in b]
    wy = [scale * harmonic(p, q) for p, q in zip(b, block_next(b))]
    wz = [jnp.where(inside_z, scale * harmonic(p, next_z(p)), zero) for p in b]
    back = block_last(wy)
    rd = []
    for t in range(7):
        d = (wx[t] + last_y(wx[t])) + (wy[t] + back[t]) + (wz[t] + last_z(wz[t])) + c[t]
        rd.append(jnp.where(d > 0, F32(OMEGA) * recip(jnp.where(d > 0, d, F32(1.0))), zero))
    e = [p * q for p, q in zip(rd, g)]
    for _ in range(7):
        fy = [w * (p - q) for w, p, q in zip(wy, e, block_next(e))]
        back = block_last(fy)
        new = []
        for t in range(7):
            fx = wx[t] * (e[t] - next_y(e[t]))
            fz = wz[t] * (e[t] - next_z(e[t]))
            flux = (fx - last_y(fx)) + (fy[t] - back[t]) + (fz - last_z(fz))
            new.append(e[t] + rd[t] * (g[t] - (flux + c[t] * e[t])))
        e = new
    return e


def k_ascend(
    idx, coarse,
    v2, wx2, wy2, wz2, rd2, ce2, ge2,
    v1, wx1, wy1, wz1, rd1, ce1, ge1,
    v0, wx0, wy0, wz0, rd0, ce0, ge0,
    rv0, rv1, r0y, r1y,
    pressure, residual,
    e3, m2, p2, p1a, p1b, p0a, p0b,
):
    ix = idx[0]
    iy = idx[1]
    odd_x = lax.rem(ix, 2)
    odd_y = lax.rem(iy, 2)
    zero = F32(0.0)

    parts = ([], [], [])
    for t in range(7):
        at = iy + (t - 3)
        inside = jnp.logical_and(at >= 0, at < 32)
        at = jnp.clip(at, 0, 31)
        for k in range(3):
            parts[k].append(jnp.where(inside, coarse[at, k], zero))
    e = solve3(*parts)
    for t in range(3):
        e3[t] = e[2 + t]

    group = iota((8, 128), 1) // 32 == iota((8, 128), 0) // 2
    for i in range(8):
        for t in range(3):
            row = jnp.broadcast_to(e3[t, i : i + 1, :], (8, 128))
            m2[24 * i + 8 * t : 24 * i + 8 * t + 8, :] = jnp.where(group, row, zero)
    spread = jnp.where(
        iota((128, 128), 0) % 32 == (iota((128, 128), 1) % 64) // 2, F32(1.0), zero
    )
    fine = dot(m2[...], spread)
    v = [v2[i] + fine[24 * i : 24 * i + 24, :] for i in range(8)]
    g = [ge2[i] for i in range(8)]
    c = [ce2[i] for i in range(8)]
    wx = [wx2[i] for i in range(8)]
    wy = [wy2[i] for i in range(8)]
    wz = [wz2[i] for i in range(8)]
    for _ in range(2):
        r = residual2(v, g, c, wx, wy, wz)
        v = [v[i] + rd2[i] * r[i] for i in range(8)]
    for i in range(8):
        p2[i] = v[i]

    p1a[...] = jnp.zeros((12, 32, 128), F32)
    for x in range(4):
        p1a[4 + x, 8:24, :] = v1[x]

    def put_x1(buf, high):
        for k in range(4):
            p1a[(8 if high else 0) + k, 8:24, :] = buf[12 + k]

    each_side(odd_x, None, None, rv0, rv1, put_x1)

    def put_y1(buf, high):
        at = 24 if high else 4
        for t in range(12):
            half = 4 * (t % 2)
            p1a[t, at : at + 4, :] = buf[38 + t // 2, half : half + 4, :]

    each_side(odd_y, None, None, r0y, r1y, put_y1)

    double16 = jnp.where(iota((32, 16), 0) // 2 == iota((32, 16), 1), F32(1.0), zero)
    lane = iota((128, 128), 0)
    for q in range(3):
        at = ix + (q - 1)
        inside = jnp.logical_and(at >= 0, at < 8)
        at = jnp.clip(at, 0, 7)
        src = jnp.where(inside, p2[at, 4:20, :], zero)
        tall = dot(double16, src)
        for h in range(2):
            hit = (lane % 64 == iota((128, 128), 1) // 2) & (lane // 64 == h)
            fine = dot(tall, jnp.where(hit, F32(1.0), zero))
            for x in range(2):
                row = 4 * q + 2 * h + x
                p1a[row] = p1a[row] + fine
    sweep(p1a, p1b, ge1, ce1, wx1, wy1, wz1, rd1, 1, 11)
    sweep(p1b, p1a, ge1, ce1, wx1, wy1, wz1, rd1, 2, 10)

    p0a[...] = jnp.zeros((16, 48, 256), F32)
    for x in range(8):
        p0a[4 + x, 8:40, :] = v0[x]

    def put_x0(buf, high):
        for k in range(3):
            for q in range(2):
                for h in range(2):
                    p0a[(12 if high else 1) + k, 8 + 16 * q : 24 + 16 * q, 128 * h : 128 * h + 128] = (
                        buf[4 * k + 2 * q + h]
                    )

    each_side(odd_x, None, None, rv0, rv1, put_x0)

    def put_y0(buf, high):
        put_strips0(p0a, 1, 14, buf, 24, high)

    each_side(odd_y, None, None, r0y, r1y, put_y0)

    double24 = jnp.where(iota((48, 24), 0) // 2 == iota((48, 24), 1), F32(1.0), zero)
    wide = jnp.where(iota((128, 256), 0) == iota((128, 256), 1) // 2, F32(1.0), zero)
    for x in range(8):
        fine = dot(dot(double24, p1a[2 + x, 4:28, :]), wide)
        for h in range(2):
            row = 2 * x + h
            p0a[row] = p0a[row] + fine
    sweep(p0a, p0b, ge0, ce0, wx0, wy0, wz0, rd0, 2, 14)
    sweep(p0b, p0a, ge0, ce0, wx0, wy0, wz0, rd0, 3, 13)

    def emit(x, here, res):
        pressure[x - 4] = here[8:40, :]
        residual[x - 4] = res[8:40, :]

    rows(p0a, ge0, ce0, wx0, wy0, wz0, 4, 12, emit)


def call(kernel, name, outs, scratch, limit, *args):
    vmem = pl.BlockSpec(memory_space=pltpu.VMEM)
    smem = pl.BlockSpec(memory_space=pltpu.SMEM)
    return pl.pallas_call(
        kernel,
        name=name,
        out_shape=[jax.ShapeDtypeStruct(s, F32) for s in outs],
        in_specs=[smem if a.ndim == 1 else vmem for a in args],
        out_specs=[vmem for _ in outs],
        scratch_shapes=[pltpu.VMEM(s, F32) for s in scratch],
        compiler_params=pltpu.CompilerParams(vmem_limit_bytes=limit * MIB),
    )(*args)


E0 = (16, 48, 256)
E1 = (12, 32, 128)
E2 = (8, 24, 128)


def per_device(source, material, flags):
    idx = jnp.stack([lax.axis_index("gx"), lax.axis_index("gy")]).astype(jnp.int32)

    s0, s1 = call(k_pack_x0, "pack_x0", [(10, 32, 256)] * 2, [], 8, idx, material, flags, source)
    r0x, r1x = swaps(s0, s1, "gx")
    b1, c1, bc2 = call(
        k_coefs, "coefs", [(4, 16, 128), (4, 16, 128), (2, 8, 128)],
        [(4, 32, 256), (2, 16, 128)], 8, material, flags,
    )
    s0, s1 = call(
        k_pack_y0, "pack_y0", [(44, 8, 128)] * 2, [], 8, idx, material, flags, source, r0x, r1x
    )
    r0y, r1y = swaps(s0, s1, "gy")
    v0, g1, s0, s1, wx0, wy0, wz0, rd0, ce0, ge0 = call(
        k_descend0, "descend0",
        [(8, 32, 256), (4, 16, 128), (10, 16, 128), (10, 16, 128)] + [E0] * 6,
        [E0, E0, E0, (4, 32, 256)], 24,
        idx, material, flags, source, r0x, r1x, r0y, r1y, b1, c1,
    )
    r0x, r1x = swaps(s0, s1, "gx")
    s0, s1 = call(k_pack_y1, "pack_y1", [(16, 8, 128)] * 2, [], 8, idx, g1, b1, c1, r0x, r1x)
    r0y, r1y = swaps(s0, s1, "gy")
    v1, pay, sv0, sv1, wx1, wy1, wz1, rd1, ce1, ge1 = call(
        k_descend1, "descend1",
        [(4, 16, 128), (8, 3, 8, 128), (16, 16, 128), (16, 16, 128)] + [E1] * 6,
        [E1, E1, E1, (2, 16, 128)], 16,
        idx, g1, b1, c1, bc2, v0, r0x, r1x, r0y, r1y,
    )
    gathered = lax.all_to_all(pay, "gx", 0, 0)
    rv0, rv1 = swaps(sv0, sv1, "gx")
    s0, s1 = call(
        k_pack_y2, "pack_y2", [(44, 8, 128)] * 2, [], 8, idx, v0, v1, rv0, rv1, gathered
    )
    r0y, r1y = swaps(s0, s1, "gy")
    v2, pay, wx2, wy2, wz2, rd2, ce2, ge2 = call(
        k_descend2, "descend2",
        [E2, (32, 3, 8, 128)] + [E2] * 6,
        [E2, (64, 128)], 16,
        idx, gathered, r0y, r1y,
    )
    coarse = lax.all_to_all(pay, "gy", 0, 0)
    pressure, residual = call(
        k_ascend, "ascend",
        [(8, 32, 256)] * 2,
        [(3, 8, 128), (192, 128), E2, E1, E1, E0, E0], 32,
        idx, coarse,
        v2, wx2, wy2, wz2, rd2, ce2, ge2,
        v1, wx1, wy1, wz1, rd1, ce1, ge1,
        v0, wx0, wy0, wz0, rd0, ce0, ge0,
        rv0, rv1, r0y, r1y,
    )
    return pressure, residual


def solution(mesh):
    spec = P("gx", "gy", None)
    return jax.shard_map(
        per_device,
        mesh=mesh,
        in_specs=(spec, spec, spec),
        out_specs=(spec, spec),
        check_vma=False,
    )
```

time: 603 us -> 133 us (0.22)
  the two profiles are of different devices: /device:TPU:7 before, /device:TPU:1 now
where the time goes in v1:
time: 133 us; the launch traced here: 132 us
  starting transfers between devices  38.8 us (29%)
  Pallas kernels  35 us (26%)
  blocking collectives  21.1 us (16%)
  local copies, waits for them, and re-layouts  19.4 us (15%)
  waiting for transfers between devices  16.8 us (13%)
    pallas_call x9, Pallas kernels, call(): pl.pallas_call(kernel, name=name, out_shape=[jax.ShapeDtypeStruct(s, F32)...  35 us
    ppermute x12, starting transfers between devices, swap(): return lax.ppermute(block, axis, pairs + [(b, a) for a, b in pairs])  27.5 us
    all_to_all x1, blocking collectives, per_device(): coarse = lax.all_to_all(pay, 'gy', 0, 0)  21.1 us
    unnamed x62, local copies, waits for them, and re-layouts  19.4 us
    ppermute x12, waiting for transfers between devices, swap(): return lax.ppermute(block, axis, pairs + [(b, a) for a, b in pairs])  15.6 us
    all_to_all x1, starting transfers between devices, per_device(): gathered = lax.all_to_all(pay, 'gx', 0, 0)  11.2 us
  transfers between devices with their start and end apart: 13, of which 7 were waited for; matrix products, arithmetic and copies ran while one was open for 0% of the time, Pallas kernels for 2%

profile of v1, /device:TPU:1, one launch (start us, length us, event | category | flops | bytes accessed | tf_op | source)
XLA Modules:
  0.0 132.0 jit_solution(11149136728222787629)
XLA Ops:
  0.7 0.9 copy-done
  1.7 0.9 copy-done.2
  2.6 0.9 copy-done.4
  4.2 2.6 %collective-permute-start = (f32[10,32,256]{2,1,0:T(8,128)S(1)}, f32[10,32,256]{2,1,0:T(8,128)S(1)}, u32[]{:S(2)}, u32[]{:S(2)}) collective-permute-start(f32[10,32,256]{2,1,0:T(8,128)S(1)} %get-tuple-element.41), channel_id=1, source_target_pairs={{0,32},{64,96},{128,160},{192,224},{32,0},{96,64},{160,128},{224,1... | collective-permute-start | bytes 983048 | tf_op jit(solution)/shard_map/ppermute | solution.py:22
  7.6 5.6 %collective-permute-done.r0.r0x = f32[10,32,256]{2,1,0:T(8,128)S(1)} collective-permute-done((f32[10,32,256]{2,1,0:T(8,128)S(1)}, f32[10,32,256]{2,1,0:T(8,128)S(1)}, u32[]{:S(2)}, u32[]{:S(2)}) %collective-permute-start) | collective-permute-done | bytes 327712 | tf_op jit(solution)/shard_map/ppermute | solution.py:22
  13.8 2.4 %collective-permute-start.2 = (f32[44,8,128]{2,1,0:T(8,128)S(1)}, f32[44,8,128]{2,1,0:T(8,128)S(1)}, u32[]{:S(2)}, u32[]{:S(2)}) collective-permute-start(f32[44,8,128]{2,1,0:T(8,128)S(1)} %get-tuple-element.43), channel_id=1, source_target_pairs={{0,1},{2,3},{4,5},{6,7},{8,9},{10,11},{12,13},{14,15},{16,17},{18,... | collective-permute-start | bytes 540680 | tf_op jit(solution)/shard_map/ppermute | solution.py:22
  16.2 3.2 %collective-permute-start.3 = (f32[44,8,128]{2,1,0:T(8,128)S(1)}, f32[44,8,128]{2,1,0:T(8,128)S(1)}, u32[]{:S(2)}, u32[]{:S(2)}) collective-permute-start(f32[44,8,128]{2,1,0:T(8,128)S(1)} %get-tuple-element.44), channel_id=1, source_target_pairs={{1,2},{3,4},{5,6},{7,8},{9,10},{11,12},{13,14},{15,16},{17,18},{19... | collective-permute-start | bytes 540680 | tf_op jit(solution)/shard_map/ppermute | solution.py:22
  19.3 2.9 %coefs.1 = (f32[4,16,128]{2,1,0:T(8,128)S(1)}, f32[4,16,128]{2,1,0:T(8,128)S(1)}, f32[2,8,128]{2,1,0:T(8,128)S(1)}) custom-call(s32[8,32,256]{2,1,0:T(8,128)S(1)} %copy-done.1, s32[8,32,256]{2,1,0:T(8,128)S(1)} %copy-done.3), custom_call_target="tpu_custom_call" | custom-call | tf_op jit(solution)/shard_map/coefs/pallas_call | solution.py:730
  23.1 10.0 %descend0.1 = (f32[8,32,256]{2,1,0:T(8,128)S(1)}, f32[4,16,128]{2,1,0:T(8,128)S(1)}, f32[10,16,128]{2,1,0:T(8,128)S(1)}, f32[10,16,128]{2,1,0:T(8,128)S(1)}, f32...) custom-call(s32[2]{0:T(128)S(1)} %pad_add_fusion.idx, ...), custom_call_target="tpu_custom_call" | custom-call | tf_op jit(solution)/shard_map/descend0/pallas_call | solution.py:730
  34.9 5.3 %collective-permute-start.4 = (f32[10,16,128]{2,1,0:T(8,128)S(1)}, f32[10,16,128]{2,1,0:T(8,128)S(1)}, u32[]{:S(2)}, u32[]{:S(2)}) collective-permute-start(f32[10,16,128]{2,1,0:T(8,128)S(1)} %get-tuple-element.50), channel_id=1, source_target_pairs={{0,32},{64,96},{128,160},{192,224},{32,0},{96,64},{160,128},{224,1... | collective-permute-start | bytes 245768 | tf_op jit(solution)/shard_map/ppermute | solution.py:22
  40.9 1.2 collective-permute-done.4.r0.r0x
  42.7 4.6 %collective-permute-start.7 = (f32[16,8,128]{2,1,0:T(8,128)S(1)}, f32[16,8,128]{2,1,0:T(8,128)S(1)}, u32[]{:S(2)}, u32[]{:S(2)}) collective-permute-start(f32[16,8,128]{2,1,0:T(8,128)S(1)} %get-tuple-element.53), channel_id=1, source_target_pairs={{1,2},{3,4},{5,6},{7,8},{9,10},{11,12},{13,14},{15,16},{17,18},{19... | collective-permute-start | bytes 196616 | tf_op jit(solution)/shard_map/ppermute | solution.py:22
  47.3 1.9 %collective-permute-done.7.r1y = f32[16,8,128]{2,1,0:T(8,128)S(1)} collective-permute-done((f32[16,8,128]{2,1,0:T(8,128)S(1)}, f32[16,8,128]{2,1,0:T(8,128)S(1)}, u32[]{:S(2)}, u32[]{:S(2)}) %collective-permute-start.7) | collective-permute-done | bytes 65568 | tf_op jit(solution)/shard_map/ppermute | solution.py:22
  49.2 5.2 %descend1.1 = (f32[4,16,128]{2,1,0:T(8,128)S(1)}, f32[8,3,8,128]{3,2,1,0:T(8,128)S(1)}, f32[16,16,128]{2,1,0:T(8,128)S(1)}, f32[16,16,128]{2,1,0:T(8,128)S(1)}, ...) custom-call(s32[2]{0:T(128)S(1)} %pad_add_fusion.idx, ...), custom_call_target="tpu_custom_call" | custom-call | tf_op jit(solution)/shard_map/descend1/pallas_call | solution.py:730
  60.4 11.2 %all-to-all-start = ((f32[8,3,8,128]{3,2,1,0:T(8,128)}), f32[8,3,8,128]{3,2,1,0:T(8,128)S(1)}, u32[]{:S(2)}, u32[]{:S(2)}) async-start(f32[8,3,8,128]{3,2,1,0:T(8,128)} %copy-done.28), calls=%async_computation | async-start | bytes 196608 | tf_op jit(solution)/shard_map/all_to_all | solution.py:774
  71.7 1.5 %collective-permute-start.8 = (f32[16,16,128]{2,1,0:T(8,128)}, f32[16,16,128]{2,1,0:T(8,128)S(1)}, u32[]{:S(2)}, u32[]{:S(2)}) collective-permute-start(f32[16,16,128]{2,1,0:T(8,128)} %copy-done.30), channel_id=1, source_target_pairs={{0,32},{64,96},{128,160},{192,224},{32,0},{96,64},{160,128},{224,1... | collective-permute-start | bytes 393224 | tf_op jit(solution)/shard_map/ppermute | solution.py:22
  73.8 2.9 %collective-permute-done.8.rv0 = f32[16,16,128]{2,1,0:T(8,128)S(1)} collective-permute-done((f32[16,16,128]{2,1,0:T(8,128)}, f32[16,16,128]{2,1,0:T(8,128)S(1)}, u32[]{:S(2)}, u32[]{:S(2)}) %collective-permute-start.8) | collective-permute-done | bytes 131104 | tf_op jit(solution)/shard_map/ppermute | solution.py:22
  78.1 1.2 all-to-all-done.gathered
  81.8 5.8 %collective-permute-start.11 = (f32[44,8,128]{2,1,0:T(8,128)S(1)}, f32[44,8,128]{2,1,0:T(8,128)S(1)}, u32[]{:S(2)}, u32[]{:S(2)}) collective-permute-start(f32[44,8,128]{2,1,0:T(8,128)S(1)} %get-tuple-element.59), channel_id=1, source_target_pairs={{1,2},{3,4},{5,6},{7,8},{9,10},{11,12},{13,14},{15,16},{17,18},{19... | collective-permute-start | bytes 540680 | tf_op jit(solution)/shard_map/ppermute | solution.py:22
  87.6 3.2 %collective-permute-done.11.r1.r1y = f32[44,8,128]{2,1,0:T(8,128)S(1)} collective-permute-done((f32[44,8,128]{2,1,0:T(8,128)S(1)}, f32[44,8,128]{2,1,0:T(8,128)S(1)}, u32[]{:S(2)}, u32[]{:S(2)}) %collective-permute-start.11) | collective-permute-done | bytes 180256 | tf_op jit(solution)/shard_map/ppermute | solution.py:22
  90.8 1.6 %descend2.1 = (f32[8,24,128]{2,1,0:T(8,128)S(1)}, f32[32,3,8,128]{3,2,1,0:T(8,128)S(1)}, f32[8,24,128]{2,1,0:T(8,128)S(1)}, f32[8,24,128]{2,1,0:T(8,128)S(1)}, f...) custom-call(s32[2]{0:T(128)S(1)} %pad_add_fusion.idx, ...), custom_call_target="tpu_custom_call" | custom-call | tf_op jit(solution)/shard_map/descend2/pallas_call | solution.py:730
  92.4 21.1 %all_to_all.10.coarse = f32[32,3,8,128]{3,2,1,0:T(8,128)S(1)} all-to-all(f32[32,3,8,128]{3,2,1,0:T(8,128)S(1)} %get-tuple-element.60), channel_id=1, replica_groups=mesh['gx'=8,'gy'=32] {'gy'}, dimensions={0} | all-to-all | bytes 786432 | tf_op jit(solution)/shard_map/all_to_all | solution.py:786
  115.3 0.9 copy-done.21
  119.0 12.9 %ascend.1 = (f32[8,32,256]{2,1,0:T(8,128)}, f32[8,32,256]{2,1,0:T(8,128)}) custom-call(s32[2]{0:T(128)S(1)} %pad_add_fusion.idx, f32[32,3,8,128]{3,2,1,0:T(8,128)S(1)} %all_to_all.10.coarse, f32[8,24,128]{2,1,0:T(8,128)S(1)} %get-tuple-element.61.v2, f32[8,24,128]{2,1,0:T(8,128)S(1)} %get-tuple-element.62.wx2, f32[8,24,128]{2,1,0:T(8,128)S(1)} %get-tuple-element.63.wy2, ...), custom_call_target="tpu_custom_call" | custom-call | tf_op jit(solution)/shard_map/ascend/pallas_call | solution.py:730
  (75 shorter events, 21.2 us)
Async XLA Ops:
  0.7 1.0 copy-start
  1.7 0.9 copy-start.2
  2.6 0.9 copy-start.4
  4.2 8.9 %collective-permute-start = (f32[10,32,256]{2,1,0:T(8,128)S(1)}, f32[10,32,256]{2,1,0:T(8,128)S(1)}, u32[]{:S(2)}, u32[]{:S(2)}) collective-permute-start(f32[10,32,256]{2,1,0:T(8,128)S(1)} %get-tuple-element.41), channel_id=1, source_target_pairs={{0,32},{64,96},{128,160},{192,224},{32,0},{96,64},{160,128},{224,1... | collective-permute-start | bytes 983048 | tf_op jit(solution)/shard_map/ppermute | solution.py:22
  6.7 12.6 %copy-start.1 = (s32[8,32,256]{2,1,0:T(8,128)S(1)}, s32[8,32,256]{2,1,0:T(8,128)}, u32[]{:S(2)}) copy-start(s32[8,32,256]{2,1,0:T(8,128)} %m.7) | copy-start | bytes 786436
  6.7 12.6 %copy-start.3 = (s32[8,32,256]{2,1,0:T(8,128)S(1)}, s32[8,32,256]{2,1,0:T(8,128)}, u32[]{:S(2)}) copy-start(s32[8,32,256]{2,1,0:T(8,128)} %f.7) | copy-start | bytes 786436
  6.7 6.4 %collective-permute-start.1 = (f32[10,32,256]{2,1,0:T(8,128)S(1)}, f32[10,32,256]{2,1,0:T(8,128)S(1)}, u32[]{:S(2)}, u32[]{:S(2)}) collective-permute-start(f32[10,32,256]{2,1,0:T(8,128)S(1)} %get-tuple-element.42), channel_id=1, source_target_pairs={{32,64},{96,128},{160,192},{64,32},{128,96},{192,160},{33,65},{97,... | collective-permute-start | bytes 983048 | tf_op jit(solution)/shard_map/ppermute | solution.py:22
  13.8 8.5 %collective-permute-start.2 = (f32[44,8,128]{2,1,0:T(8,128)S(1)}, f32[44,8,128]{2,1,0:T(8,128)S(1)}, u32[]{:S(2)}, u32[]{:S(2)}) collective-permute-start(f32[44,8,128]{2,1,0:T(8,128)S(1)} %get-tuple-element.43), channel_id=1, source_target_pairs={{0,1},{2,3},{4,5},{6,7},{8,9},{10,11},{12,13},{14,15},{16,17},{18,... | collective-permute-start | bytes 540680 | tf_op jit(solution)/shard_map/ppermute | solution.py:22
  16.2 6.9 %copy-start.5 = (f32[8,32,256]{2,1,0:T(8,128)S(1)}, f32[8,32,256]{2,1,0:T(8,128)}, u32[]{:S(2)}) copy-start(f32[8,32,256]{2,1,0:T(8,128)} %g.5) | copy-start | bytes 786436
  16.2 6.9 %collective-permute-start.3 = (f32[44,8,128]{2,1,0:T(8,128)S(1)}, f32[44,8,128]{2,1,0:T(8,128)S(1)}, u32[]{:S(2)}, u32[]{:S(2)}) collective-permute-start(f32[44,8,128]{2,1,0:T(8,128)S(1)} %get-tuple-element.44), channel_id=1, source_target_pairs={{1,2},{3,4},{5,6},{7,8},{9,10},{11,12},{13,14},{15,16},{17,18},{19... | collective-permute-start | bytes 540680 | tf_op jit(solution)/shard_map/ppermute | solution.py:22
  34.9 7.1 %collective-permute-start.4 = (f32[10,16,128]{2,1,0:T(8,128)S(1)}, f32[10,16,128]{2,1,0:T(8,128)S(1)}, u32[]{:S(2)}, u32[]{:S(2)}) collective-permute-start(f32[10,16,128]{2,1,0:T(8,128)S(1)} %get-tuple-element.50), channel_id=1, source_target_pairs={{0,32},{64,96},{128,160},{192,224},{32,0},{96,64},{160,128},{224,1... | collective-permute-start | bytes 245768 | tf_op jit(solution)/shard_map/ppermute | solution.py:22
  40.2 1.8 %collective-permute-start.5 = (f32[10,16,128]{2,1,0:T(8,128)S(1)}, f32[10,16,128]{2,1,0:T(8,128)S(1)}, u32[]{:S(2)}, u32[]{:S(2)}) collective-permute-start(f32[10,16,128]{2,1,0:T(8,128)S(1)} %get-tuple-element.51), channel_id=1, source_target_pairs={{32,64},{96,128},{160,192},{64,32},{128,96},{192,160},{33,65},{97,... | collective-permute-start | bytes 245768 | tf_op jit(solution)/shard_map/ppermute | solution.py:22
  42.6 4.7 %collective-permute-start.6 = (f32[16,8,128]{2,1,0:T(8,128)S(1)}, f32[16,8,128]{2,1,0:T(8,128)S(1)}, u32[]{:S(2)}, u32[]{:S(2)}) collective-permute-start(f32[16,8,128]{2,1,0:T(8,128)S(1)} %get-tuple-element.52), channel_id=1, source_target_pairs={{0,1},{2,3},{4,5},{6,7},{8,9},{10,11},{12,13},{14,15},{16,17},{18,... | collective-permute-start | bytes 196616 | tf_op jit(solution)/shard_map/ppermute | solution.py:22
  42.7 6.5 %collective-permute-start.7 = (f32[16,8,128]{2,1,0:T(8,128)S(1)}, f32[16,8,128]{2,1,0:T(8,128)S(1)}, u32[]{:S(2)}, u32[]{:S(2)}) collective-permute-start(f32[16,8,128]{2,1,0:T(8,128)S(1)} %get-tuple-element.53), channel_id=1, source_target_pairs={{1,2},{3,4},{5,6},{7,8},{9,10},{11,12},{13,14},{15,16},{17,18},{19... | collective-permute-start | bytes 196616 | tf_op jit(solution)/shard_map/ppermute | solution.py:22
  60.4 18.8 %all-to-all-start = ((f32[8,3,8,128]{3,2,1,0:T(8,128)}), f32[8,3,8,128]{3,2,1,0:T(8,128)S(1)}, u32[]{:S(2)}, u32[]{:S(2)}) async-start(f32[8,3,8,128]{3,2,1,0:T(8,128)} %copy-done.28), calls=%async_computation | async-start | bytes 196608 | tf_op jit(solution)/shard_map/all_to_all | solution.py:774
  71.7 5.1 %collective-permute-start.8 = (f32[16,16,128]{2,1,0:T(8,128)}, f32[16,16,128]{2,1,0:T(8,128)S(1)}, u32[]{:S(2)}, u32[]{:S(2)}) collective-permute-start(f32[16,16,128]{2,1,0:T(8,128)} %copy-done.30), channel_id=1, source_target_pairs={{0,32},{64,96},{128,160},{192,224},{32,0},{96,64},{160,128},{224,1... | collective-permute-start | bytes 393224 | tf_op jit(solution)/shard_map/ppermute | solution.py:22
  73.1 4.3 %collective-permute-start.9 = (f32[16,16,128]{2,1,0:T(8,128)}, f32[16,16,128]{2,1,0:T(8,128)S(1)}, u32[]{:S(2)}, u32[]{:S(2)}) collective-permute-start(f32[16,16,128]{2,1,0:T(8,128)} %copy-done.29), channel_id=1, source_target_pairs={{32,64},{96,128},{160,192},{64,32},{128,96},{192,160},{33,65},{97,... | collective-permute-start | bytes 393224 | tf_op jit(solution)/shard_map/ppermute | solution.py:22
  81.1 32.4 %copy-start.9 = (f32[16,48,256]{2,1,0:T(8,128)S(1)}, f32[16,48,256]{2,1,0:T(8,128)}, u32[]{:S(2)}) copy-start(f32[16,48,256]{2,1,0:T(8,128)} %copy-done.8) | copy-start | bytes 2359300
  81.7 31.8 %copy-start.7 = (f32[16,48,256]{2,1,0:T(8,128)S(1)}, f32[16,48,256]{2,1,0:T(8,128)}, u32[]{:S(2)}) copy-start(f32[16,48,256]{2,1,0:T(8,128)} %copy-done.6) | copy-start | bytes 2359300
  81.7 5.9 %collective-permute-start.10 = (f32[44,8,128]{2,1,0:T(8,128)S(1)}, f32[44,8,128]{2,1,0:T(8,128)S(1)}, u32[]{:S(2)}, u32[]{:S(2)}) collective-permute-start(f32[44,8,128]{2,1,0:T(8,128)S(1)} %get-tuple-element.58), channel_id=1, source_target_pairs={{0,1},{2,3},{4,5},{6,7},{8,9},{10,11},{12,13},{14,15},{16,17},{18,... | collective-permute-start | bytes 540680 | tf_op jit(solution)/shard_map/ppermute | solution.py:22
  81.8 9.0 %collective-permute-start.11 = (f32[44,8,128]{2,1,0:T(8,128)S(1)}, f32[44,8,128]{2,1,0:T(8,128)S(1)}, u32[]{:S(2)}, u32[]{:S(2)}) collective-permute-start(f32[44,8,128]{2,1,0:T(8,128)S(1)} %get-tuple-element.59), channel_id=1, source_target_pairs={{1,2},{3,4},{5,6},{7,8},{9,10},{11,12},{13,14},{15,16},{17,18},{19... | collective-permute-start | bytes 540680 | tf_op jit(solution)/shard_map/ppermute | solution.py:22
  92.4 21.1 %copy-start.12 = (f32[16,16,128]{2,1,0:T(8,128)S(1)}, f32[16,16,128]{2,1,0:T(8,128)}, u32[]{:S(2)}) copy-start(f32[16,16,128]{2,1,0:T(8,128)} %copy-done.10) | copy-start | bytes 393220
  92.4 21.1 %copy-start.15 = (f32[16,16,128]{2,1,0:T(8,128)S(1)}, f32[16,16,128]{2,1,0:T(8,128)}, u32[]{:S(2)}) copy-start(f32[16,16,128]{2,1,0:T(8,128)} %copy-done.13) | copy-start | bytes 393220
  113.4 0.9 copy-start.17
  (20 other events, 15.6 us)

commit v2 on v0

v2 whole, which is shorter than its diff:
```python
import jax
import jax.numpy as jnp
from jax import lax
from jax.experimental import pallas as pl
from jax.experimental.pallas import tpu as pltpu
from jax.sharding import PartitionSpec as P

F32 = jnp.float32
BF16 = jnp.bfloat16
OMEGA = 0.8
SHIFT = 0.001
ROBIN = 2.0
INVERSE_SOLID = 1.0 / 3.0
INVERSE_DENSE = 0.125
MIB = 1 << 20


def shift(block, axis, step):
    count = lax.axis_size(axis)
    return lax.ppermute(block, axis, [(i, (i + step) % count) for i in range(count)])


def exchange(low, high, axis):
    return shift(high, axis, 1), shift(low, axis, -1)


def swap_chips(block, axis, parity):
    count = lax.axis_size(axis)
    pairs = [(i, i + 2) for i in range(count - 2) if (i // 2) % 2 == parity]
    if parity == 1:
        pairs = [(0, 1)] + pairs + [(count - 2, count - 1)]
    return lax.ppermute(block, axis, pairs + [(b, a) for a, b in pairs])


def iota(shape, dim):
    return lax.broadcasted_iota(jnp.int32, shape, dim)


def pick(a, w):
    count = a.shape[0]
    a1 = a.astype(BF16)
    rest = a - a1.astype(F32)
    a2 = rest.astype(BF16)
    a3 = (rest - a2.astype(F32)).astype(BF16)
    out = jnp.dot(
        jnp.concatenate([a1, a2, a3], axis=0), w.astype(BF16), preferred_element_type=F32
    )
    return out[:count] + out[count : 2 * count] + out[2 * count :]


def inverse_density(material):
    return jnp.where(
        material == 0, F32(1.0), jnp.where(material == 1, F32(INVERSE_SOLID), F32(INVERSE_DENSE))
    )


def reaction_of(flags):
    return F32(SHIFT) + F32(ROBIN) * flags.astype(F32)


def harmonic(a, b):
    return (2.0 * a * b) * (1.0 / jnp.maximum(a + b, F32(1e-30)))


def step_of(d):
    return jnp.where(d > 0, F32(OMEGA) / jnp.where(d > 0, d, F32(1.0)), F32(0.0))


def fold_level0(tmp):
    parts = []
    for h in range(2):
        parts.append(
            jnp.concatenate(
                [
                    tmp[x, h, pl.ds(0, 16, stride=2), :] + tmp[x, h, pl.ds(1, 16, stride=2), :]
                    for x in range(4)
                ],
                axis=0,
            )
        )
    w = jnp.where(iota((256, 128), 0) // 2 == iota((256, 128), 1), F32(0.125), F32(0.0))
    return pick(jnp.concatenate(parts, axis=1), w)


def fold_level1(tmp):
    parts = [
        tmp[x, pl.ds(0, 8, stride=2), :] + tmp[x, pl.ds(1, 8, stride=2), :] for x in range(2)
    ]
    row = iota((256, 128), 0)
    lane = iota((256, 128), 1)
    hit = ((row % 128) // 2 == lane % 64) & (row // 128 == lane // 64)
    return pick(jnp.concatenate(parts, axis=1), jnp.where(hit, F32(0.125), F32(0.0)))


def fold_level2(tiles):
    count = tiles.shape[0] // 64
    hit = (iota((128, 128), 0) % 64) // 2 == iota((128, 128), 1) % 32
    t = pick(tiles, jnp.where(hit, F32(0.125), F32(0.0))).reshape(count, 8, 8, 128)
    keep = iota(t.shape, 2) // 2 == iota(t.shape, 3) // 32
    t = jnp.sum(jnp.where(keep, t, F32(0.0)), axis=2)
    return [t[k] for k in range(count)]


def next_y(v):
    return pltpu.roll(v, v.shape[0] - 1, 0)


def last_y(v):
    return pltpu.roll(v, 1, 0)


def next_z(v):
    return pltpu.roll(v, v.shape[1] - 1, 1)


def last_z(v):
    return pltpu.roll(v, 1, 1)


def weights(b, s, v, scaling, low, high, unroll):
    wx, wy, wz, wl, rd, c, g = s
    scale = F32(scaling)
    prev = scale * harmonic(b[low - 1], b[low])
    wx[low - 1] = prev
    shape = prev.shape
    inside = iota(shape, 1) < shape[1] - 1

    def body(x, prev):
        here = b[x]
        cur = scale * harmonic(here, b[x + 1])
        wx[x] = cur
        fy = scale * harmonic(here, next_y(here))
        wy[x] = fy
        fz = jnp.where(inside, scale * harmonic(here, next_z(here)), F32(0.0))
        wz[x] = fz
        fl = last_z(fz)
        wl[x] = fl
        r = step_of((prev + cur) + (fy + last_y(fy)) + (fz + fl) + c[x])
        rd[x] = r
        v[x] = r * g[x]
        return cur

    lax.fori_loop(low, high, body, prev, unroll=unroll)


def row_residual(v, s, x, prev):
    wx, wy, wz, wl, rd, c, g = s
    here = v[x]
    cur = wx[x] * (here - v[x + 1])
    fy = wy[x] * (here - next_y(here))
    fz = wz[x] * (here - next_z(here)) + wl[x] * (here - last_z(here))
    flux = (cur - prev) + (fy - last_y(fy)) + fz
    return here, g[x] - (flux + c[x] * here), cur


def sweep(src, dst, s, low, high, unroll):
    rd = s[4]

    def body(x, prev):
        here, res, cur = row_residual(src, s, x, prev)
        dst[x] = here + rd[x] * res
        return cur

    first = s[0][low - 1] * (src[low - 1] - src[low])
    lax.fori_loop(low, high, body, first, unroll=unroll)


def residual_rows(v, s, low, high):
    prev = s[0][low - 1] * (v[low - 1] - v[low])
    for x in range(low, high):
        here, res, prev = row_residual(v, s, x, prev)
        yield x, here, res


def gate(inside, value):
    return jnp.where(inside, value, F32(0.0))


def k_pack_x0(idx, m, f, g, low, high, b0, c0, g0, mv, fv, sems):
    copies = [
        pltpu.make_async_copy(m, mv, sems.at[0]),
        pltpu.make_async_copy(f, fv, sems.at[1]),
        pltpu.make_async_copy(g, g0, sems.at[2]),
    ]
    for copy in copies:
        copy.start()
    copies[0].wait()
    for x in range(8):
        b0[x] = inverse_density(mv[x])
    for k in range(4):
        low[k] = gate(idx[0] > 0, b0[k])
        high[k] = gate(idx[0] < idx[2] - 1, b0[4 + k])
    copies[1].wait()
    for x in range(8):
        c0[x] = reaction_of(fv[x])
    for k in range(3):
        low[4 + k] = c0[k]
        high[4 + k] = c0[5 + k]
    copies[2].wait()
    for k in range(3):
        low[7 + k] = g0[k]
        high[7 + k] = g0[5 + k]


def split_pair(tmp, k, value):
    for h in range(2):
        tmp[k, h] = value[:, 128 * h : 128 * h + 128]


def k_coefs(b0, c0, b1, c1, bc2, tmp0, tmp1):
    for k, (src, out) in enumerate(((b0, b1), (c0, c1))):
        for x in range(4):
            split_pair(tmp0, x, src[2 * x] + src[2 * x + 1])
        t = fold_level0(tmp0)
        for x in range(4):
            out[x] = t[16 * x : 16 * x + 16]
        for x in range(2):
            tmp1[x] = t[32 * x : 32 * x + 16] + t[32 * x + 16 : 32 * x + 32]
        bc2[k] = fold_level1(tmp1)


def strip_tiles(out, t, value):
    out[t, 0:4, :] = value[:, 0:128]
    out[t, 4:8, :] = value[:, 128:256]


def k_pack_y0(idx, b0, c0, g0, below, above, low, high):
    for out, at, inside in ((low, 0, idx[1] > 0), (high, 28, idx[1] < idx[3] - 1)):
        cut = pl.ds(at, 4)
        t = 0
        for own, base, reach in ((b0, 0, 4), (c0, 4, 3), (g0, 7, 3)):
            for x in range(-reach, 8 + reach):
                if x < 0:
                    val = below[base + x + reach, cut, :]
                elif x < 8:
                    val = own[x, cut, :]
                else:
                    val = above[base + x - 8, cut, :]
                strip_tiles(out, t, gate(inside, val) if base == 0 else val)
                t += 1


def put_strips0(ext, first_row, count, buf, base, high):
    at = 40 if high else 4
    for k in range(count):
        ext[first_row + k, at : at + 4, 0:128] = buf[base + k, 0:4, :]
        ext[first_row + k, at : at + 4, 128:256] = buf[base + k, 4:8, :]


def assemble0(b0, c0, g0, below, above, left, right, be, ce, ge):
    zeros = jnp.zeros((8, 256), F32)
    for ext, own, base, reach, strips in (
        (be, b0, 0, 4, 0), (ce, c0, 4, 3, 16), (ge, g0, 7, 3, 30)
    ):
        for x in range(16):
            ext[x, 0:8, :] = zeros
            ext[x, 40:48, :] = zeros
        for x in range(-reach, 8 + reach):
            if x < 0:
                val = below[base + x + reach]
            elif x < 8:
                val = own[x]
            else:
                val = above[base + x - 8]
            ext[4 + x, 8:40, :] = val
        put_strips0(ext, 4 - reach, 8 + 2 * reach, left, strips, False)
        put_strips0(ext, 4 - reach, 8 + 2 * reach, right, strips, True)


def k_descend0(
    idx, b0, c0, g0, below, above, left, right, b1, c1,
    v0, g1, low, high,
    be, ce, ge, wx, wy, wz, wl, rd, va, vb, tmp,
):
    assemble0(b0, c0, g0, below, above, left, right, be, ce, ge)
    s = (wx, wy, wz, wl, rd, ce, ge)
    weights(be, s, va, 1.0, 1, 15, 7)
    sweep(va, vb, s, 2, 14, 6)
    sweep(vb, va, s, 3, 13, 5)
    for x in range(8):
        v0[x] = va[4 + x, 8:40, :]
    kept = None
    for x, here, res in residual_rows(va, s, 4, 12):
        if x % 2 == 0:
            kept = res[8:40, :]
        else:
            split_pair(tmp, (x - 4) // 2, kept + res[8:40, :])
    t = fold_level0(tmp)
    for x in range(4):
        g1[x] = t[16 * x : 16 * x + 16]
        low[x] = gate(idx[0] > 0, b1[x])
        high[x] = gate(idx[0] < idx[2] - 1, b1[x])
    for k in range(3):
        low[4 + k] = c1[k]
        high[4 + k] = c1[1 + k]
        low[7 + k] = t[16 * k : 16 * k + 16]
        high[7 + k] = t[16 * k + 16 : 16 * k + 32]


def k_pack_y1(idx, g1, b1, c1, below, above, low, high):
    for out, at, inside in ((low, 0, idx[1] > 0), (high, 12, idx[1] < idx[3] - 1)):
        cut = pl.ds(at, 4)
        t = 0
        for own, base, reach in ((b1, 0, 4), (c1, 4, 3), (g1, 7, 3)):
            for x in range(-reach, 4 + reach):
                if x < 0:
                    val = below[base + x + reach, cut, :]
                elif x < 4:
                    val = own[x, cut, :]
                else:
                    val = above[base + x - 4, cut, :]
                half = 4 * (t % 2)
                out[t // 2, half : half + 4, :] = gate(inside, val) if base == 0 else val
                t += 1


def k_descend1(
    idx, g1, b1, c1, bc2, v0, below, above, left, right,
    v1, pay, low, high, be, ce, ge,
    wx, wy, wz, wl, rd, va, vb, tmp,
):
    zeros = jnp.zeros((8, 128), F32)
    t = 0
    for ext, own, base, reach in ((be, b1, 0, 4), (ce, c1, 4, 3), (ge, g1, 7, 3)):
        for x in range(12):
            ext[x, 0:8, :] = zeros
            ext[x, 24:32, :] = zeros
        for x in range(-reach, 4 + reach):
            if x < 0:
                val = below[base + x + reach]
            elif x < 4:
                val = own[x]
            else:
                val = above[base + x - 4]
            ext[4 + x, 8:24, :] = val
            half = 4 * (t % 2)
            ext[4 + x, 4:8, :] = left[t // 2, half : half + 4, :]
            ext[4 + x, 24:28, :] = right[t // 2, half : half + 4, :]
            t += 1

    s = (wx, wy, wz, wl, rd, ce, ge)
    weights(be, s, va, 0.25, 1, 11, 10)
    sweep(va, vb, s, 2, 10, 8)
    sweep(vb, va, s, 3, 9, 6)
    for x in range(4):
        v1[x] = va[4 + x, 8:24, :]
    kept = None
    for x, here, res in residual_rows(va, s, 4, 8):
        if x % 2 == 0:
            kept = res[8:24, :]
        else:
            tmp[(x - 4) // 2] = kept + res[8:24, :]
    g2 = fold_level1(tmp)
    for k in range(8):
        pay[k, 0] = g2
        pay[k, 1] = bc2[0]
        pay[k, 2] = bc2[1]

    for out, first in ((low, 0), (high, 5)):
        for k in range(3):
            for q in range(2):
                for h in range(2):
                    out[4 * k + 2 * q + h] = v0[
                        first + k, 16 * q : 16 * q + 16, 128 * h : 128 * h + 128
                    ]
        for k in range(4):
            out[12 + k] = va[4 + k, 8:24, :]


def k_pack_y2(idx, v0, v1, below, above, gathered, low, high):
    for out, is_high, inside in (
        (low, False, idx[1] > 0), (high, True, idx[1] < idx[3] - 1)
    ):
        for k in range(3):
            for i in range(8):
                val = gathered[i, k]
                out[8 * k + i] = gate(inside, val) if k == 1 else val
        cut = pl.ds(28 if is_high else 0, 4)
        part = pl.ds(12 if is_high else 0, 4)
        q = 1 if is_high else 0
        for t, x in enumerate(range(-3, 11)):
            if 0 <= x < 8:
                strip_tiles(out, 24 + t, v0[x, cut, :])
            else:
                src = below if x < 0 else above
                k = 4 * (x + 3 if x < 0 else x - 8) + 2 * q
                for h in range(2):
                    out[24 + t, 4 * h : 4 * h + 4, :] = src[k + h, part, :]
        for t, x in enumerate(range(-4, 8)):
            if x < 0:
                val = below[12 + x + 4, part, :]
            elif x < 4:
                val = v1[x, part, :]
            else:
                val = above[12 + x - 4, part, :]
            half = 4 * (t % 2)
            out[38 + t // 2, half : half + 4, :] = val


def upper(shape):
    return iota(shape, len(shape) - 1) >= 64


def pair_next(v):
    mask = upper(v[0].shape)
    out = []
    for i in range(8):
        after = v[i + 1] if i < 7 else jnp.zeros_like(v[0])
        out.append(pltpu.roll(jnp.where(mask, v[i], after), 64, 1))
    return out


def pair_last(f):
    mask = upper(f[0].shape)
    out = []
    for i in range(8):
        before = f[i - 1] if i > 0 else jnp.zeros_like(f[0])
        out.append(pltpu.roll(jnp.where(mask, before, f[i]), 64, 1))
    return out


def weights2(b, c, scaling):
    scale = F32(scaling)
    inside = iota(b[0].shape, 1) % 64 < 63
    wx = [scale * harmonic(p, q) for p, q in zip(b, pair_next(b))]
    wy = [scale * harmonic(p, next_y(p)) for p in b]
    wz = [jnp.where(inside, scale * harmonic(p, next_z(p)), F32(0.0)) for p in b]
    back = pair_last(wx)
    rd = []
    for i in range(8):
        d = (wx[i] + back[i]) + (wy[i] + last_y(wy[i])) + (wz[i] + last_z(wz[i])) + c[i]
        rd.append(step_of(d))
    return wx, wy, wz, rd


def residual2(v, g, c, wx, wy, wz):
    fx = [w * (p - q) for w, p, q in zip(wx, v, pair_next(v))]
    back = pair_last(fx)
    out = []
    for i in range(8):
        fy = wy[i] * (v[i] - next_y(v[i]))
        fz = wz[i] * (v[i] - next_z(v[i]))
        flux = (fx[i] - back[i]) + (fy - last_y(fy)) + (fz - last_z(fz))
        out.append(g[i] - (flux + c[i] * v[i]))
    return out


def k_descend2(gathered, left, right, v2, pay, wx2, wy2, wz2, rd2, ce2, ge2, be2, tmp):
    for k, ext in enumerate((ge2, be2, ce2)):
        for i in range(8):
            ext[i, 0:8, :] = left[8 * k + i]
            ext[i, 8:16, :] = gathered[i, k]
            ext[i, 16:24, :] = right[8 * k + i]
    b = [be2[i] for i in range(8)]
    c = [ce2[i] for i in range(8)]
    g = [ge2[i] for i in range(8)]
    wx, wy, wz, rd = weights2(b, c, 0.0625)
    for i in range(8):
        wx2[i] = wx[i]
        wy2[i] = wy[i]
        wz2[i] = wz[i]
        rd2[i] = rd[i]
    v = [p * q for p, q in zip(rd, g)]
    for _ in range(2):
        r = residual2(v, g, c, wx, wy, wz)
        v = [p + q * s for p, q, s in zip(v, rd, r)]
    r = residual2(v, g, c, wx, wy, wz)
    for i in range(8):
        v2[i] = v[i]
    for k, src in enumerate((r, b, c)):
        for t in range(2):
            for i in range(8):
                at = 64 * (2 * k + t) + 8 * i
                tmp[at : at + 8, :] = src[i][4 + 8 * t : 12 + 8 * t, :]
    for t, tile in enumerate(fold_level2(tmp[...])):
        pay[t] = tile


TILES = 6


def block_next(v):
    head = iota(v[0].shape, 1) < 32
    out = []
    for t in range(TILES):
        after = v[t + 1] if t < TILES - 1 else jnp.zeros_like(v[0])
        out.append(pltpu.roll(jnp.where(head, after, v[t]), 96, 1))
    return out


def block_last(f):
    tail = iota(f[0].shape, 1) >= 96
    out = []
    for t in range(TILES):
        before = f[t - 1] if t > 0 else jnp.zeros_like(f[0])
        out.append(pltpu.roll(jnp.where(tail, before, f[t]), 32, 1))
    return out


def solve3(g, b, c):
    scale = F32(0.015625)
    shape = g[0].shape
    inside_x = iota(shape, 0) < 7
    inside_z = iota(shape, 1) % 32 < 31
    zero = F32(0.0)
    wx = [jnp.where(inside_x, scale * harmonic(p, next_y(p)), zero) for p in b]
    wy = [scale * harmonic(p, q) for p, q in zip(b, block_next(b))]
    wz = [jnp.where(inside_z, scale * harmonic(p, next_z(p)), zero) for p in b]
    xl = [last_y(p) for p in wx]
    yl = block_last(wy)
    zl = [last_z(p) for p in wz]
    rd = []
    for t in range(TILES):
        d = (wx[t] + xl[t]) + (wy[t] + yl[t]) + (wz[t] + zl[t]) + c[t]
        rd.append(step_of(d))
    e = [p * q for p, q in zip(rd, g)]
    for _ in range(7):
        up = block_next(e)
        down = block_last(e)
        new = []
        for t in range(TILES):
            h = e[t]
            flux = wx[t] * (h - next_y(h)) + xl[t] * (h - last_y(h))
            flux = flux + (wy[t] * (h - up[t]) + yl[t] * (h - down[t]))
            flux = flux + (wz[t] * (h - next_z(h)) + zl[t] * (h - last_z(h)))
            new.append(h + rd[t] * (g[t] - (flux + c[t] * h)))
        e = new
    return e


def k_prepare(
    b0, c0, g0, below0, above0, left0, right0, be1, ce1, ge1,
    v0, v1, below, above, left, right,
    p0, ce, ge, wx, wy, wz, wl, rd, p1, wx1, wy1, wz1, wl1, rd1,
    be, va, va1,
):
    assemble0(b0, c0, g0, below0, above0, left0, right0, be, ce, ge)
    weights(be, (wx, wy, wz, wl, rd, ce, ge), va, 1.0, 2, 14, 6)
    weights(be1, (wx1, wy1, wz1, wl1, rd1, ce1, ge1), va1, 0.25, 1, 11, 10)
    narrow = jnp.zeros((8, 128), F32)
    wide = jnp.zeros((8, 256), F32)
    for t, x in enumerate(range(-4, 8)):
        p1[t, 0:8, :] = narrow
        p1[t, 24:32, :] = narrow
        if x < 0:
            p1[t, 8:24, :] = below[12 + x + 4]
        elif x < 4:
            p1[t, 8:24, :] = v1[x]
        else:
            p1[t, 8:24, :] = above[12 + x - 4]
        half = 4 * (t % 2)
        p1[t, 4:8, :] = left[38 + t // 2, half : half + 4, :]
        p1[t, 24:28, :] = right[38 + t // 2, half : half + 4, :]
    for x in range(-3, 11):
        p0[4 + x, 0:8, :] = wide
        p0[4 + x, 40:48, :] = wide
        if 0 <= x < 8:
            p0[4 + x, 8:40, :] = v0[x]
        else:
            src = below if x < 0 else above
            k = 4 * (x + 3 if x < 0 else x - 8)
            for q in range(2):
                for h in range(2):
                    p0[4 + x, 8 + 16 * q : 24 + 16 * q, 128 * h : 128 * h + 128] = (
                        src[k + 2 * q + h]
                    )
    put_strips0(p0, 1, 14, left, 24, False)
    put_strips0(p0, 1, 14, right, 24, True)


def k_ascend(
    idx, own3, r0, r1, v2, wx2, wy2, wz2, rd2, ce2, ge2,
    p0, ce0, ge0, wx0, wy0, wz0, wl0, rd0,
    p1, ce1, ge1, wx1, wy1, wz1, wl1, rd1,
    pressure, residual,
    all3, m2, p2, p1a, p1b, p0a, p0b, f1, f0,
):
    ix = idx[0]
    iy = idx[1]
    count = idx[3]
    even_chip = lax.rem(iy // 2, 2) == 0
    zero = F32(0.0)

    for k in range(3):
        first = [jnp.where(even_chip, r1[2 * k + t], r0[2 * k + t]) for t in range(2)]
        last = [jnp.where(even_chip, r0[2 * k + t], r1[2 * k + t]) for t in range(2)]
        at = TILES * k
        all3[at] = gate(iy >= 2, first[0])
        all3[at + 1] = jnp.where(iy >= 2, first[1], gate(iy == 1, first[0]))
        all3[at + 2] = own3[2 * k]
        all3[at + 3] = own3[2 * k + 1]
        all3[at + 4] = jnp.where(iy < count - 2, last[0], gate(iy == count - 2, last[1]))
        all3[at + 5] = gate(iy < count - 2, last[1])
    e = solve3(*[[all3[TILES * k + t] for t in range(TILES)] for k in range(3)])

    group = iota((8, 128), 1) // 32 == iota((8, 128), 0) // 2
    for t in range(2):
        for i in range(8):
            row = jnp.broadcast_to(e[2 + t][i : i + 1, :], (8, 128))
            m2[16 * i + 8 * t : 16 * i + 8 * t + 8, :] = jnp.where(group, row, zero)
    spread = jnp.where(
        iota((128, 128), 0) % 32 == (iota((128, 128), 1) % 64) // 2, F32(1.0), zero
    )
    fine = pick(m2[...], spread)
    for i in range(8):
        p2[i] = v2[i]
        p2[i, 4:20, :] += fine[16 * i : 16 * i + 16, :]
    v = [p2[i] for i in range(8)]
    g = [ge2[i] for i in range(8)]
    c = [ce2[i] for i in range(8)]
    wx = [wx2[i] for i in range(8)]
    wy = [wy2[i] for i in range(8)]
    wz = [wz2[i] for i in range(8)]
    for _ in range(2):
        r = residual2(v, g, c, wx, wy, wz)
        v = [v[i] + rd2[i] * r[i] for i in range(8)]
    for i in range(8):
        p2[i] = v[i]

    parts = []
    for q in range(3):
        at = ix + (q - 1)
        inside = jnp.logical_and(at >= 0, at < idx[2])
        parts.append(jnp.where(inside, p2[jnp.clip(at, 0, 7), 4:20, :], zero))
    row = iota((128, 256), 0)
    lane = iota((128, 256), 1)
    hit = (row % 64 == (lane % 128) // 2) & (row // 64 == lane // 128)
    fine = pick(jnp.concatenate(parts, axis=0), jnp.where(hit, F32(1.0), zero))
    for q in range(3):
        for h in range(2):
            part = fine[16 * q : 16 * q + 16, 128 * h : 128 * h + 128]
            f1[2 * q + h, pl.ds(0, 16, stride=2), :] = part
            f1[2 * q + h, pl.ds(1, 16, stride=2), :] = part
    for x in range(12):
        p1a[x] = p1[x] + f1[x // 2]
    s1 = (wx1, wy1, wz1, wl1, rd1, ce1, ge1)
    sweep(p1a, p1b, s1, 1, 11, 10)
    sweep(p1b, p1a, s1, 2, 10, 8)

    wide = jnp.where(iota((128, 256), 0) == iota((128, 256), 1) // 2, F32(1.0), zero)
    fine = pick(jnp.concatenate([p1a[2 + x, 4:28, :] for x in range(8)], axis=0), wide)
    for x in range(8):
        for h in range(2):
            part = fine[24 * x : 24 * x + 24, 128 * h : 128 * h + 128]
            f0[x, h, pl.ds(0, 24, stride=2), :] = part
            f0[x, h, pl.ds(1, 24, stride=2), :] = part
    for x in range(1, 15):
        for h in range(2):
            cut = pl.ds(128 * h, 128)
            p0a[x, :, cut] = p0[x, :, cut] + f0[x // 2, h]
    s0 = (wx0, wy0, wz0, wl0, rd0, ce0, ge0)
    sweep(p0a, p0b, s0, 2, 14, 6)
    sweep(p0b, p0a, s0, 3, 13, 5)
    for x, here, res in residual_rows(p0a, s0, 4, 12):
        pressure[x - 4] = here[8:40, :]
        residual[x - 4] = res[8:40, :]


def call(kernel, name, outs, scratch, limit, *args, anywhere=()):
    vmem = pl.BlockSpec(memory_space=pltpu.VMEM)
    smem = pl.BlockSpec(memory_space=pltpu.SMEM)
    hbm = pl.BlockSpec(memory_space=pltpu.HBM)
    specs = [smem if a.ndim == 1 else vmem for a in args]
    for k in anywhere:
        specs[k] = hbm
    return pl.pallas_call(
        kernel,
        name=name,
        out_shape=[jax.ShapeDtypeStruct(s, F32) for s in outs],
        in_specs=specs,
        out_specs=[vmem for _ in outs],
        scratch_shapes=[pltpu.VMEM(s, F32) if isinstance(s, tuple) else s for s in scratch],
        compiler_params=pltpu.CompilerParams(vmem_limit_bytes=limit * MIB),
    )(*args)


B0 = (8, 32, 256)
E0 = (16, 48, 256)
E1 = (12, 32, 128)
E2 = (8, 24, 128)


def per_device(source, material, flags):
    idx = jnp.stack(
        [
            lax.axis_index("gx").astype(jnp.int32),
            lax.axis_index("gy").astype(jnp.int32),
            jnp.int32(lax.axis_size("gx")),
            jnp.int32(lax.axis_size("gy")),
        ]
    )

    low, high, b0, c0, g0 = call(
        k_pack_x0, "pack_x0", [(10, 32, 256)] * 2 + [B0] * 3,
        [pltpu.VMEM(B0, jnp.int32), pltpu.VMEM(B0, jnp.int32), pltpu.SemaphoreType.DMA((3,))],
        4, idx, material, flags, source, anywhere=(1, 2, 3),
    )
    below0, above0 = exchange(low, high, "gx")
    b1, c1, bc2 = call(
        k_coefs, "coefs", [(4, 16, 128), (4, 16, 128), (2, 8, 128)],
        [(4, 2, 32, 128), (2, 16, 128)], 4, b0, c0,
    )
    low, high = call(
        k_pack_y0, "pack_y0", [(44, 8, 128)] * 2, [], 4, idx, b0, c0, g0, below0, above0
    )
    left0, right0 = exchange(low, high, "gy")
    blocks0 = (b0, c0, g0, below0, above0, left0, right0)
    v0, g1, low, high = call(
        k_descend0, "descend0",
        [B0, (4, 16, 128), (10, 16, 128), (10, 16, 128)],
        [E0] * 10 + [(4, 2, 32, 128)], 12,
        idx, *blocks0, b1, c1,
    )
    below, above = exchange(low, high, "gx")
    low, high = call(
        k_pack_y1, "pack_y1", [(16, 8, 128)] * 2, [], 4, idx, g1, b1, c1, below, above
    )
    left, right = exchange(low, high, "gy")
    v1, pay, low, high, be1, ce1, ge1 = call(
        k_descend1, "descend1",
        [(4, 16, 128), (8, 3, 8, 128), (16, 16, 128), (16, 16, 128)] + [E1] * 3,
        [E1] * 7 + [(2, 16, 128)], 4,
        idx, g1, b1, c1, bc2, v0, below, above, left, right,
    )
    gathered = lax.all_to_all(pay, "gx", 0, 0)
    below, above = exchange(low, high, "gx")
    low, high = call(
        k_pack_y2, "pack_y2", [(44, 8, 128)] * 2, [], 4, idx, v0, v1, below, above, gathered
    )
    left, right = exchange(low, high, "gy")
    v2, own3, *s2 = call(
        k_descend2, "descend2", [E2, (6, 8, 128)] + [E2] * 6, [E2, (384, 128)], 4,
        gathered, left, right,
    )
    r0, r1 = swap_chips(own3, "gy", 0), swap_chips(own3, "gy", 1)
    p0, ce0, ge0, wx0, wy0, wz0, wl0, rd0, p1, *w1 = call(
        k_prepare, "prepare", [E0] * 8 + [E1] * 6, [E0, E0, E1], 8,
        *blocks0, be1, ce1, ge1, v0, v1, below, above, left, right,
    )
    pressure, residual = call(
        k_ascend, "ascend", [B0] * 2,
        [(18, 8, 128), (128, 128), E2, E1, E1, E0, E0, (6, 32, 128), (8, 2, 48, 128)], 8,
        idx, own3, r0, r1, v2, *s2,
        p0, ce0, ge0, wx0, wy0, wz0, wl0, rd0, p1, ce1, ge1, *w1,
    )
    return pressure, residual


def solution(mesh):
    spec = P("gx", "gy", None)
    return jax.shard_map(
        per_device,
        mesh=mesh,
        in_specs=(spec, spec, spec),
        out_specs=(spec, spec),
        check_vma=False,
    )
```

time: 603 us -> 79.3 us (0.13)
  the two profiles are of different devices: /device:TPU:7 before, /device:TPU:2 now
where the time goes in v2:
time: 79.3 us; the launch traced here: 79.1 us
  starting transfers between devices  33.8 us (43%)
  waiting for transfers between devices  26.9 us (34%)
  Pallas kernels  14.7 us (19%)
  local copies, waits for them, and re-layouts  2.85 us (4%)
    ppermute x12, waiting for transfers between devices, shift(): lax.ppermute(block, axis, [(i, (i + step) % count) for i in range(count)])  24 us
    ppermute x12, starting transfers between devices, shift(): lax.ppermute(block, axis, [(i, (i + step) % count) for i in range(count)])  18.1 us
    pallas_call x10, Pallas kernels, call(): pl.pallas_call(kernel, name=name, out_shape=[jax.ShapeDtypeStruct(s, F32)...  14.7 us
    ppermute x2, starting transfers between devices, swap_chips(): return lax.ppermute(block, axis, pairs + [(b, a) for a, b in pairs])  9.27 us
    all_to_all x1, starting transfers between devices, per_device(): gathered = lax.all_to_all(pay, 'gx', 0, 0)  6.44 us
    unnamed x6, local copies, waits for them, and re-layouts  2.85 us
    ppermute x2, waiting for transfers between devices, swap_chips(): return lax.ppermute(block, axis, pairs + [(b, a) for a, b in pairs])  2.61 us
  transfers between devices with their start and end apart: 15, of which 9 were waited for; matrix products, arithmetic and copies ran while one was open for 0% of the time, Pallas kernels for 2%

profile of v2, /device:TPU:2, one launch (start us, length us, event | category | flops | bytes accessed | tf_op | source)
XLA Modules:
  0.0 79.1 jit_solution(14499744965556060743)
XLA Ops:
  0.7 0.9 %copy-done = s32[8,32,256]{2,1,0:T(8,128)S(1)} copy-done((s32[8,32,256]{2,1,0:T(8,128)S(1)}, s32[8,32,256]{2,1,0:T(8,128)}, u32[]{:S(2)}) %copy-start) | copy-done | bytes 262168
  1.7 0.9 %copy-done.1 = s32[8,32,256]{2,1,0:T(8,128)S(1)} copy-done((s32[8,32,256]{2,1,0:T(8,128)S(1)}, s32[8,32,256]{2,1,0:T(8,128)}, u32[]{:S(2)}) %copy-start.1) | copy-done | bytes 262168
  4.3 2.0 %collective-permute-start = (f32[10,32,256]{2,1,0:T(8,128)S(1)}, f32[10,32,256]{2,1,0:T(8,128)S(1)}, u32[]{:S(2)}, u32[]{:S(2)}) collective-permute-start(f32[10,32,256]{2,1,0:T(8,128)S(1)} %get-tuple-element.52), channel_id=1, source_target_pairs={{0,32},{32,64},{64,96},{96,128},{128,160},{160,192},{192,224},{224... | collective-permute-start | bytes 983048 | tf_op jit(solution)/shard_map/ppermute | solution.py:20
  6.3 4.0 %collective-permute-start.1 = (f32[10,32,256]{2,1,0:T(8,128)S(1)}, f32[10,32,256]{2,1,0:T(8,128)S(1)}, u32[]{:S(2)}, u32[]{:S(2)}) collective-permute-start(f32[10,32,256]{2,1,0:T(8,128)S(1)} %get-tuple-element.53), channel_id=1, source_target_pairs={{0,224},{32,0},{64,32},{96,64},{128,96},{160,128},{192,160},{224,1... | collective-permute-start | bytes 983048 | tf_op jit(solution)/shard_map/ppermute | solution.py:20
  10.3 7.6 %collective-permute-done.below.below0 = f32[10,32,256]{2,1,0:T(8,128)S(1)} collective-permute-done((f32[10,32,256]{2,1,0:T(8,128)S(1)}, f32[10,32,256]{2,1,0:T(8,128)S(1)}, u32[]{:S(2)}, u32[]{:S(2)}) %collective-permute-start) | collective-permute-done | bytes 327712 | tf_op jit(solution)/shard_map/ppermute | solution.py:20
  18.7 1.7 %collective-permute-start.3 = (f32[44,8,128]{2,1,0:T(8,128)S(1)}, f32[44,8,128]{2,1,0:T(8,128)S(1)}, u32[]{:S(2)}, u32[]{:S(2)}) collective-permute-start(f32[44,8,128]{2,1,0:T(8,128)S(1)} %get-tuple-element.55), channel_id=1, source_target_pairs={{0,31},{1,0},{2,1},{3,2},{4,3},{5,4},{6,5},{7,6},{8,7},{9,8},{10,9... | collective-permute-start | bytes 540680 | tf_op jit(solution)/shard_map/ppermute | solution.py:20
  20.9 2.7 %collective-permute-done.2.left.left0 = f32[44,8,128]{2,1,0:T(8,128)S(1)} collective-permute-done((f32[44,8,128]{2,1,0:T(8,128)S(1)}, f32[44,8,128]{2,1,0:T(8,128)S(1)}, u32[]{:S(2)}, u32[]{:S(2)}) %collective-permute-start.2) | collective-permute-done | bytes 180256 | tf_op jit(solution)/shard_map/ppermute | solution.py:20
  23.6 3.2 %descend0.1 = (f32[8,32,256]{2,1,0:T(8,128)S(1)}, f32[4,16,128]{2,1,0:T(8,128)S(1)}, f32[10,16,128]{2,1,0:T(8,128)S(1)}, f32[10,16,128]{2,1,0:T(8,128)S(1)}) custom-call(s32[4]{0:T(128)S(1)} %pad_add_fusion.idx, f32[8,32,256]{2,1,0:T(8,128)S(1)} %get-tuple-element.49.b0, f32[8,32,256]{2,1,0:T(8,128)S(1)} %get-tuple-element.50.c0, ...), custom_call_target="tpu_custom_call" | custom-call | tf_op jit(solution)/shard_map/descend0/pallas_call | solution.py:666
  26.8 3.2 %collective-permute-start.5 = (f32[10,16,128]{2,1,0:T(8,128)S(1)}, f32[10,16,128]{2,1,0:T(8,128)S(1)}, u32[]{:S(2)}, u32[]{:S(2)}) collective-permute-start(f32[10,16,128]{2,1,0:T(8,128)S(1)} %get-tuple-element.62), channel_id=1, source_target_pairs={{0,224},{32,0},{64,32},{96,64},{128,96},{160,128},{192,160},{224,1... | collective-permute-start | bytes 245768 | tf_op jit(solution)/shard_map/ppermute | solution.py:20
  30.1 2.6 %collective-permute-done.4.below = f32[10,16,128]{2,1,0:T(8,128)S(1)} collective-permute-done((f32[10,16,128]{2,1,0:T(8,128)S(1)}, f32[10,16,128]{2,1,0:T(8,128)S(1)}, u32[]{:S(2)}, u32[]{:S(2)}) %collective-permute-start.4) | collective-permute-done | bytes 81952 | tf_op jit(solution)/shard_map/ppermute | solution.py:20
  33.8 1.3 %collective-permute-start.7 = (f32[16,8,128]{2,1,0:T(8,128)S(1)}, f32[16,8,128]{2,1,0:T(8,128)S(1)}, u32[]{:S(2)}, u32[]{:S(2)}) collective-permute-start(f32[16,8,128]{2,1,0:T(8,128)S(1)} %get-tuple-element.64), channel_id=1, source_target_pairs={{0,31},{1,0},{2,1},{3,2},{4,3},{5,4},{6,5},{7,6},{8,7},{9,8},{10,9... | collective-permute-start | bytes 196616 | tf_op jit(solution)/shard_map/ppermute | solution.py:20
  35.1 1.9 %collective-permute-done.6.left = f32[16,8,128]{2,1,0:T(8,128)S(1)} collective-permute-done((f32[16,8,128]{2,1,0:T(8,128)S(1)}, f32[16,8,128]{2,1,0:T(8,128)S(1)}, u32[]{:S(2)}, u32[]{:S(2)}) %collective-permute-start.6) | collective-permute-done | bytes 65568 | tf_op jit(solution)/shard_map/ppermute | solution.py:20
  37.0 1.8 %descend1.1 = (f32[4,16,128]{2,1,0:T(8,128)S(1)}, f32[8,3,8,128]{3,2,1,0:T(8,128)}, f32[16,16,128]{2,1,0:T(8,128)S(1)}, f32[16,16,128]{2,1,0:T(8,128)S(1)}, f32[...) custom-call(s32[4]{0:T(128)S(1)} %pad_add_fusion.idx, ...), custom_call_target="tpu_custom_call" | custom-call | tf_op jit(solution)/shard_map/descend1/pallas_call | solution.py:666
  38.8 6.4 %all-to-all-start = ((f32[8,3,8,128]{3,2,1,0:T(8,128)}), f32[8,3,8,128]{3,2,1,0:T(8,128)S(1)}, u32[]{:S(2)}, u32[]{:S(2)}) async-start(f32[8,3,8,128]{3,2,1,0:T(8,128)} %get-tuple-element.65), calls=%async_computation | async-start | bytes 196608 | tf_op jit(solution)/shard_map/all_to_all | solution.py:725
  45.3 2.0 %collective-permute-start.8 = (f32[16,16,128]{2,1,0:T(8,128)S(1)}, f32[16,16,128]{2,1,0:T(8,128)S(1)}, u32[]{:S(2)}, u32[]{:S(2)}) collective-permute-start(f32[16,16,128]{2,1,0:T(8,128)S(1)} %get-tuple-element.67), channel_id=1, source_target_pairs={{0,32},{32,64},{64,96},{96,128},{128,160},{160,192},{192,224},{224... | collective-permute-start | bytes 393224 | tf_op jit(solution)/shard_map/ppermute | solution.py:20
  47.3 1.2 %collective-permute-start.9 = (f32[16,16,128]{2,1,0:T(8,128)S(1)}, f32[16,16,128]{2,1,0:T(8,128)S(1)}, u32[]{:S(2)}, u32[]{:S(2)}) collective-permute-start(f32[16,16,128]{2,1,0:T(8,128)S(1)} %get-tuple-element.68), channel_id=1, source_target_pairs={{0,224},{32,0},{64,32},{96,64},{128,96},{160,128},{192,160},{224,1... | collective-permute-start | bytes 393224 | tf_op jit(solution)/shard_map/ppermute | solution.py:20
  48.5 5.9 %collective-permute-done.8.below = f32[16,16,128]{2,1,0:T(8,128)S(1)} collective-permute-done((f32[16,16,128]{2,1,0:T(8,128)S(1)}, f32[16,16,128]{2,1,0:T(8,128)S(1)}, u32[]{:S(2)}, u32[]{:S(2)}) %collective-permute-start.8) | collective-permute-done | bytes 131104 | tf_op jit(solution)/shard_map/ppermute | solution.py:20
  55.7 1.5 %collective-permute-start.11 = (f32[44,8,128]{2,1,0:T(8,128)S(1)}, f32[44,8,128]{2,1,0:T(8,128)S(1)}, u32[]{:S(2)}, u32[]{:S(2)}) collective-permute-start(f32[44,8,128]{2,1,0:T(8,128)S(1)} %get-tuple-element.70), channel_id=1, source_target_pairs={{0,31},{1,0},{2,1},{3,2},{4,3},{5,4},{6,5},{7,6},{8,7},{9,8},{10,9... | collective-permute-start | bytes 540680 | tf_op jit(solution)/shard_map/ppermute | solution.py:20
  57.2 3.2 %collective-permute-done.10.left = f32[44,8,128]{2,1,0:T(8,128)S(1)} collective-permute-done((f32[44,8,128]{2,1,0:T(8,128)S(1)}, f32[44,8,128]{2,1,0:T(8,128)S(1)}, u32[]{:S(2)}, u32[]{:S(2)}) %collective-permute-start.10) | collective-permute-done | bytes 180256 | tf_op jit(solution)/shard_map/ppermute | solution.py:20
  60.4 1.0 %descend2.1 = (f32[8,24,128]{2,1,0:T(8,128)S(1)}, f32[6,8,128]{2,1,0:T(8,128)S(1)}, f32[8,24,128]{2,1,0:T(8,128)S(1)}, f32[8,24,128]{2,1,0:T(8,128)S(1)}, f32[8,...) custom-call(f32[8,3,8,128]{3,2,1,0:T(8,128)S(1)} %all-to-all-done.gather, ...), custom_call_target="tpu_custom_call" | custom-call | tf_op jit(solution)/shard_map/descend2/pallas_call | solution.py:666
  61.4 9.3 %collective-permute-start.12 = (f32[6,8,128]{2,1,0:T(8,128)S(1)}, f32[6,8,128]{2,1,0:T(8,128)S(1)}, u32[]{:S(2)}, u32[]{:S(2)}) collective-permute-start(f32[6,8,128]{2,1,0:T(8,128)S(1)} %get-tuple-element.71.own3), channel_id=1, source_target_pairs={{0,2},{1,3},{4,6},{5,7},{8,10},{9,11},{12,14},{13,15},{16,18},{17,... | collective-permute-start | bytes 73736 | tf_op jit(solution)/shard_map/ppermute | solution.py:32
  70.7 1.2 %prepare.1 = (f32[16,48,256]{2,1,0:T(8,128)S(1)}, f32[16,48,256]{2,1,0:T(8,128)S(1)}, f32[16,48,256]{2,1,0:T(8,128)S(1)}, f32[16,48,256]{2,1,0:T(8,128)S(1)}, f3...) custom-call(f32[8,32,256]{2,1,0:T(8,128)S(1)} %get-tuple-element.49., ...), custom_call_target="tpu_custom_call" | custom-call | tf_op jit(solution)/shard_map/prepare/pallas_call | solution.py:666
  72.5 2.0 %collective-permute-done.13.r1 = f32[6,8,128]{2,1,0:T(8,128)S(1)} collective-permute-done((f32[6,8,128]{2,1,0:T(8,128)S(1)}, f32[6,8,128]{2,1,0:T(8,128)S(1)}, u32[]{:S(2)}, u32[]{:S(2)}) %collective-permute-start.13) | collective-permute-done | bytes 24608 | tf_op jit(solution)/shard_map/ppermute | solution.py:32
  74.5 4.6 %ascend.1 = (f32[8,32,256]{2,1,0:T(8,128)}, f32[8,32,256]{2,1,0:T(8,128)}) custom-call(s32[4]{0:T(128)S(1)} %pad_add_fusion.idx, f32[6,8,128]{2,1,0:T(8,128)S(1)} %get-tuple-element.71.own3, f32[6,8,128]{2,1,0:T(8,128)S(1)} %collective-permute-done.12.r0, f32[6,8,128]{2,1,0:T(8,128)S(1)} %collective-permute-done.13.r1, ...), custom_call_target="tpu_custom_call" | custom-call | tf_op jit(solution)/shard_map/ascend/pallas_call | solution.py:666
  (23 shorter events, 6.0 us)
Async XLA Ops:
  0.7 1.0 %copy-start = (s32[8,32,256]{2,1,0:T(8,128)S(1)}, s32[8,32,256]{2,1,0:T(8,128)}, u32[]{:S(2)}) copy-start(s32[8,32,256]{2,1,0:T(8,128)} %m.1) | copy-start | bytes 786436
  1.7 0.9 %copy-start.1 = (s32[8,32,256]{2,1,0:T(8,128)S(1)}, s32[8,32,256]{2,1,0:T(8,128)}, u32[]{:S(2)}) copy-start(s32[8,32,256]{2,1,0:T(8,128)} %f.1) | copy-start | bytes 786436
  2.6 0.9 %copy-start.2 = (f32[8,32,256]{2,1,0:T(8,128)S(1)}, f32[8,32,256]{2,1,0:T(8,128)}, u32[]{:S(2)}) copy-start(f32[8,32,256]{2,1,0:T(8,128)} %g.1) | copy-start | bytes 786436
  4.3 13.6 %collective-permute-start = (f32[10,32,256]{2,1,0:T(8,128)S(1)}, f32[10,32,256]{2,1,0:T(8,128)S(1)}, u32[]{:S(2)}, u32[]{:S(2)}) collective-permute-start(f32[10,32,256]{2,1,0:T(8,128)S(1)} %get-tuple-element.52), channel_id=1, source_target_pairs={{0,32},{32,64},{64,96},{96,128},{128,160},{160,192},{192,224},{224... | collective-permute-start | bytes 983048 | tf_op jit(solution)/shard_map/ppermute | solution.py:20
  6.3 11.7 %collective-permute-start.1 = (f32[10,32,256]{2,1,0:T(8,128)S(1)}, f32[10,32,256]{2,1,0:T(8,128)S(1)}, u32[]{:S(2)}, u32[]{:S(2)}) collective-permute-start(f32[10,32,256]{2,1,0:T(8,128)S(1)} %get-tuple-element.53), channel_id=1, source_target_pairs={{0,224},{32,0},{64,32},{96,64},{128,96},{160,128},{192,160},{224,1... | collective-permute-start | bytes 983048 | tf_op jit(solution)/shard_map/ppermute | solution.py:20
  18.6 5.0 %collective-permute-start.2 = (f32[44,8,128]{2,1,0:T(8,128)S(1)}, f32[44,8,128]{2,1,0:T(8,128)S(1)}, u32[]{:S(2)}, u32[]{:S(2)}) collective-permute-start(f32[44,8,128]{2,1,0:T(8,128)S(1)} %get-tuple-element.54), channel_id=1, source_target_pairs={{0,1},{1,2},{2,3},{3,4},{4,5},{5,6},{6,7},{7,8},{8,9},{9,10},{10,1... | collective-permute-start | bytes 540680 | tf_op jit(solution)/shard_map/ppermute | solution.py:20
  18.7 4.9 %collective-permute-start.3 = (f32[44,8,128]{2,1,0:T(8,128)S(1)}, f32[44,8,128]{2,1,0:T(8,128)S(1)}, u32[]{:S(2)}, u32[]{:S(2)}) collective-permute-start(f32[44,8,128]{2,1,0:T(8,128)S(1)} %get-tuple-element.55), channel_id=1, source_target_pairs={{0,31},{1,0},{2,1},{3,2},{4,3},{5,4},{6,5},{7,6},{8,7},{9,8},{10,9... | collective-permute-start | bytes 540680 | tf_op jit(solution)/shard_map/ppermute | solution.py:20
  26.8 5.9 %collective-permute-start.4 = (f32[10,16,128]{2,1,0:T(8,128)S(1)}, f32[10,16,128]{2,1,0:T(8,128)S(1)}, u32[]{:S(2)}, u32[]{:S(2)}) collective-permute-start(f32[10,16,128]{2,1,0:T(8,128)S(1)} %get-tuple-element.61), channel_id=1, source_target_pairs={{0,32},{32,64},{64,96},{96,128},{128,160},{160,192},{192,224},{224... | collective-permute-start | bytes 245768 | tf_op jit(solution)/shard_map/ppermute | solution.py:20
  26.8 5.8 %collective-permute-start.5 = (f32[10,16,128]{2,1,0:T(8,128)S(1)}, f32[10,16,128]{2,1,0:T(8,128)S(1)}, u32[]{:S(2)}, u32[]{:S(2)}) collective-permute-start(f32[10,16,128]{2,1,0:T(8,128)S(1)} %get-tuple-element.62), channel_id=1, source_target_pairs={{0,224},{32,0},{64,32},{96,64},{128,96},{160,128},{192,160},{224,1... | collective-permute-start | bytes 245768 | tf_op jit(solution)/shard_map/ppermute | solution.py:20
  33.3 3.8 %collective-permute-start.6 = (f32[16,8,128]{2,1,0:T(8,128)S(1)}, f32[16,8,128]{2,1,0:T(8,128)S(1)}, u32[]{:S(2)}, u32[]{:S(2)}) collective-permute-start(f32[16,8,128]{2,1,0:T(8,128)S(1)} %get-tuple-element.63), channel_id=1, source_target_pairs={{0,1},{1,2},{2,3},{3,4},{4,5},{5,6},{6,7},{7,8},{8,9},{9,10},{10,1... | collective-permute-start | bytes 196616 | tf_op jit(solution)/shard_map/ppermute | solution.py:20
  33.8 3.2 %collective-permute-start.7 = (f32[16,8,128]{2,1,0:T(8,128)S(1)}, f32[16,8,128]{2,1,0:T(8,128)S(1)}, u32[]{:S(2)}, u32[]{:S(2)}) collective-permute-start(f32[16,8,128]{2,1,0:T(8,128)S(1)} %get-tuple-element.64), channel_id=1, source_target_pairs={{0,31},{1,0},{2,1},{3,2},{4,3},{5,4},{6,5},{7,6},{8,7},{9,8},{10,9... | collective-permute-start | bytes 196616 | tf_op jit(solution)/shard_map/ppermute | solution.py:20
  38.8 16.0 %all-to-all-start = ((f32[8,3,8,128]{3,2,1,0:T(8,128)}), f32[8,3,8,128]{3,2,1,0:T(8,128)S(1)}, u32[]{:S(2)}, u32[]{:S(2)}) async-start(f32[8,3,8,128]{3,2,1,0:T(8,128)} %get-tuple-element.65), calls=%async_computation | async-start | bytes 196608 | tf_op jit(solution)/shard_map/all_to_all | solution.py:725
  45.3 9.2 %collective-permute-start.8 = (f32[16,16,128]{2,1,0:T(8,128)S(1)}, f32[16,16,128]{2,1,0:T(8,128)S(1)}, u32[]{:S(2)}, u32[]{:S(2)}) collective-permute-start(f32[16,16,128]{2,1,0:T(8,128)S(1)} %get-tuple-element.67), channel_id=1, source_target_pairs={{0,32},{32,64},{64,96},{96,128},{128,160},{160,192},{192,224},{224... | collective-permute-start | bytes 393224 | tf_op jit(solution)/shard_map/ppermute | solution.py:20
  47.3 7.2 %collective-permute-start.9 = (f32[16,16,128]{2,1,0:T(8,128)S(1)}, f32[16,16,128]{2,1,0:T(8,128)S(1)}, u32[]{:S(2)}, u32[]{:S(2)}) collective-permute-start(f32[16,16,128]{2,1,0:T(8,128)S(1)} %get-tuple-element.68), channel_id=1, source_target_pairs={{0,224},{32,0},{64,32},{96,64},{128,96},{160,128},{192,160},{224,1... | collective-permute-start | bytes 393224 | tf_op jit(solution)/shard_map/ppermute | solution.py:20
  55.4 5.0 %collective-permute-start.10 = (f32[44,8,128]{2,1,0:T(8,128)S(1)}, f32[44,8,128]{2,1,0:T(8,128)S(1)}, u32[]{:S(2)}, u32[]{:S(2)}) collective-permute-start(f32[44,8,128]{2,1,0:T(8,128)S(1)} %get-tuple-element.69), channel_id=1, source_target_pairs={{0,1},{1,2},{2,3},{3,4},{4,5},{5,6},{6,7},{7,8},{8,9},{9,10},{10,1... | collective-permute-start | bytes 540680 | tf_op jit(solution)/shard_map/ppermute | solution.py:20
  55.7 4.7 %collective-permute-start.11 = (f32[44,8,128]{2,1,0:T(8,128)S(1)}, f32[44,8,128]{2,1,0:T(8,128)S(1)}, u32[]{:S(2)}, u32[]{:S(2)}) collective-permute-start(f32[44,8,128]{2,1,0:T(8,128)S(1)} %get-tuple-element.70), channel_id=1, source_target_pairs={{0,31},{1,0},{2,1},{3,2},{4,3},{5,4},{6,5},{7,6},{8,7},{9,8},{10,9... | collective-permute-start | bytes 540680 | tf_op jit(solution)/shard_map/ppermute | solution.py:20
  61.4 11.1 %collective-permute-start.12 = (f32[6,8,128]{2,1,0:T(8,128)S(1)}, f32[6,8,128]{2,1,0:T(8,128)S(1)}, u32[]{:S(2)}, u32[]{:S(2)}) collective-permute-start(f32[6,8,128]{2,1,0:T(8,128)S(1)} %get-tuple-element.71.own3), channel_id=1, source_target_pairs={{0,2},{1,3},{4,6},{5,7},{8,10},{9,11},{12,14},{13,15},{16,18},{17,... | collective-permute-start | bytes 73736 | tf_op jit(solution)/shard_map/ppermute | solution.py:32
  70.7 3.8 %collective-permute-start.13 = (f32[6,8,128]{2,1,0:T(8,128)S(1)}, f32[6,8,128]{2,1,0:T(8,128)S(1)}, u32[]{:S(2)}, u32[]{:S(2)}) collective-permute-start(f32[6,8,128]{2,1,0:T(8,128)S(1)} %get-tuple-element.71.own3), channel_id=1, source_target_pairs={{0,1},{2,4},{3,5},{6,8},{7,9},{10,12},{11,13},{14,16},{15,17},{18,... | collective-permute-start | bytes 73736 | tf_op jit(solution)/shard_map/ppermute | solution.py:32

commit v3 on v2

--- a/solution.py
+++ b/solution.py
@@ -172,11 +172,15 @@
         yield x, here, res
 
 
+def place(axis):
+    return lax.axis_index(axis)
+
+
 def gate(inside, value):
     return jnp.where(inside, value, F32(0.0))
 
 
-def k_pack_x0(idx, m, f, g, low, high, b0, c0, g0, mv, fv, sems):
+def k_load0(m, f, g, left, right, b0, c0, g0, mv, fv, sems):
     copies = [
         pltpu.make_async_copy(m, mv, sems.at[0]),
         pltpu.make_async_copy(f, fv, sems.at[1]),
@@ -187,17 +191,26 @@
     copies[0].wait()
     for x in range(8):
         b0[x] = inverse_density(mv[x])
-    for k in range(4):
-        low[k] = gate(idx[0] > 0, b0[k])
-        high[k] = gate(idx[0] < idx[2] - 1, b0[4 + k])
+        strip_tiles(left, x, gate(place("gy") > 0, b0[x, 0:4, :]))
+        strip_tiles(right, x, gate(place("gy") < lax.axis_size("gy") - 1, b0[x, 28:32, :]))
     copies[1].wait()
     for x in range(8):
         c0[x] = reaction_of(fv[x])
+        strip_tiles(left, 8 + x, c0[x, 0:4, :])
+        strip_tiles(right, 8 + x, c0[x, 28:32, :])
+    copies[2].wait()
+    for x in range(8):
+        strip_tiles(left, 16 + x, g0[x, 0:4, :])
+        strip_tiles(right, 16 + x, g0[x, 28:32, :])
+
+
+def k_edge0(b0, c0, g0, low, high):
+    for k in range(4):
+        low[k] = gate(place("gx") > 0, b0[k])
+        high[k] = gate(place("gx") < lax.axis_size("gx") - 1, b0[4 + k])
     for k in range(3):
         low[4 + k] = c0[k]
         high[4 + k] = c0[5 + k]
-    copies[2].wait()
-    for k in range(3):
         low[7 + k] = g0[k]
         high[7 + k] = g0[5 + k]
 
@@ -224,55 +237,53 @@
     out[t, 4:8, :] = value[:, 128:256]
 
 
-def k_pack_y0(idx, b0, c0, g0, below, above, low, high):
-    for out, at, inside in ((low, 0, idx[1] > 0), (high, 28, idx[1] < idx[3] - 1)):
-        cut = pl.ds(at, 4)
-        t = 0
-        for own, base, reach in ((b0, 0, 4), (c0, 4, 3), (g0, 7, 3)):
-            for x in range(-reach, 8 + reach):
-                if x < 0:
-                    val = below[base + x + reach, cut, :]
-                elif x < 8:
-                    val = own[x, cut, :]
-                else:
-                    val = above[base + x - 8, cut, :]
-                strip_tiles(out, t, gate(inside, val) if base == 0 else val)
-                t += 1
-
-
-def put_strips0(ext, first_row, count, buf, base, high):
+def k_corner0(left, right, low, high):
+    for side, strips in enumerate((left, right)):
+        for k in range(4):
+            low[10 * side + k] = gate(place("gx") > 0, strips[k])
+            high[10 * side + k] = gate(place("gx") < lax.axis_size("gx") - 1, strips[4 + k])
+        for k in range(3):
+            low[10 * side + 4 + k] = strips[8 + k]
+            high[10 * side + 4 + k] = strips[13 + k]
+            low[10 * side + 7 + k] = strips[16 + k]
+            high[10 * side + 7 + k] = strips[21 + k]
+
+
+def put_strip0(ext, row, tile, high):
     at = 40 if high else 4
-    for k in range(count):
-        ext[first_row + k, at : at + 4, 0:128] = buf[base + k, 0:4, :]
-        ext[first_row + k, at : at + 4, 128:256] = buf[base + k, 4:8, :]
-
-
-def assemble0(b0, c0, g0, below, above, left, right, be, ce, ge):
+    ext[row, at : at + 4, 0:128] = tile[0:4, :]
+    ext[row, at : at + 4, 128:256] = tile[4:8, :]
+
+
+def assemble0(b0, c0, g0, below, above, left, right, under, over, be, ce, ge):
     zeros = jnp.zeros((8, 256), F32)
-    for ext, own, base, reach, strips in (
-        (be, b0, 0, 4, 0), (ce, c0, 4, 3, 16), (ge, g0, 7, 3, 30)
+    for which, (ext, own, base, reach) in enumerate(
+        ((be, b0, 0, 4), (ce, c0, 4, 3), (ge, g0, 7, 3))
     ):
         for x in range(16):
             ext[x, 0:8, :] = zeros
             ext[x, 40:48, :] = zeros
         for x in range(-reach, 8 + reach):
             if x < 0:
-                val = below[base + x + reach]
+                k = base + x + reach
+                val, strips = below[k], (under[k], under[10 + k])
             elif x < 8:
-                val = own[x]
+                k = 8 * which + x
+                val, strips = own[x], (left[k], right[k])
             else:
-                val = above[base + x - 8]
+                k = base + x - 8
+                val, strips = above[k], (over[k], over[10 + k])
             ext[4 + x, 8:40, :] = val
-        put_strips0(ext, 4 - reach, 8 + 2 * reach, left, strips, False)
-        put_strips0(ext, 4 - reach, 8 + 2 * reach, right, strips, True)
+            put_strip0(ext, 4 + x, strips[0], False)
+            put_strip0(ext, 4 + x, strips[1], True)
 
 
 def k_descend0(
-    idx, b0, c0, g0, below, above, left, right, b1, c1,
+    b0, c0, g0, below, above, left, right, under, over, b1, c1,
     v0, g1, low, high,
     be, ce, ge, wx, wy, wz, wl, rd, va, vb, tmp,
 ):
-    assemble0(b0, c0, g0, below, above, left, right, be, ce, ge)
+    assemble0(b0, c0, g0, below, above, left, right, under, over, be, ce, ge)
     s = (wx, wy, wz, wl, rd, ce, ge)
     weights(be, s, va, 1.0, 1, 15, 7)
     sweep(va, vb, s, 2, 14, 6)
@@ -288,8 +299,8 @@
     t = fold_level0(tmp)
     for x in range(4):
         g1[x] = t[16 * x : 16 * x + 16]
-        low[x] = gate(idx[0] > 0, b1[x])
-        high[x] = gate(idx[0] < idx[2] - 1, b1[x])
+        low[x] = gate(place("gx") > 0, b1[x])
+        high[x] = gate(place("gx") < lax.axis_size("gx") - 1, b1[x])
     for k in range(3):
         low[4 + k] = c1[k]
         high[4 + k] = c1[1 + k]
@@ -297,8 +308,8 @@
         high[7 + k] = t[16 * k + 16 : 16 * k + 32]
 
 
-def k_pack_y1(idx, g1, b1, c1, below, above, low, high):
-    for out, at, inside in ((low, 0, idx[1] > 0), (high, 12, idx[1] < idx[3] - 1)):
+def k_pack_y1(g1, b1, c1, v0, below, above, low, high, vlow, vhigh):
+    for out, at, inside in ((low, 0, place("gy") > 0), (high, 12, place("gy") < lax.axis_size("gy") - 1)):
         cut = pl.ds(at, 4)
         t = 0
         for own, base, reach in ((b1, 0, 4), (c1, 4, 3), (g1, 7, 3)):
@@ -312,10 +323,15 @@
                 half = 4 * (t % 2)
                 out[t // 2, half : half + 4, :] = gate(inside, val) if base == 0 else val
                 t += 1
+        for x in range(8):
+            strip_tiles(out, 16 + x, v0[x, pl.ds(0 if at == 0 else 28, 4), :])
+    for k in range(3):
+        vlow[k] = v0[k]
+        vhigh[k] = v0[5 + k]
 
 
 def k_descend1(
-    idx, g1, b1, c1, bc2, v0, below, above, left, right,
+    g1, b1, c1, bc2, below, above, left, right,
     v1, pay, low, high, be, ce, ge,
     wx, wy, wz, wl, rd, va, vb, tmp,
 ):
@@ -357,44 +373,33 @@
         pay[k, 2] = bc2[1]
 
     for out, first in ((low, 0), (high, 5)):
+        for k in range(4):
+            for q in range(2):
+                out[2 * k + q] = va[4 + k, 8 + 8 * q : 16 + 8 * q, :]
         for k in range(3):
-            for q in range(2):
-                for h in range(2):
-                    out[4 * k + 2 * q + h] = v0[
-                        first + k, 16 * q : 16 * q + 16, 128 * h : 128 * h + 128
-                    ]
-        for k in range(4):
-            out[12 + k] = va[4 + k, 8:24, :]
-
-
-def k_pack_y2(idx, v0, v1, below, above, gathered, low, high):
+            out[8 + k] = left[16 + first + k]
+            out[11 + k] = right[16 + first + k]
+
+
+def k_pack_y2(v1, below, above, gathered, low, high):
     for out, is_high, inside in (
-        (low, False, idx[1] > 0), (high, True, idx[1] < idx[3] - 1)
+        (low, False, place("gy") > 0), (high, True, place("gy") < lax.axis_size("gy") - 1)
     ):
         for k in range(3):
             for i in range(8):
                 val = gathered[i, k]
                 out[8 * k + i] = gate(inside, val) if k == 1 else val
-        cut = pl.ds(28 if is_high else 0, 4)
-        part = pl.ds(12 if is_high else 0, 4)
         q = 1 if is_high else 0
-        for t, x in enumerate(range(-3, 11)):
-            if 0 <= x < 8:
-                strip_tiles(out, 24 + t, v0[x, cut, :])
-            else:
-                src = below if x < 0 else above
-                k = 4 * (x + 3 if x < 0 else x - 8) + 2 * q
-                for h in range(2):
-                    out[24 + t, 4 * h : 4 * h + 4, :] = src[k + h, part, :]
+        cut = pl.ds(4 * q, 4)
         for t, x in enumerate(range(-4, 8)):
             if x < 0:
-                val = below[12 + x + 4, part, :]
+                val = below[2 * (x + 4) + q, cut, :]
             elif x < 4:
-                val = v1[x, part, :]
+                val = v1[x, pl.ds(12 * q, 4), :]
             else:
-                val = above[12 + x - 4, part, :]
+                val = above[2 * (x - 4) + q, cut, :]
             half = 4 * (t % 2)
-            out[38 + t // 2, half : half + 4, :] = val
+            out[24 + t // 2, half : half + 4, :] = val
 
 
 def upper(shape):
@@ -529,12 +534,12 @@
 
 
 def k_prepare(
-    b0, c0, g0, below0, above0, left0, right0, be1, ce1, ge1,
-    v0, v1, below, above, left, right,
+    b0, c0, g0, below0, above0, left0, right0, under0, over0, be1, ce1, ge1,
+    v0, below, above, left, right, v1, below1, above1, left1, right1,
     p0, ce, ge, wx, wy, wz, wl, rd, p1, wx1, wy1, wz1, wl1, rd1,
     be, va, va1,
 ):
-    assemble0(b0, c0, g0, below0, above0, left0, right0, be, ce, ge)
+    assemble0(b0, c0, g0, below0, above0, left0, right0, under0, over0, be, ce, ge)
     weights(be, (wx, wy, wz, wl, rd, ce, ge), va, 1.0, 2, 14, 6)
     weights(be1, (wx1, wy1, wz1, wl1, rd1, ce1, ge1), va1, 0.25, 1, 11, 10)
     narrow = jnp.zeros((8, 128), F32)
@@ -542,42 +547,41 @@
     for t, x in enumerate(range(-4, 8)):
         p1[t, 0:8, :] = narrow
         p1[t, 24:32, :] = narrow
-        if x < 0:
-            p1[t, 8:24, :] = below[12 + x + 4]
-        elif x < 4:
+        if 0 <= x < 4:
             p1[t, 8:24, :] = v1[x]
         else:
-            p1[t, 8:24, :] = above[12 + x - 4]
+            for q in range(2):
+                src, k = (below1, x + 4) if x < 0 else (above1, x - 4)
+                p1[t, 8 + 8 * q : 16 + 8 * q, :] = src[2 * k + q]
         half = 4 * (t % 2)
-        p1[t, 4:8, :] = left[38 + t // 2, half : half + 4, :]
-        p1[t, 24:28, :] = right[38 + t // 2, half : half + 4, :]
+        p1[t, 4:8, :] = left1[24 + t // 2, half : half + 4, :]
+        p1[t, 24:28, :] = right1[24 + t // 2, half : half + 4, :]
     for x in range(-3, 11):
         p0[4 + x, 0:8, :] = wide
         p0[4 + x, 40:48, :] = wide
-        if 0 <= x < 8:
-            p0[4 + x, 8:40, :] = v0[x]
+        if x < 0:
+            k = x + 3
+            val, strips = below[k], (below1[8 + k], below1[11 + k])
+        elif x < 8:
+            val, strips = v0[x], (left[16 + x], right[16 + x])
         else:
-            src = below if x < 0 else above
-            k = 4 * (x + 3 if x < 0 else x - 8)
-            for q in range(2):
-                for h in range(2):
-                    p0[4 + x, 8 + 16 * q : 24 + 16 * q, 128 * h : 128 * h + 128] = (
-                        src[k + 2 * q + h]
-                    )
-    put_strips0(p0, 1, 14, left, 24, False)
-    put_strips0(p0, 1, 14, right, 24, True)
+            k = x - 8
+            val, strips = above[k], (above1[8 + k], above1[11 + k])
+        p0[4 + x, 8:40, :] = val
+        put_strip0(p0, 4 + x, strips[0], False)
+        put_strip0(p0, 4 + x, strips[1], True)
 
 
 def k_ascend(
-    idx, own3, r0, r1, v2, wx2, wy2, wz2, rd2, ce2, ge2,
+    own3, r0, r1, v2, wx2, wy2, wz2, rd2, ce2, ge2,
     p0, ce0, ge0, wx0, wy0, wz0, wl0, rd0,
     p1, ce1, ge1, wx1, wy1, wz1, wl1, rd1,
     pressure, residual,
     all3, m2, p2, p1a, p1b, p0a, p0b, f1, f0,
 ):
-    ix = idx[0]
-    iy = idx[1]
-    count = idx[3]
+    ix = place("gx")
+    iy = place("gy")
+    count = lax.axis_size("gy")
     even_chip = lax.rem(iy // 2, 2) == 0
     zero = F32(0.0)
 
@@ -620,7 +624,7 @@
     parts = []
     for q in range(3):
         at = ix + (q - 1)
-        inside = jnp.logical_and(at >= 0, at < idx[2])
+        inside = jnp.logical_and(at >= 0, at < lax.axis_size("gx"))
         parts.append(jnp.where(inside, p2[jnp.clip(at, 0, 7), 4:20, :], zero))
     row = iota((128, 256), 0)
     lane = iota((128, 256), 1)
@@ -658,9 +662,8 @@
 
 def call(kernel, name, outs, scratch, limit, *args, anywhere=()):
     vmem = pl.BlockSpec(memory_space=pltpu.VMEM)
-    smem = pl.BlockSpec(memory_space=pltpu.SMEM)
     hbm = pl.BlockSpec(memory_space=pltpu.HBM)
-    specs = [smem if a.ndim == 1 else vmem for a in args]
+    specs = [vmem for _ in args]
     for k in anywhere:
         specs[k] = hbm
     return pl.pallas_call(
@@ -681,66 +684,63 @@
 
 
 def per_device(source, material, flags):
-    idx = jnp.stack(
-        [
-            lax.axis_index("gx").astype(jnp.int32),
-            lax.axis_index("gy").astype(jnp.int32),
-            jnp.int32(lax.axis_size("gx")),
-            jnp.int32(lax.axis_size("gy")),
-        ]
-    )
-
-    low, high, b0, c0, g0 = call(
-        k_pack_x0, "pack_x0", [(10, 32, 256)] * 2 + [B0] * 3,
+    source, material, flags = (
+        pltpu.with_memory_space_constraint(a, pltpu.HBM) for a in (source, material, flags)
+    )
+    left, right, b0, c0, g0 = call(
+        k_load0, "load0", [(24, 8, 128)] * 2 + [B0] * 3,
         [pltpu.VMEM(B0, jnp.int32), pltpu.VMEM(B0, jnp.int32), pltpu.SemaphoreType.DMA((3,))],
-        4, idx, material, flags, source, anywhere=(1, 2, 3),
-    )
+        4, material, flags, source, anywhere=(0, 1, 2),
+    )
+    left0, right0 = exchange(left, right, "gy")
+    low, high = call(k_edge0, "edge0", [(10, 32, 256)] * 2, [], 4, b0, c0, g0)
     below0, above0 = exchange(low, high, "gx")
+    low, high = call(k_corner0, "corner0", [(20, 8, 128)] * 2, [], 4, left0, right0)
+    under0, over0 = exchange(low, high, "gx")
     b1, c1, bc2 = call(
         k_coefs, "coefs", [(4, 16, 128), (4, 16, 128), (2, 8, 128)],
         [(4, 2, 32, 128), (2, 16, 128)], 4, b0, c0,
     )
-    low, high = call(
-        k_pack_y0, "pack_y0", [(44, 8, 128)] * 2, [], 4, idx, b0, c0, g0, below0, above0
-    )
-    left0, right0 = exchange(low, high, "gy")
-    blocks0 = (b0, c0, g0, below0, above0, left0, right0)
+    blocks0 = (b0, c0, g0, below0, above0, left0, right0, under0, over0)
     v0, g1, low, high = call(
         k_descend0, "descend0",
         [B0, (4, 16, 128), (10, 16, 128), (10, 16, 128)],
         [E0] * 10 + [(4, 2, 32, 128)], 12,
-        idx, *blocks0, b1, c1,
+        *blocks0, b1, c1,
     )
     below, above = exchange(low, high, "gx")
-    low, high = call(
-        k_pack_y1, "pack_y1", [(16, 8, 128)] * 2, [], 4, idx, g1, b1, c1, below, above
+    low, high, vlow, vhigh = call(
+        k_pack_y1, "pack_y1", [(24, 8, 128)] * 2 + [(3, 32, 256)] * 2, [], 4,
+        g1, b1, c1, v0, below, above,
     )
     left, right = exchange(low, high, "gy")
+    vbelow, vabove = exchange(vlow, vhigh, "gx")
     v1, pay, low, high, be1, ce1, ge1 = call(
         k_descend1, "descend1",
-        [(4, 16, 128), (8, 3, 8, 128), (16, 16, 128), (16, 16, 128)] + [E1] * 3,
+        [(4, 16, 128), (8, 3, 8, 128), (14, 8, 128), (14, 8, 128)] + [E1] * 3,
         [E1] * 7 + [(2, 16, 128)], 4,
-        idx, g1, b1, c1, bc2, v0, below, above, left, right,
+        g1, b1, c1, bc2, below, above, left, right,
     )
     gathered = lax.all_to_all(pay, "gx", 0, 0)
-    below, above = exchange(low, high, "gx")
+    below1, above1 = exchange(low, high, "gx")
     low, high = call(
-        k_pack_y2, "pack_y2", [(44, 8, 128)] * 2, [], 4, idx, v0, v1, below, above, gathered
-    )
-    left, right = exchange(low, high, "gy")
+        k_pack_y2, "pack_y2", [(30, 8, 128)] * 2, [], 4, v1, below1, above1, gathered
+    )
+    left1, right1 = exchange(low, high, "gy")
     v2, own3, *s2 = call(
         k_descend2, "descend2", [E2, (6, 8, 128)] + [E2] * 6, [E2, (384, 128)], 4,
-        gathered, left, right,
+        gathered, left1, right1,
     )
     r0, r1 = swap_chips(own3, "gy", 0), swap_chips(own3, "gy", 1)
     p0, ce0, ge0, wx0, wy0, wz0, wl0, rd0, p1, *w1 = call(
         k_prepare, "prepare", [E0] * 8 + [E1] * 6, [E0, E0, E1], 8,
-        *blocks0, be1, ce1, ge1, v0, v1, below, above, left, right,
+        *blocks0, be1, ce1, ge1, v0, vbelow, vabove, left, right,
+        v1, below1, above1, left1, right1,
     )
     pressure, residual = call(
         k_ascend, "ascend", [B0] * 2,
         [(18, 8, 128), (128, 128), E2, E1, E1, E0, E0, (6, 32, 128), (8, 2, 48, 128)], 8,
-        idx, own3, r0, r1, v2, *s2,
+        own3, r0, r1, v2, *s2,
         p0, ce0, ge0, wx0, wy0, wz0, wl0, rd0, p1, ce1, ge1, *w1,
     )
     return pressure, residual

time: 79.3 us -> 71.5 us (0.902)
  waiting for transfers between devices: 26.9 us -> 18.4 us
  starting transfers between devices: 33.8 us -> 40.3 us
  local copies, waits for them, and re-layouts: 2.85 us -> 0 us
  Pallas kernels: 14.7 us -> 11.9 us
    ppermute x12 -> x16, waiting for transfers between devices: 24 us -> 13.9 us  [shift(): lax.ppermute(block, axis, [(i, (i + step) % count) for i in range(count)])]
    ppermute x12 -> x16, starting transfers between devices: 18.1 us -> 25.1 us  [shift(): lax.ppermute(block, axis, [(i, (i + step) % count) for i in range(count)])]
    unnamed x6 -> x0, local copies, waits for them, and re-layouts: 2.85 us -> none
    pallas_call x10 -> x11, Pallas kernels: 14.7 us -> 11.9 us  [call(): pl.pallas_call(kernel, name=name, out_shape=[jax.ShapeDtypeStruct(s, F32)...]
    all_to_all x1, waiting for transfers between devices: 0.32 us -> 1.86 us  [per_device(): gathered = lax.all_to_all(pay, 'gx', 0, 0)]
  transfers between devices with their start and end apart: 15 -> 19, of which waited for: 9 -> 8; matrix products, arithmetic and copies ran while one was open for 0% -> 0% of each run, Pallas kernels for 2% -> 4%
where the time goes in v3:
time: 71.5 us; the launch traced here: 71.3 us
  starting transfers between devices  40.3 us (56%)
  waiting for transfers between devices  18.4 us (26%)
  Pallas kernels  11.9 us (17%)
  between operations  0.72 us (1%)
    ppermute x16, starting transfers between devices, shift(): lax.ppermute(block, axis, [(i, (i + step) % count) for i in range(count)])  25.1 us
    ppermute x16, waiting for transfers between devices, shift(): lax.ppermute(block, axis, [(i, (i + step) % count) for i in range(count)])  13.9 us
    pallas_call x11, Pallas kernels, call(): pl.pallas_call(kernel, name=name, out_shape=[jax.ShapeDtypeStruct(s, F32)...  11.9 us
    ppermute x2, starting transfers between devices, swap_chips(): return lax.ppermute(block, axis, pairs + [(b, a) for a, b in pairs])  9.07 us
    all_to_all x1, starting transfers between devices, per_device(): gathered = lax.all_to_all(pay, 'gx', 0, 0)  6.14 us
    ppermute x2, waiting for transfers between devices, swap_chips(): return lax.ppermute(block, axis, pairs + [(b, a) for a, b in pairs])  2.6 us
    all_to_all x1, waiting for transfers between devices, per_device(): gathered = lax.all_to_all(pay, 'gx', 0, 0)  1.86 us
  transfers between devices with their start and end apart: 19, of which 8 were waited for; matrix products, arithmetic and copies ran while one was open for 0% of the time, Pallas kernels for 4%

profile of v3, /device:TPU:2, one launch (start us, length us, event | category | flops | bytes accessed | tf_op | source)
XLA Modules:
  0.0 71.3 jit_solution(12503434006015284754)
XLA Ops:
  0.6 1.1 %load0.1 = (f32[24,8,128]{2,1,0:T(8,128)S(1)}, f32[24,8,128]{2,1,0:T(8,128)S(1)}, f32[8,32,256]{2,1,0:T(8,128)S(1)}, f32[8,32,256]{2,1,0:T(8,128)S(1)}, f32[8,32,256]{2,1,0:T(8,128)S(1)}) custom-call(s32[8,32,256]{2,1,0:T(8,128)} %m.1, s32[8,32,256]{2,1,0:T(8,128)} %f.1, f32[8,32,256]{2,1,0:T(8,128)} %g.1), custom_call_target="tpu_custom_call" | custom-call | tf_op jit(solution)/shard_map/load0/pallas_call | solution.py:669
  1.9 2.0 %collective-permute-start = (f32[10,32,256]{2,1,0:T(8,128)S(1)}, f32[10,32,256]{2,1,0:T(8,128)S(1)}, u32[]{:S(2)}, u32[]{:S(2)}) collective-permute-start(f32[10,32,256]{2,1,0:T(8,128)S(1)} %get-tuple-element.56), channel_id=1, source_target_pairs={{0,32},{32,64},{64,96},{96,128},{128,160},{160,192},{192,224},{224... | collective-permute-start | bytes 983048 | tf_op jit(solution)/shard_map/ppermute | solution.py:20
  3.8 4.0 %collective-permute-start.1 = (f32[10,32,256]{2,1,0:T(8,128)S(1)}, f32[10,32,256]{2,1,0:T(8,128)S(1)}, u32[]{:S(2)}, u32[]{:S(2)}) collective-permute-start(f32[10,32,256]{2,1,0:T(8,128)S(1)} %get-tuple-element.57), channel_id=1, source_target_pairs={{0,224},{32,0},{64,32},{96,64},{128,96},{160,128},{192,160},{224,1... | collective-permute-start | bytes 983048 | tf_op jit(solution)/shard_map/ppermute | solution.py:20
  7.9 1.7 %collective-permute-start.3 = (f32[24,8,128]{2,1,0:T(8,128)S(1)}, f32[24,8,128]{2,1,0:T(8,128)S(1)}, u32[]{:S(2)}, u32[]{:S(2)}) collective-permute-start(f32[24,8,128]{2,1,0:T(8,128)S(1)} %get-tuple-element.59), channel_id=1, source_target_pairs={{0,31},{1,0},{2,1},{3,2},{4,3},{5,4},{6,5},{7,6},{8,7},{9,8},{10,9... | collective-permute-start | bytes 294920 | tf_op jit(solution)/shard_map/ppermute | solution.py:20
  9.6 2.3 %collective-permute-done.2.left.left0 = f32[24,8,128]{2,1,0:T(8,128)S(1)} collective-permute-done((f32[24,8,128]{2,1,0:T(8,128)S(1)}, f32[24,8,128]{2,1,0:T(8,128)S(1)}, u32[]{:S(2)}, u32[]{:S(2)}) %collective-permute-start.2) | collective-permute-done | bytes 98336 | tf_op jit(solution)/shard_map/ppermute | solution.py:20
  12.0 3.2 %collective-permute-start.5 = (f32[20,8,128]{2,1,0:T(8,128)S(1)}, f32[20,8,128]{2,1,0:T(8,128)S(1)}, u32[]{:S(2)}, u32[]{:S(2)}) collective-permute-start(f32[20,8,128]{2,1,0:T(8,128)S(1)} %get-tuple-element.61), channel_id=1, source_target_pairs={{0,224},{32,0},{64,32},{96,64},{128,96},{160,128},{192,160},{224,1... | collective-permute-start | bytes 245768 | tf_op jit(solution)/shard_map/ppermute | solution.py:20
  15.8 1.9 %collective-permute-done.4.under.under0 = f32[20,8,128]{2,1,0:T(8,128)S(1)} collective-permute-done((f32[20,8,128]{2,1,0:T(8,128)S(1)}, f32[20,8,128]{2,1,0:T(8,128)S(1)}, u32[]{:S(2)}, u32[]{:S(2)}) %collective-permute-start.4) | collective-permute-done | bytes 81952 | tf_op jit(solution)/shard_map/ppermute | solution.py:20
  17.7 2.6 %descend0.1 = (f32[8,32,256]{2,1,0:T(8,128)S(1)}, f32[4,16,128]{2,1,0:T(8,128)S(1)}, f32[10,16,128]{2,1,0:T(8,128)S(1)}, f32[10,16,128]{2,1,0:T(8,128)S(1)}) custom-call(f32[8,32,256]{2,1,0:T(8,128)S(1)} %get-tuple-element.53.b0, f32[8,32,256]{2,1,0:T(8,128)S(1)} %get-tuple-element.54.c0, f32[8,32,256]{2,1,0:T(8,128)S(1)} %get-tuple-element.55.g0, ...), custom_call_target="tpu_custom_call" | custom-call | tf_op jit(solution)/shard_map/descend0/pallas_call | solution.py:669
  20.4 3.6 %collective-permute-start.7 = (f32[10,16,128]{2,1,0:T(8,128)S(1)}, f32[10,16,128]{2,1,0:T(8,128)S(1)}, u32[]{:S(2)}, u32[]{:S(2)}) collective-permute-start(f32[10,16,128]{2,1,0:T(8,128)S(1)} %get-tuple-element.67), channel_id=1, source_target_pairs={{0,224},{32,0},{64,32},{96,64},{128,96},{160,128},{192,160},{224,1... | collective-permute-start | bytes 245768 | tf_op jit(solution)/shard_map/ppermute | solution.py:20
  24.0 2.9 %collective-permute-done.6.below = f32[10,16,128]{2,1,0:T(8,128)S(1)} collective-permute-done((f32[10,16,128]{2,1,0:T(8,128)S(1)}, f32[10,16,128]{2,1,0:T(8,128)S(1)}, u32[]{:S(2)}, u32[]{:S(2)}) %collective-permute-start.6) | collective-permute-done | bytes 81952 | tf_op jit(solution)/shard_map/ppermute | solution.py:20
  27.1 1.7 %collective-permute-start.9 = (f32[24,8,128]{2,1,0:T(8,128)S(1)}, f32[24,8,128]{2,1,0:T(8,128)S(1)}, u32[]{:S(2)}, u32[]{:S(2)}) collective-permute-start(f32[24,8,128]{2,1,0:T(8,128)S(1)} %get-tuple-element.70), channel_id=1, source_target_pairs={{0,31},{1,0},{2,1},{3,2},{4,3},{5,4},{6,5},{7,6},{8,7},{9,8},{10,9... | collective-permute-start | bytes 294920 | tf_op jit(solution)/shard_map/ppermute | solution.py:20
  28.8 2.3 %collective-permute-done.8.left = f32[24,8,128]{2,1,0:T(8,128)S(1)} collective-permute-done((f32[24,8,128]{2,1,0:T(8,128)S(1)}, f32[24,8,128]{2,1,0:T(8,128)S(1)}, u32[]{:S(2)}, u32[]{:S(2)}) %collective-permute-start.8) | collective-permute-done | bytes 98336 | tf_op jit(solution)/shard_map/ppermute | solution.py:20
  31.1 1.3 %descend1.1 = (f32[4,16,128]{2,1,0:T(8,128)S(1)}, f32[8,3,8,128]{3,2,1,0:T(8,128)}, f32[14,8,128]{2,1,0:T(8,128)S(1)}, f32[14,8,128]{2,1,0:T(8,128)S(1)}, f32[12...) custom-call(f32[4,16,128]{2,1,0:T(8,128)S(1)} %get-tuple-element.64.g1, ...), custom_call_target="tpu_custom_call" | custom-call | tf_op jit(solution)/shard_map/descend1/pallas_call | solution.py:669
  32.4 6.1 %all-to-all-start = ((f32[8,3,8,128]{3,2,1,0:T(8,128)}), f32[8,3,8,128]{3,2,1,0:T(8,128)S(1)}, u32[]{:S(2)}, u32[]{:S(2)}) async-start(f32[8,3,8,128]{3,2,1,0:T(8,128)} %get-tuple-element.71), calls=%async_computation | async-start | bytes 196608 | tf_op jit(solution)/shard_map/all_to_all | solution.py:724
  38.5 2.0 %collective-permute-start.10 = (f32[14,8,128]{2,1,0:T(8,128)S(1)}, f32[14,8,128]{2,1,0:T(8,128)S(1)}, u32[]{:S(2)}, u32[]{:S(2)}) collective-permute-start(f32[14,8,128]{2,1,0:T(8,128)S(1)} %get-tuple-element.73), channel_id=1, source_target_pairs={{0,32},{32,64},{64,96},{96,128},{128,160},{160,192},{192,224},{224... | collective-permute-start | bytes 172040 | tf_op jit(solution)/shard_map/ppermute | solution.py:20
  40.5 1.2 %collective-permute-start.11 = (f32[14,8,128]{2,1,0:T(8,128)S(1)}, f32[14,8,128]{2,1,0:T(8,128)S(1)}, u32[]{:S(2)}, u32[]{:S(2)}) collective-permute-start(f32[14,8,128]{2,1,0:T(8,128)S(1)} %get-tuple-element.74), channel_id=1, source_target_pairs={{0,224},{32,0},{64,32},{96,64},{128,96},{160,128},{192,160},{224,1... | collective-permute-start | bytes 172040 | tf_op jit(solution)/shard_map/ppermute | solution.py:20
  41.8 4.5 %collective-permute-done.10.below.below1 = f32[14,8,128]{2,1,0:T(8,128)S(1)} collective-permute-done((f32[14,8,128]{2,1,0:T(8,128)S(1)}, f32[14,8,128]{2,1,0:T(8,128)S(1)}, u32[]{:S(2)}, u32[]{:S(2)}) %collective-permute-start.10) | collective-permute-done | bytes 57376 | tf_op jit(solution)/shard_map/ppermute | solution.py:20
  46.3 1.9 %all-to-all-done.gathered = f32[8,3,8,128]{3,2,1,0:T(8,128)S(1)} async-done(((f32[8,3,8,128]{3,2,1,0:T(8,128)}), f32[8,3,8,128]{3,2,1,0:T(8,128)S(1)}, u32[]{:S(2)}, u32[]{:S(2)}) %all-to-all-start) | async-done | bytes 98336 | tf_op jit(solution)/shard_map/all_to_all | solution.py:724
  48.5 1.6 %collective-permute-start.13 = (f32[30,8,128]{2,1,0:T(8,128)S(1)}, f32[30,8,128]{2,1,0:T(8,128)S(1)}, u32[]{:S(2)}, u32[]{:S(2)}) collective-permute-start(f32[30,8,128]{2,1,0:T(8,128)S(1)} %get-tuple-element.76), channel_id=1, source_target_pairs={{0,31},{1,0},{2,1},{3,2},{4,3},{5,4},{6,5},{7,6},{8,7},{9,8},{10,9... | collective-permute-start | bytes 368648 | tf_op jit(solution)/shard_map/ppermute | solution.py:20
  50.4 3.0 %collective-permute-start.17 = (f32[3,32,256]{2,1,0:T(8,128)S(1)}, f32[3,32,256]{2,1,0:T(8,128)S(1)}, u32[]{:S(2)}, u32[]{:S(2)}) collective-permute-start(f32[3,32,256]{2,1,0:T(8,128)S(1)} %get-tuple-element.89), channel_id=1, source_target_pairs={{0,224},{32,0},{64,32},{96,64},{128,96},{160,128},{192,160},{224,1... | collective-permute-start | bytes 294920 | tf_op jit(solution)/shard_map/ppermute | solution.py:20
  54.4 9.1 %collective-permute-start.14 = (f32[6,8,128]{2,1,0:T(8,128)S(1)}, f32[6,8,128]{2,1,0:T(8,128)S(1)}, u32[]{:S(2)}, u32[]{:S(2)}) collective-permute-start(f32[6,8,128]{2,1,0:T(8,128)S(1)} %get-tuple-element.77.own3), channel_id=1, source_target_pairs={{0,2},{1,3},{4,6},{5,7},{8,10},{9,11},{12,14},{13,15},{16,18},{17,... | collective-permute-start | bytes 73736 | tf_op jit(solution)/shard_map/ppermute | solution.py:32
  63.5 1.2 %prepare.1 = (f32[16,48,256]{2,1,0:T(8,128)S(1)}, f32[16,48,256]{2,1,0:T(8,128)S(1)}, f32[16,48,256]{2,1,0:T(8,128)S(1)}, f32[16,48,256]{2,1,0:T(8,128)S(1)}, f3...) custom-call(f32[8,32,256]{2,1,0:T(8,128)S(1)} %get-tuple-element.53., ...), custom_call_target="tpu_custom_call" | custom-call | tf_op jit(solution)/shard_map/prepare/pallas_call | solution.py:669
  65.3 2.0 %collective-permute-done.15.r1 = f32[6,8,128]{2,1,0:T(8,128)S(1)} collective-permute-done((f32[6,8,128]{2,1,0:T(8,128)S(1)}, f32[6,8,128]{2,1,0:T(8,128)S(1)}, u32[]{:S(2)}, u32[]{:S(2)}) %collective-permute-start.15) | collective-permute-done | bytes 24608 | tf_op jit(solution)/shard_map/ppermute | solution.py:32
  67.3 4.0 %ascend.1 = (f32[8,32,256]{2,1,0:T(8,128)}, f32[8,32,256]{2,1,0:T(8,128)}) custom-call(f32[6,8,128]{2,1,0:T(8,128)S(1)} %get-tuple-element.77.own3, f32[6,8,128]{2,1,0:T(8,128)S(1)} %collective-permute-done.14.r0, f32[6,8,128]{2,1,0:T(8,128)S(1)} %collective-permute-done.15.r1, f32[8,24,128]{2,1,0:T(8,128)S(1)} %get-tuple-element.78.v2, ...), custom_call_target="tpu_custom_call" | custom-call | tf_op jit(solution)/shard_map/ascend/pallas_call | solution.py:669
  (25 shorter events, 3.2 us)
Async XLA Ops:
  1.9 15.8 %collective-permute-start = (f32[10,32,256]{2,1,0:T(8,128)S(1)}, f32[10,32,256]{2,1,0:T(8,128)S(1)}, u32[]{:S(2)}, u32[]{:S(2)}) collective-permute-start(f32[10,32,256]{2,1,0:T(8,128)S(1)} %get-tuple-element.56), channel_id=1, source_target_pairs={{0,32},{32,64},{64,96},{96,128},{128,160},{160,192},{192,224},{224... | collective-permute-start | bytes 983048 | tf_op jit(solution)/shard_map/ppermute | solution.py:20
  3.8 13.8 %collective-permute-start.1 = (f32[10,32,256]{2,1,0:T(8,128)S(1)}, f32[10,32,256]{2,1,0:T(8,128)S(1)}, u32[]{:S(2)}, u32[]{:S(2)}) collective-permute-start(f32[10,32,256]{2,1,0:T(8,128)S(1)} %get-tuple-element.57), channel_id=1, source_target_pairs={{0,224},{32,0},{64,32},{96,64},{128,96},{160,128},{192,160},{224,1... | collective-permute-start | bytes 983048 | tf_op jit(solution)/shard_map/ppermute | solution.py:20
  7.9 4.0 %collective-permute-start.2 = (f32[24,8,128]{2,1,0:T(8,128)S(1)}, f32[24,8,128]{2,1,0:T(8,128)S(1)}, u32[]{:S(2)}, u32[]{:S(2)}) collective-permute-start(f32[24,8,128]{2,1,0:T(8,128)S(1)} %get-tuple-element.58), channel_id=1, source_target_pairs={{0,1},{1,2},{2,3},{3,4},{4,5},{5,6},{6,7},{7,8},{8,9},{9,10},{10,1... | collective-permute-start | bytes 294920 | tf_op jit(solution)/shard_map/ppermute | solution.py:20
  7.9 4.0 %collective-permute-start.3 = (f32[24,8,128]{2,1,0:T(8,128)S(1)}, f32[24,8,128]{2,1,0:T(8,128)S(1)}, u32[]{:S(2)}, u32[]{:S(2)}) collective-permute-start(f32[24,8,128]{2,1,0:T(8,128)S(1)} %get-tuple-element.59), channel_id=1, source_target_pairs={{0,31},{1,0},{2,1},{3,2},{4,3},{5,4},{6,5},{7,6},{8,7},{9,8},{10,9... | collective-permute-start | bytes 294920 | tf_op jit(solution)/shard_map/ppermute | solution.py:20
  11.9 5.7 %collective-permute-start.4 = (f32[20,8,128]{2,1,0:T(8,128)S(1)}, f32[20,8,128]{2,1,0:T(8,128)S(1)}, u32[]{:S(2)}, u32[]{:S(2)}) collective-permute-start(f32[20,8,128]{2,1,0:T(8,128)S(1)} %get-tuple-element.60), channel_id=1, source_target_pairs={{0,32},{32,64},{64,96},{96,128},{128,160},{160,192},{192,224},{224... | collective-permute-start | bytes 245768 | tf_op jit(solution)/shard_map/ppermute | solution.py:20
  12.0 5.6 %collective-permute-start.5 = (f32[20,8,128]{2,1,0:T(8,128)S(1)}, f32[20,8,128]{2,1,0:T(8,128)S(1)}, u32[]{:S(2)}, u32[]{:S(2)}) collective-permute-start(f32[20,8,128]{2,1,0:T(8,128)S(1)} %get-tuple-element.61), channel_id=1, source_target_pairs={{0,224},{32,0},{64,32},{96,64},{128,96},{160,128},{192,160},{224,1... | collective-permute-start | bytes 245768 | tf_op jit(solution)/shard_map/ppermute | solution.py:20
  20.3 6.6 %collective-permute-start.6 = (f32[10,16,128]{2,1,0:T(8,128)S(1)}, f32[10,16,128]{2,1,0:T(8,128)S(1)}, u32[]{:S(2)}, u32[]{:S(2)}) collective-permute-start(f32[10,16,128]{2,1,0:T(8,128)S(1)} %get-tuple-element.66), channel_id=1, source_target_pairs={{0,32},{32,64},{64,96},{96,128},{128,160},{160,192},{192,224},{224... | collective-permute-start | bytes 245768 | tf_op jit(solution)/shard_map/ppermute | solution.py:20
  20.4 6.5 %collective-permute-start.7 = (f32[10,16,128]{2,1,0:T(8,128)S(1)}, f32[10,16,128]{2,1,0:T(8,128)S(1)}, u32[]{:S(2)}, u32[]{:S(2)}) collective-permute-start(f32[10,16,128]{2,1,0:T(8,128)S(1)} %get-tuple-element.67), channel_id=1, source_target_pairs={{0,224},{32,0},{64,32},{96,64},{128,96},{160,128},{192,160},{224,1... | collective-permute-start | bytes 245768 | tf_op jit(solution)/shard_map/ppermute | solution.py:20
  27.0 4.1 %collective-permute-start.8 = (f32[24,8,128]{2,1,0:T(8,128)S(1)}, f32[24,8,128]{2,1,0:T(8,128)S(1)}, u32[]{:S(2)}, u32[]{:S(2)}) collective-permute-start(f32[24,8,128]{2,1,0:T(8,128)S(1)} %get-tuple-element.69), channel_id=1, source_target_pairs={{0,1},{1,2},{2,3},{3,4},{4,5},{5,6},{6,7},{7,8},{8,9},{9,10},{10,1... | collective-permute-start | bytes 294920 | tf_op jit(solution)/shard_map/ppermute | solution.py:20
  27.1 4.0 %collective-permute-start.9 = (f32[24,8,128]{2,1,0:T(8,128)S(1)}, f32[24,8,128]{2,1,0:T(8,128)S(1)}, u32[]{:S(2)}, u32[]{:S(2)}) collective-permute-start(f32[24,8,128]{2,1,0:T(8,128)S(1)} %get-tuple-element.70), channel_id=1, source_target_pairs={{0,31},{1,0},{2,1},{3,2},{4,3},{5,4},{6,5},{7,6},{8,7},{9,8},{10,9... | collective-permute-start | bytes 294920 | tf_op jit(solution)/shard_map/ppermute | solution.py:20
  32.4 15.8 %all-to-all-start = ((f32[8,3,8,128]{3,2,1,0:T(8,128)}), f32[8,3,8,128]{3,2,1,0:T(8,128)S(1)}, u32[]{:S(2)}, u32[]{:S(2)}) async-start(f32[8,3,8,128]{3,2,1,0:T(8,128)} %get-tuple-element.71), calls=%async_computation | async-start | bytes 196608 | tf_op jit(solution)/shard_map/all_to_all | solution.py:724
  38.5 7.8 %collective-permute-start.10 = (f32[14,8,128]{2,1,0:T(8,128)S(1)}, f32[14,8,128]{2,1,0:T(8,128)S(1)}, u32[]{:S(2)}, u32[]{:S(2)}) collective-permute-start(f32[14,8,128]{2,1,0:T(8,128)S(1)} %get-tuple-element.73), channel_id=1, source_target_pairs={{0,32},{32,64},{64,96},{96,128},{128,160},{160,192},{192,224},{224... | collective-permute-start | bytes 172040 | tf_op jit(solution)/shard_map/ppermute | solution.py:20
  40.5 5.7 %collective-permute-start.11 = (f32[14,8,128]{2,1,0:T(8,128)S(1)}, f32[14,8,128]{2,1,0:T(8,128)S(1)}, u32[]{:S(2)}, u32[]{:S(2)}) collective-permute-start(f32[14,8,128]{2,1,0:T(8,128)S(1)} %get-tuple-element.74), channel_id=1, source_target_pairs={{0,224},{32,0},{64,32},{96,64},{128,96},{160,128},{192,160},{224,1... | collective-permute-start | bytes 172040 | tf_op jit(solution)/shard_map/ppermute | solution.py:20
  48.2 5.2 %collective-permute-start.12 = (f32[30,8,128]{2,1,0:T(8,128)S(1)}, f32[30,8,128]{2,1,0:T(8,128)S(1)}, u32[]{:S(2)}, u32[]{:S(2)}) collective-permute-start(f32[30,8,128]{2,1,0:T(8,128)S(1)} %get-tuple-element.75), channel_id=1, source_target_pairs={{0,1},{1,2},{2,3},{3,4},{4,5},{5,6},{6,7},{7,8},{8,9},{9,10},{10,1... | collective-permute-start | bytes 368648 | tf_op jit(solution)/shard_map/ppermute | solution.py:20
  48.5 4.9 %collective-permute-start.13 = (f32[30,8,128]{2,1,0:T(8,128)S(1)}, f32[30,8,128]{2,1,0:T(8,128)S(1)}, u32[]{:S(2)}, u32[]{:S(2)}) collective-permute-start(f32[30,8,128]{2,1,0:T(8,128)S(1)} %get-tuple-element.76), channel_id=1, source_target_pairs={{0,31},{1,0},{2,1},{3,2},{4,3},{5,4},{6,5},{7,6},{8,7},{9,8},{10,9... | collective-permute-start | bytes 368648 | tf_op jit(solution)/shard_map/ppermute | solution.py:20
  50.2 13.3 %collective-permute-start.16 = (f32[3,32,256]{2,1,0:T(8,128)S(1)}, f32[3,32,256]{2,1,0:T(8,128)S(1)}, u32[]{:S(2)}, u32[]{:S(2)}) collective-permute-start(f32[3,32,256]{2,1,0:T(8,128)S(1)} %get-tuple-element.88), channel_id=1, source_target_pairs={{0,32},{32,64},{64,96},{96,128},{128,160},{160,192},{192,224},{224... | collective-permute-start | bytes 294920 | tf_op jit(solution)/shard_map/ppermute | solution.py:20
  50.4 13.0 %collective-permute-start.17 = (f32[3,32,256]{2,1,0:T(8,128)S(1)}, f32[3,32,256]{2,1,0:T(8,128)S(1)}, u32[]{:S(2)}, u32[]{:S(2)}) collective-permute-start(f32[3,32,256]{2,1,0:T(8,128)S(1)} %get-tuple-element.89), channel_id=1, source_target_pairs={{0,224},{32,0},{64,32},{96,64},{128,96},{160,128},{192,160},{224,1... | collective-permute-start | bytes 294920 | tf_op jit(solution)/shard_map/ppermute | solution.py:20
  54.4 10.9 %collective-permute-start.14 = (f32[6,8,128]{2,1,0:T(8,128)S(1)}, f32[6,8,128]{2,1,0:T(8,128)S(1)}, u32[]{:S(2)}, u32[]{:S(2)}) collective-permute-start(f32[6,8,128]{2,1,0:T(8,128)S(1)} %get-tuple-element.77.own3), channel_id=1, source_target_pairs={{0,2},{1,3},{4,6},{5,7},{8,10},{9,11},{12,14},{13,15},{16,18},{17,... | collective-permute-start | bytes 73736 | tf_op jit(solution)/shard_map/ppermute | solution.py:32
  63.5 3.8 %collective-permute-start.15 = (f32[6,8,128]{2,1,0:T(8,128)S(1)}, f32[6,8,128]{2,1,0:T(8,128)S(1)}, u32[]{:S(2)}, u32[]{:S(2)}) collective-permute-start(f32[6,8,128]{2,1,0:T(8,128)S(1)} %get-tuple-element.77.own3), channel_id=1, source_target_pairs={{0,1},{2,4},{3,5},{6,8},{7,9},{10,12},{11,13},{14,16},{15,17},{18,... | collective-permute-start | bytes 73736 | tf_op jit(solution)/shard_map/ppermute | solution.py:32

commit v4 on v3

--- a/solution.py
+++ b/solution.py
@@ -192,7 +192,8 @@
     for x in range(8):
         b0[x] = inverse_density(mv[x])
         strip_tiles(left, x, gate(place("gy") > 0, b0[x, 0:4, :]))
-        strip_tiles(right, x, gate(place("gy") < lax.axis_size("gy") - 1, b0[x, 28:32, :]))
+        inside = place("gy") < lax.axis_size("gy") - 1
+        strip_tiles(right, x, gate(inside, b0[x, 28:32, :]))
     copies[1].wait()
     for x in range(8):
         c0[x] = reaction_of(fv[x])
@@ -205,14 +206,13 @@
 
 
 def k_edge0(b0, c0, g0, low, high):
-    for k in range(4):
+    for k in range(3):
         low[k] = gate(place("gx") > 0, b0[k])
-        high[k] = gate(place("gx") < lax.axis_size("gx") - 1, b0[4 + k])
-    for k in range(3):
-        low[4 + k] = c0[k]
-        high[4 + k] = c0[5 + k]
-        low[7 + k] = g0[k]
-        high[7 + k] = g0[5 + k]
+        high[k] = gate(place("gx") < lax.axis_size("gx") - 1, b0[5 + k])
+        low[3 + k] = c0[k] + harmonic(b0[2], b0[3]) if k == 2 else c0[k]
+        high[3 + k] = c0[5 + k] + harmonic(b0[5], b0[4]) if k == 0 else c0[5 + k]
+        low[6 + k] = g0[k]
+        high[6 + k] = g0[5 + k]
 
 
 def split_pair(tmp, k, value):
@@ -237,45 +237,52 @@
     out[t, 4:8, :] = value[:, 128:256]
 
 
+CORNER = 7
+
+
 def k_corner0(left, right, low, high):
     for side, strips in enumerate((left, right)):
-        for k in range(4):
-            low[10 * side + k] = gate(place("gx") > 0, strips[k])
-            high[10 * side + k] = gate(place("gx") < lax.axis_size("gx") - 1, strips[4 + k])
+        at = CORNER * side
         for k in range(3):
-            low[10 * side + 4 + k] = strips[8 + k]
-            high[10 * side + 4 + k] = strips[13 + k]
-            low[10 * side + 7 + k] = strips[16 + k]
-            high[10 * side + 7 + k] = strips[21 + k]
+            low[at + k] = gate(place("gx") > 0, strips[k])
+            high[at + k] = gate(place("gx") < lax.axis_size("gx") - 1, strips[5 + k])
+        for k in range(2):
+            low[at + 3 + k] = strips[8 + k]
+            high[at + 3 + k] = strips[14 + k]
+            low[at + 5 + k] = strips[16 + k]
+            high[at + 5 + k] = strips[22 + k]
 
 
 def put_strip0(ext, row, tile, high):
-    at = 40 if high else 4
+    at = 36 if high else 0
     ext[row, at : at + 4, 0:128] = tile[0:4, :]
     ext[row, at : at + 4, 128:256] = tile[4:8, :]
 
 
 def assemble0(b0, c0, g0, below, above, left, right, under, over, be, ce, ge):
-    zeros = jnp.zeros((8, 256), F32)
-    for which, (ext, own, base, reach) in enumerate(
-        ((be, b0, 0, 4), (ce, c0, 4, 3), (ge, g0, 7, 3))
+    zero = jnp.zeros((8, 128), F32)
+    for which, (ext, own, corner, reach) in enumerate(
+        ((be, b0, 0, 3), (ce, c0, 3, 2), (ge, g0, 5, 2))
     ):
-        for x in range(16):
-            ext[x, 0:8, :] = zeros
-            ext[x, 40:48, :] = zeros
-        for x in range(-reach, 8 + reach):
+        for x in range(-3, 11):
             if x < 0:
-                k = base + x + reach
-                val, strips = below[k], (under[k], under[10 + k])
+                val = below[3 * which + x + 3]
+                k = corner + x + reach
+                near = x >= -reach
+                strips = (under[k], under[CORNER + k]) if near else (zero, zero)
             elif x < 8:
-                k = 8 * which + x
-                val, strips = own[x], (left[k], right[k])
+                val = own[x]
+                strips = left[8 * which + x], right[8 * which + x]
             else:
-                k = base + x - 8
-                val, strips = above[k], (over[k], over[10 + k])
-            ext[4 + x, 8:40, :] = val
+                val = above[3 * which + x - 8]
+                k = corner + x - 8
+                near = x - 8 < reach
+                strips = (over[k], over[CORNER + k]) if near else (zero, zero)
+            ext[4 + x, 4:36, :] = val
             put_strip0(ext, 4 + x, strips[0], False)
             put_strip0(ext, 4 + x, strips[1], True)
+    for x in (0, 15):
+        be[x] = jnp.zeros(be.shape[1:], F32)
 
 
 def k_descend0(
@@ -289,13 +296,13 @@
     sweep(va, vb, s, 2, 14, 6)
     sweep(vb, va, s, 3, 13, 5)
     for x in range(8):
-        v0[x] = va[4 + x, 8:40, :]
+        v0[x] = va[4 + x, 4:36, :]
     kept = None
     for x, here, res in residual_rows(va, s, 4, 12):
         if x % 2 == 0:
-            kept = res[8:40, :]
+            kept = res
         else:
-            split_pair(tmp, (x - 4) // 2, kept + res[8:40, :])
+            split_pair(tmp, (x - 4) // 2, (kept + res)[4:36, :])
     t = fold_level0(tmp)
     for x in range(4):
         g1[x] = t[16 * x : 16 * x + 16]
@@ -308,7 +315,7 @@
         high[7 + k] = t[16 * k + 16 : 16 * k + 32]
 
 
-def k_pack_y1(g1, b1, c1, v0, below, above, low, high, vlow, vhigh):
+def k_pack_y1(g1, b1, c1, v0, below, above, low, high):
     for out, at, inside in ((low, 0, place("gy") > 0), (high, 12, place("gy") < lax.axis_size("gy") - 1)):
         cut = pl.ds(at, 4)
         t = 0
@@ -325,14 +332,11 @@
                 t += 1
         for x in range(8):
             strip_tiles(out, 16 + x, v0[x, pl.ds(0 if at == 0 else 28, 4), :])
-    for k in range(3):
-        vlow[k] = v0[k]
-        vhigh[k] = v0[5 + k]
 
 
 def k_descend1(
     g1, b1, c1, bc2, below, above, left, right,
-    v1, pay, low, high, be, ce, ge,
+    v1, pay, be, ce, ge,
     wx, wy, wz, wl, rd, va, vb, tmp,
 ):
     zeros = jnp.zeros((8, 128), F32)
@@ -372,32 +376,39 @@
         pay[k, 1] = bc2[0]
         pay[k, 2] = bc2[1]
 
-    for out, first in ((low, 0), (high, 5)):
+
+def k_pack_v(v0, v1, left, right, low, high):
+    for out, first, edge in ((low, 0, 0), (high, 5, 6)):
+        for k in range(3):
+            for q in range(4):
+                for h in range(2):
+                    out[8 * k + 2 * q + h] = v0[
+                        first + k, 8 * q : 8 * q + 8, 128 * h : 128 * h + 128
+                    ]
+        for k in range(2):
+            out[24 + k] = left[16 + edge + k]
+            out[26 + k] = right[16 + edge + k]
         for k in range(4):
             for q in range(2):
-                out[2 * k + q] = va[4 + k, 8 + 8 * q : 16 + 8 * q, :]
-        for k in range(3):
-            out[8 + k] = left[16 + first + k]
-            out[11 + k] = right[16 + first + k]
+                out[28 + 2 * k + q] = v1[k, 8 * q : 8 * q + 8, :]
 
 
 def k_pack_y2(v1, below, above, gathered, low, high):
-    for out, is_high, inside in (
-        (low, False, place("gy") > 0), (high, True, place("gy") < lax.axis_size("gy") - 1)
+    for out, q, inside in (
+        (low, 0, place("gy") > 0), (high, 1, place("gy") < lax.axis_size("gy") - 1)
     ):
         for k in range(3):
             for i in range(8):
                 val = gathered[i, k]
                 out[8 * k + i] = gate(inside, val) if k == 1 else val
-        q = 1 if is_high else 0
         cut = pl.ds(4 * q, 4)
         for t, x in enumerate(range(-4, 8)):
             if x < 0:
-                val = below[2 * (x + 4) + q, cut, :]
+                val = below[28 + 2 * (x + 4) + q, cut, :]
             elif x < 4:
                 val = v1[x, pl.ds(12 * q, 4), :]
             else:
-                val = above[2 * (x - 4) + q, cut, :]
+                val = above[28 + 2 * (x - 4) + q, cut, :]
             half = 4 * (t % 2)
             out[24 + t // 2, half : half + 4, :] = val
 
@@ -535,39 +546,39 @@
 
 def k_prepare(
     b0, c0, g0, below0, above0, left0, right0, under0, over0, be1, ce1, ge1,
-    v0, below, above, left, right, v1, below1, above1, left1, right1,
+    v0, v1, left, right, below, above, left1, right1,
     p0, ce, ge, wx, wy, wz, wl, rd, p1, wx1, wy1, wz1, wl1, rd1,
     be, va, va1,
 ):
     assemble0(b0, c0, g0, below0, above0, left0, right0, under0, over0, be, ce, ge)
     weights(be, (wx, wy, wz, wl, rd, ce, ge), va, 1.0, 2, 14, 6)
     weights(be1, (wx1, wy1, wz1, wl1, rd1, ce1, ge1), va1, 0.25, 1, 11, 10)
-    narrow = jnp.zeros((8, 128), F32)
-    wide = jnp.zeros((8, 256), F32)
+    zero = jnp.zeros((8, 128), F32)
     for t, x in enumerate(range(-4, 8)):
-        p1[t, 0:8, :] = narrow
-        p1[t, 24:32, :] = narrow
+        p1[t, 0:8, :] = zero
+        p1[t, 24:32, :] = zero
         if 0 <= x < 4:
             p1[t, 8:24, :] = v1[x]
         else:
+            src, k = (below, x + 4) if x < 0 else (above, x - 4)
             for q in range(2):
-                src, k = (below1, x + 4) if x < 0 else (above1, x - 4)
-                p1[t, 8 + 8 * q : 16 + 8 * q, :] = src[2 * k + q]
+                p1[t, 8 + 8 * q : 16 + 8 * q, :] = src[28 + 2 * k + q]
         half = 4 * (t % 2)
         p1[t, 4:8, :] = left1[24 + t // 2, half : half + 4, :]
         p1[t, 24:28, :] = right1[24 + t // 2, half : half + 4, :]
     for x in range(-3, 11):
-        p0[4 + x, 0:8, :] = wide
-        p0[4 + x, 40:48, :] = wide
-        if x < 0:
-            k = x + 3
-            val, strips = below[k], (below1[8 + k], below1[11 + k])
-        elif x < 8:
-            val, strips = v0[x], (left[16 + x], right[16 + x])
+        if 0 <= x < 8:
+            p0[4 + x, 4:36, :] = v0[x]
+            strips = left[16 + x], right[16 + x]
         else:
-            k = x - 8
-            val, strips = above[k], (above1[8 + k], above1[11 + k])
-        p0[4 + x, 8:40, :] = val
+            src, k = (below, x + 3) if x < 0 else (above, x - 8)
+            for q in range(4):
+                for h in range(2):
+                    p0[4 + x, 4 + 8 * q : 12 + 8 * q, 128 * h : 128 * h + 128] = (
+                        src[8 * k + 2 * q + h]
+                    )
+            e = x + 2 if x < 0 else x - 8
+            strips = (src[24 + e], src[26 + e]) if 0 <= e < 2 else (zero, zero)
         put_strip0(p0, 4 + x, strips[0], False)
         put_strip0(p0, 4 + x, strips[1], True)
 
@@ -577,7 +588,7 @@
     p0, ce0, ge0, wx0, wy0, wz0, wl0, rd0,
     p1, ce1, ge1, wx1, wy1, wz1, wl1, rd1,
     pressure, residual,
-    all3, m2, p2, p1a, p1b, p0a, p0b, f1, f0,
+    all3, m2, p2, p1a, p1b, p0a, p0b, f1, f0, own, res0, sems,
 ):
     ix = place("gx")
     iy = place("gy")
@@ -642,12 +653,12 @@
     sweep(p1b, p1a, s1, 2, 10, 8)
 
     wide = jnp.where(iota((128, 256), 0) == iota((128, 256), 1) // 2, F32(1.0), zero)
-    fine = pick(jnp.concatenate([p1a[2 + x, 4:28, :] for x in range(8)], axis=0), wide)
+    fine = pick(jnp.concatenate([p1a[2 + x, 6:26, :] for x in range(8)], axis=0), wide)
     for x in range(8):
         for h in range(2):
-            part = fine[24 * x : 24 * x + 24, 128 * h : 128 * h + 128]
-            f0[x, h, pl.ds(0, 24, stride=2), :] = part
-            f0[x, h, pl.ds(1, 24, stride=2), :] = part
+            part = fine[20 * x : 20 * x + 20, 128 * h : 128 * h + 128]
+            f0[x, h, pl.ds(0, 20, stride=2), :] = part
+            f0[x, h, pl.ds(1, 20, stride=2), :] = part
     for x in range(1, 15):
         for h in range(2):
             cut = pl.ds(128 * h, 128)
@@ -655,12 +666,21 @@
     s0 = (wx0, wy0, wz0, wl0, rd0, ce0, ge0)
     sweep(p0a, p0b, s0, 2, 14, 6)
     sweep(p0b, p0a, s0, 3, 13, 5)
+    for x in range(8):
+        own[x] = p0a[4 + x, 4:36, :]
+    copies = [pltpu.make_async_copy(own, pressure, sems.at[0])]
+    copies[0].start()
     for x, here, res in residual_rows(p0a, s0, 4, 12):
-        pressure[x - 4] = here[8:40, :]
-        residual[x - 4] = res[8:40, :]
-
-
-def call(kernel, name, outs, scratch, limit, *args, anywhere=()):
+        res0[x - 4] = res[4:36, :]
+        if x % 4 == 3:
+            cut = pl.ds(x - 7, 4)
+            copies.append(pltpu.make_async_copy(res0.at[cut], residual.at[cut], sems.at[x // 4]))
+            copies[-1].start()
+    for copy in copies:
+        copy.wait()
+
+
+def call(kernel, name, outs, scratch, limit, *args, anywhere=(), to_hbm=False):
     vmem = pl.BlockSpec(memory_space=pltpu.VMEM)
     hbm = pl.BlockSpec(memory_space=pltpu.HBM)
     specs = [vmem for _ in args]
@@ -671,14 +691,14 @@
         name=name,
         out_shape=[jax.ShapeDtypeStruct(s, F32) for s in outs],
         in_specs=specs,
-        out_specs=[vmem for _ in outs],
+        out_specs=[hbm if to_hbm else vmem for _ in outs],
         scratch_shapes=[pltpu.VMEM(s, F32) if isinstance(s, tuple) else s for s in scratch],
         compiler_params=pltpu.CompilerParams(vmem_limit_bytes=limit * MIB),
     )(*args)
 
 
 B0 = (8, 32, 256)
-E0 = (16, 48, 256)
+E0 = (16, 40, 256)
 E1 = (12, 32, 128)
 E2 = (8, 24, 128)
 
@@ -693,9 +713,9 @@
         4, material, flags, source, anywhere=(0, 1, 2),
     )
     left0, right0 = exchange(left, right, "gy")
-    low, high = call(k_edge0, "edge0", [(10, 32, 256)] * 2, [], 4, b0, c0, g0)
+    low, high = call(k_edge0, "edge0", [(9, 32, 256)] * 2, [], 4, b0, c0, g0)
     below0, above0 = exchange(low, high, "gx")
-    low, high = call(k_corner0, "corner0", [(20, 8, 128)] * 2, [], 4, left0, right0)
+    low, high = call(k_corner0, "corner0", [(14, 8, 128)] * 2, [], 4, left0, right0)
     under0, over0 = exchange(low, high, "gx")
     b1, c1, bc2 = call(
         k_coefs, "coefs", [(4, 16, 128), (4, 16, 128), (2, 8, 128)],
@@ -709,22 +729,21 @@
         *blocks0, b1, c1,
     )
     below, above = exchange(low, high, "gx")
-    low, high, vlow, vhigh = call(
-        k_pack_y1, "pack_y1", [(24, 8, 128)] * 2 + [(3, 32, 256)] * 2, [], 4,
-        g1, b1, c1, v0, below, above,
+    low, high = call(
+        k_pack_y1, "pack_y1", [(24, 8, 128)] * 2, [], 4, g1, b1, c1, v0, below, above
     )
     left, right = exchange(low, high, "gy")
-    vbelow, vabove = exchange(vlow, vhigh, "gx")
-    v1, pay, low, high, be1, ce1, ge1 = call(
+    v1, pay, be1, ce1, ge1 = call(
         k_descend1, "descend1",
-        [(4, 16, 128), (8, 3, 8, 128), (14, 8, 128), (14, 8, 128)] + [E1] * 3,
+        [(4, 16, 128), (8, 3, 8, 128)] + [E1] * 3,
         [E1] * 7 + [(2, 16, 128)], 4,
         g1, b1, c1, bc2, below, above, left, right,
     )
     gathered = lax.all_to_all(pay, "gx", 0, 0)
-    below1, above1 = exchange(low, high, "gx")
+    low, high = call(k_pack_v, "pack_v", [(36, 8, 128)] * 2, [], 4, v0, v1, left, right)
+    below, above = exchange(low, high, "gx")
     low, high = call(
-        k_pack_y2, "pack_y2", [(30, 8, 128)] * 2, [], 4, v1, below1, above1, gathered
+        k_pack_y2, "pack_y2", [(30, 8, 128)] * 2, [], 4, v1, below, above, gathered
     )
     left1, right1 = exchange(low, high, "gy")
     v2, own3, *s2 = call(
@@ -734,14 +753,14 @@
     r0, r1 = swap_chips(own3, "gy", 0), swap_chips(own3, "gy", 1)
     p0, ce0, ge0, wx0, wy0, wz0, wl0, rd0, p1, *w1 = call(
         k_prepare, "prepare", [E0] * 8 + [E1] * 6, [E0, E0, E1], 8,
-        *blocks0, be1, ce1, ge1, v0, vbelow, vabove, left, right,
-        v1, below1, above1, left1, right1,
+        *blocks0, be1, ce1, ge1, v0, v1, left, right, below, above, left1, right1,
     )
     pressure, residual = call(
         k_ascend, "ascend", [B0] * 2,
-        [(18, 8, 128), (128, 128), E2, E1, E1, E0, E0, (6, 32, 128), (8, 2, 48, 128)], 8,
-        own3, r0, r1, v2, *s2,
-        p0, ce0, ge0, wx0, wy0, wz0, wl0, rd0, p1, ce1, ge1, *w1,
+        [(18, 8, 128), (128, 128), E2, E1, E1, E0, E0, (6, 32, 128), (8, 2, 40, 128),
+         B0, B0, pltpu.SemaphoreType.DMA((3,))],
+        8, own3, r0, r1, v2, *s2,
+        p0, ce0, ge0, wx0, wy0, wz0, wl0, rd0, p1, ce1, ge1, *w1, to_hbm=True,
     )
     return pressure, residual
 

time: 71.5 us -> 70.4 us (0.985)
  starting transfers between devices: 40.3 us -> 36.8 us
  waiting for transfers between devices: 18.4 us -> 21.1 us
    ppermute x16 -> x14, waiting for transfers between devices: 13.9 us -> 18.3 us  [shift(): lax.ppermute(block, axis, [(i, (i + step) % count) for i in range(count)])]
    ppermute x16 -> x14, starting transfers between devices: 25.1 us -> 21.7 us  [shift(): lax.ppermute(block, axis, [(i, (i + step) % count) for i in range(count)])]
    all_to_all x1, waiting for transfers between devices: 1.86 us -> 0.01 us  [per_device(): gathered = lax.all_to_all(pay, 'gx', 0, 0)]
    pallas_call x11 -> x12, Pallas kernels: 11.9 us -> 11.4 us  [call(): pl.pallas_call(kernel, name=name, out_shape=[jax.ShapeDtypeStruct(s, F32)...]
  transfers between devices with their start and end apart: 19 -> 17, of which waited for: 8 -> 8; matrix products, arithmetic and copies ran while one was open for 0% -> 0% of each run, Pallas kernels for 4% -> 2%
where the time goes in v4:
time: 70.4 us; the launch traced here: 70.2 us
  starting transfers between devices  36.8 us (52%)
  waiting for transfers between devices  21.1 us (30%)
  Pallas kernels  11.4 us (16%)
  between operations  0.89 us (1%)
    ppermute x14, starting transfers between devices, shift(): lax.ppermute(block, axis, [(i, (i + step) % count) for i in range(count)])  21.7 us
    ppermute x14, waiting for transfers between devices, shift(): lax.ppermute(block, axis, [(i, (i + step) % count) for i in range(count)])  18.3 us
    pallas_call x12, Pallas kernels, call(): pl.pallas_call(kernel, name=name, out_shape=[jax.ShapeDtypeStruct(s, F32)...  11.4 us
    ppermute x2, starting transfers between devices, swap_chips(): return lax.ppermute(block, axis, pairs + [(b, a) for a, b in pairs])  8.97 us
    all_to_all x1, starting transfers between devices, per_device(): gathered = lax.all_to_all(pay, 'gx', 0, 0)  6.12 us
    ppermute x2, waiting for transfers between devices, swap_chips(): return lax.ppermute(block, axis, pairs + [(b, a) for a, b in pairs])  2.77 us
  transfers between devices with their start and end apart: 17, of which 8 were waited for; matrix products, arithmetic and copies ran while one was open for 0% of the time, Pallas kernels for 2%

profile of v4, /device:TPU:2, one launch (start us, length us, event | category | flops | bytes accessed | tf_op | source)
XLA Modules:
  0.0 70.2 jit_solution(4573361352691043293)
XLA Ops:
  0.6 1.1 %load0.1 = (f32[24,8,128]{2,1,0:T(8,128)S(1)}, f32[24,8,128]{2,1,0:T(8,128)S(1)}, f32[8,32,256]{2,1,0:T(8,128)S(1)}, f32[8,32,256]{2,1,0:T(8,128)S(1)}, f32[8,32,256]{2,1,0:T(8,128)S(1)}) custom-call(s32[8,32,256]{2,1,0:T(8,128)} %m.1, s32[8,32,256]{2,1,0:T(8,128)} %f.1, f32[8,32,256]{2,1,0:T(8,128)} %g.1), custom_call_target="tpu_custom_call" | custom-call | tf_op jit(solution)/shard_map/load0/pallas_call | solution.py:689
  1.8 2.0 %collective-permute-start = (f32[9,32,256]{2,1,0:T(8,128)S(1)}, f32[9,32,256]{2,1,0:T(8,128)S(1)}, u32[]{:S(2)}, u32[]{:S(2)}) collective-permute-start(f32[9,32,256]{2,1,0:T(8,128)S(1)} %get-tuple-element.54), channel_id=1, source_target_pairs={{0,32},{32,64},{64,96},{96,128},{128,160},{160,192},{192,224},{224... | collective-permute-start | bytes 884744 | tf_op jit(solution)/shard_map/ppermute | solution.py:20
  3.8 4.0 %collective-permute-start.1 = (f32[9,32,256]{2,1,0:T(8,128)S(1)}, f32[9,32,256]{2,1,0:T(8,128)S(1)}, u32[]{:S(2)}, u32[]{:S(2)}) collective-permute-start(f32[9,32,256]{2,1,0:T(8,128)S(1)} %get-tuple-element.55), channel_id=1, source_target_pairs={{0,224},{32,0},{64,32},{96,64},{128,96},{160,128},{192,160},{224,1... | collective-permute-start | bytes 884744 | tf_op jit(solution)/shard_map/ppermute | solution.py:20
  7.9 1.7 %collective-permute-start.3 = (f32[24,8,128]{2,1,0:T(8,128)S(1)}, f32[24,8,128]{2,1,0:T(8,128)S(1)}, u32[]{:S(2)}, u32[]{:S(2)}) collective-permute-start(f32[24,8,128]{2,1,0:T(8,128)S(1)} %get-tuple-element.57), channel_id=1, source_target_pairs={{0,31},{1,0},{2,1},{3,2},{4,3},{5,4},{6,5},{7,6},{8,7},{9,8},{10,9... | collective-permute-start | bytes 294920 | tf_op jit(solution)/shard_map/ppermute | solution.py:20
  9.6 2.3 %collective-permute-done.2.left.left0 = f32[24,8,128]{2,1,0:T(8,128)S(1)} collective-permute-done((f32[24,8,128]{2,1,0:T(8,128)S(1)}, f32[24,8,128]{2,1,0:T(8,128)S(1)}, u32[]{:S(2)}, u32[]{:S(2)}) %collective-permute-start.2) | collective-permute-done | bytes 98336 | tf_op jit(solution)/shard_map/ppermute | solution.py:20
  12.0 3.2 %collective-permute-start.5 = (f32[14,8,128]{2,1,0:T(8,128)S(1)}, f32[14,8,128]{2,1,0:T(8,128)S(1)}, u32[]{:S(2)}, u32[]{:S(2)}) collective-permute-start(f32[14,8,128]{2,1,0:T(8,128)S(1)} %get-tuple-element.59), channel_id=1, source_target_pairs={{0,224},{32,0},{64,32},{96,64},{128,96},{160,128},{192,160},{224,1... | collective-permute-start | bytes 172040 | tf_op jit(solution)/shard_map/ppermute | solution.py:20
  15.8 1.6 %collective-permute-done.4.under.under0 = f32[14,8,128]{2,1,0:T(8,128)S(1)} collective-permute-done((f32[14,8,128]{2,1,0:T(8,128)S(1)}, f32[14,8,128]{2,1,0:T(8,128)S(1)}, u32[]{:S(2)}, u32[]{:S(2)}) %collective-permute-start.4) | collective-permute-done | bytes 57376 | tf_op jit(solution)/shard_map/ppermute | solution.py:20
  17.4 2.3 %descend0.1 = (f32[8,32,256]{2,1,0:T(8,128)S(1)}, f32[4,16,128]{2,1,0:T(8,128)S(1)}, f32[10,16,128]{2,1,0:T(8,128)S(1)}, f32[10,16,128]{2,1,0:T(8,128)S(1)}) custom-call(f32[8,32,256]{2,1,0:T(8,128)S(1)} %get-tuple-element.51.b0, f32[8,32,256]{2,1,0:T(8,128)S(1)} %get-tuple-element.52.c0, f32[8,32,256]{2,1,0:T(8,128)S(1)} %get-tuple-element.53.g0, ...), custom_call_target="tpu_custom_call" | custom-call | tf_op jit(solution)/shard_map/descend0/pallas_call | solution.py:689
  19.8 3.3 %collective-permute-start.7 = (f32[10,16,128]{2,1,0:T(8,128)S(1)}, f32[10,16,128]{2,1,0:T(8,128)S(1)}, u32[]{:S(2)}, u32[]{:S(2)}) collective-permute-start(f32[10,16,128]{2,1,0:T(8,128)S(1)} %get-tuple-element.65), channel_id=1, source_target_pairs={{0,224},{32,0},{64,32},{96,64},{128,96},{160,128},{192,160},{224,1... | collective-permute-start | bytes 245768 | tf_op jit(solution)/shard_map/ppermute | solution.py:20
  23.1 3.0 %collective-permute-done.6.below = f32[10,16,128]{2,1,0:T(8,128)S(1)} collective-permute-done((f32[10,16,128]{2,1,0:T(8,128)S(1)}, f32[10,16,128]{2,1,0:T(8,128)S(1)}, u32[]{:S(2)}, u32[]{:S(2)}) %collective-permute-start.6) | collective-permute-done | bytes 81952 | tf_op jit(solution)/shard_map/ppermute | solution.py:20
  26.3 1.7 %collective-permute-start.9 = (f32[24,8,128]{2,1,0:T(8,128)S(1)}, f32[24,8,128]{2,1,0:T(8,128)S(1)}, u32[]{:S(2)}, u32[]{:S(2)}) collective-permute-start(f32[24,8,128]{2,1,0:T(8,128)S(1)} %get-tuple-element.68), channel_id=1, source_target_pairs={{0,31},{1,0},{2,1},{3,2},{4,3},{5,4},{6,5},{7,6},{8,7},{9,8},{10,9... | collective-permute-start | bytes 294920 | tf_op jit(solution)/shard_map/ppermute | solution.py:20
  28.0 2.3 %collective-permute-done.8.left = f32[24,8,128]{2,1,0:T(8,128)S(1)} collective-permute-done((f32[24,8,128]{2,1,0:T(8,128)S(1)}, f32[24,8,128]{2,1,0:T(8,128)S(1)}, u32[]{:S(2)}, u32[]{:S(2)}) %collective-permute-start.8) | collective-permute-done | bytes 98336 | tf_op jit(solution)/shard_map/ppermute | solution.py:20
  30.3 1.3 %descend1.1 = (f32[4,16,128]{2,1,0:T(8,128)S(1)}, f32[8,3,8,128]{3,2,1,0:T(8,128)}, f32[12,32,128]{2,1,0:T(8,128)S(1)}, f32[12,32,128]{2,1,0:T(8,128)S(1)}, f32[12,32,128]{2,1,0:T(8,128)S(1)}) custom-call(f32[4,16,128]{2,1,0:T(8,128)S(1)} %get-tuple-element.62.g1, f32[4,16,128]{2,1,0:T(8,128)S(1)} %get-tuple-element.60.b1, ...), custom_call_target="tpu_custom_call" | custom-call | tf_op jit(solution)/shard_map/descend1/pallas_call | solution.py:689
  31.6 6.1 %all-to-all-start = ((f32[8,3,8,128]{3,2,1,0:T(8,128)}), f32[8,3,8,128]{3,2,1,0:T(8,128)S(1)}, u32[]{:S(2)}, u32[]{:S(2)}) async-start(f32[8,3,8,128]{3,2,1,0:T(8,128)} %get-tuple-element.69), calls=%async_computation | async-start | bytes 196608 | tf_op jit(solution)/shard_map/all_to_all | solution.py:742
  37.7 2.1 %collective-permute-start.10 = (f32[36,8,128]{2,1,0:T(8,128)S(1)}, f32[36,8,128]{2,1,0:T(8,128)S(1)}, u32[]{:S(2)}, u32[]{:S(2)}) collective-permute-start(f32[36,8,128]{2,1,0:T(8,128)S(1)} %get-tuple-element.71), channel_id=1, source_target_pairs={{0,32},{32,64},{64,96},{96,128},{128,160},{160,192},{192,224},{224... | collective-permute-start | bytes 442376 | tf_op jit(solution)/shard_map/ppermute | solution.py:20
  39.8 1.3 %collective-permute-start.11 = (f32[36,8,128]{2,1,0:T(8,128)S(1)}, f32[36,8,128]{2,1,0:T(8,128)S(1)}, u32[]{:S(2)}, u32[]{:S(2)}) collective-permute-start(f32[36,8,128]{2,1,0:T(8,128)S(1)} %get-tuple-element.72), channel_id=1, source_target_pairs={{0,224},{32,0},{64,32},{96,64},{128,96},{160,128},{192,160},{224,1... | collective-permute-start | bytes 442376 | tf_op jit(solution)/shard_map/ppermute | solution.py:20
  41.1 6.6 %collective-permute-done.10.below = f32[36,8,128]{2,1,0:T(8,128)S(1)} collective-permute-done((f32[36,8,128]{2,1,0:T(8,128)S(1)}, f32[36,8,128]{2,1,0:T(8,128)S(1)}, u32[]{:S(2)}, u32[]{:S(2)}) %collective-permute-start.10) | collective-permute-done | bytes 147488 | tf_op jit(solution)/shard_map/ppermute | solution.py:20
  48.1 1.6 %collective-permute-start.13 = (f32[30,8,128]{2,1,0:T(8,128)S(1)}, f32[30,8,128]{2,1,0:T(8,128)S(1)}, u32[]{:S(2)}, u32[]{:S(2)}) collective-permute-start(f32[30,8,128]{2,1,0:T(8,128)S(1)} %get-tuple-element.74), channel_id=1, source_target_pairs={{0,31},{1,0},{2,1},{3,2},{4,3},{5,4},{6,5},{7,6},{8,7},{9,8},{10,9... | collective-permute-start | bytes 368648 | tf_op jit(solution)/shard_map/ppermute | solution.py:20
  49.7 2.6 %collective-permute-done.12.left.left1 = f32[30,8,128]{2,1,0:T(8,128)S(1)} collective-permute-done((f32[30,8,128]{2,1,0:T(8,128)S(1)}, f32[30,8,128]{2,1,0:T(8,128)S(1)}, u32[]{:S(2)}, u32[]{:S(2)}) %collective-permute-start.12) | collective-permute-done | bytes 122912 | tf_op jit(solution)/shard_map/ppermute | solution.py:20
  52.3 1.0 %descend2.1 = (f32[8,24,128]{2,1,0:T(8,128)S(1)}, f32[6,8,128]{2,1,0:T(8,128)S(1)}, f32[8,24,128]{2,1,0:T(8,128)S(1)}, f32[8,24,128]{2,1,0:T(8,128)S(1)}, f32[8,...) custom-call(f32[8,3,8,128]{3,2,1,0:T(8,128)S(1)} %all-to-all-done.gather, ...), custom_call_target="tpu_custom_call" | custom-call | tf_op jit(solution)/shard_map/descend2/pallas_call | solution.py:689
  53.3 9.0 %collective-permute-start.14 = (f32[6,8,128]{2,1,0:T(8,128)S(1)}, f32[6,8,128]{2,1,0:T(8,128)S(1)}, u32[]{:S(2)}, u32[]{:S(2)}) collective-permute-start(f32[6,8,128]{2,1,0:T(8,128)S(1)} %get-tuple-element.75.own3), channel_id=1, source_target_pairs={{0,2},{1,3},{4,6},{5,7},{8,10},{9,11},{12,14},{13,15},{16,18},{17,... | collective-permute-start | bytes 73736 | tf_op jit(solution)/shard_map/ppermute | solution.py:32
  62.2 1.0 %prepare.1 = (f32[16,40,256]{2,1,0:T(8,128)S(1)}, f32[16,40,256]{2,1,0:T(8,128)S(1)}, f32[16,40,256]{2,1,0:T(8,128)S(1)}, f32[16,40,256]{2,1,0:T(8,128)S(1)}, f3...) custom-call(f32[8,32,256]{2,1,0:T(8,128)S(1)} %get-tuple-element.51., ...), custom_call_target="tpu_custom_call" | custom-call | tf_op jit(solution)/shard_map/prepare/pallas_call | solution.py:689
  64.0 2.0 %collective-permute-done.15.r1 = f32[6,8,128]{2,1,0:T(8,128)S(1)} collective-permute-done((f32[6,8,128]{2,1,0:T(8,128)S(1)}, f32[6,8,128]{2,1,0:T(8,128)S(1)}, u32[]{:S(2)}, u32[]{:S(2)}) %collective-permute-start.15) | collective-permute-done | bytes 24608 | tf_op jit(solution)/shard_map/ppermute | solution.py:32
  66.1 4.0 %ascend.1 = (f32[8,32,256]{2,1,0:T(8,128)}, f32[8,32,256]{2,1,0:T(8,128)}) custom-call(f32[6,8,128]{2,1,0:T(8,128)S(1)} %get-tuple-element.75.own3, f32[6,8,128]{2,1,0:T(8,128)S(1)} %collective-permute-done.14.r0, f32[6,8,128]{2,1,0:T(8,128)S(1)} %collective-permute-done.15.r1, f32[8,24,128]{2,1,0:T(8,128)S(1)} %get-tuple-element.76.v2, ...), custom_call_target="tpu_custom_call" | custom-call | tf_op jit(solution)/shard_map/ascend/pallas_call | solution.py:689
  (22 shorter events, 2.1 us)
Async XLA Ops:
  1.8 15.6 %collective-permute-start = (f32[9,32,256]{2,1,0:T(8,128)S(1)}, f32[9,32,256]{2,1,0:T(8,128)S(1)}, u32[]{:S(2)}, u32[]{:S(2)}) collective-permute-start(f32[9,32,256]{2,1,0:T(8,128)S(1)} %get-tuple-element.54), channel_id=1, source_target_pairs={{0,32},{32,64},{64,96},{96,128},{128,160},{160,192},{192,224},{224... | collective-permute-start | bytes 884744 | tf_op jit(solution)/shard_map/ppermute | solution.py:20
  3.8 13.6 %collective-permute-start.1 = (f32[9,32,256]{2,1,0:T(8,128)S(1)}, f32[9,32,256]{2,1,0:T(8,128)S(1)}, u32[]{:S(2)}, u32[]{:S(2)}) collective-permute-start(f32[9,32,256]{2,1,0:T(8,128)S(1)} %get-tuple-element.55), channel_id=1, source_target_pairs={{0,224},{32,0},{64,32},{96,64},{128,96},{160,128},{192,160},{224,1... | collective-permute-start | bytes 884744 | tf_op jit(solution)/shard_map/ppermute | solution.py:20
  7.9 4.0 %collective-permute-start.2 = (f32[24,8,128]{2,1,0:T(8,128)S(1)}, f32[24,8,128]{2,1,0:T(8,128)S(1)}, u32[]{:S(2)}, u32[]{:S(2)}) collective-permute-start(f32[24,8,128]{2,1,0:T(8,128)S(1)} %get-tuple-element.56), channel_id=1, source_target_pairs={{0,1},{1,2},{2,3},{3,4},{4,5},{5,6},{6,7},{7,8},{8,9},{9,10},{10,1... | collective-permute-start | bytes 294920 | tf_op jit(solution)/shard_map/ppermute | solution.py:20
  7.9 4.0 %collective-permute-start.3 = (f32[24,8,128]{2,1,0:T(8,128)S(1)}, f32[24,8,128]{2,1,0:T(8,128)S(1)}, u32[]{:S(2)}, u32[]{:S(2)}) collective-permute-start(f32[24,8,128]{2,1,0:T(8,128)S(1)} %get-tuple-element.57), channel_id=1, source_target_pairs={{0,31},{1,0},{2,1},{3,2},{4,3},{5,4},{6,5},{7,6},{8,7},{9,8},{10,9... | collective-permute-start | bytes 294920 | tf_op jit(solution)/shard_map/ppermute | solution.py:20
  11.9 5.5 %collective-permute-start.4 = (f32[14,8,128]{2,1,0:T(8,128)S(1)}, f32[14,8,128]{2,1,0:T(8,128)S(1)}, u32[]{:S(2)}, u32[]{:S(2)}) collective-permute-start(f32[14,8,128]{2,1,0:T(8,128)S(1)} %get-tuple-element.58), channel_id=1, source_target_pairs={{0,32},{32,64},{64,96},{96,128},{128,160},{160,192},{192,224},{224... | collective-permute-start | bytes 172040 | tf_op jit(solution)/shard_map/ppermute | solution.py:20
  12.0 5.4 %collective-permute-start.5 = (f32[14,8,128]{2,1,0:T(8,128)S(1)}, f32[14,8,128]{2,1,0:T(8,128)S(1)}, u32[]{:S(2)}, u32[]{:S(2)}) collective-permute-start(f32[14,8,128]{2,1,0:T(8,128)S(1)} %get-tuple-element.59), channel_id=1, source_target_pairs={{0,224},{32,0},{64,32},{96,64},{128,96},{160,128},{192,160},{224,1... | collective-permute-start | bytes 172040 | tf_op jit(solution)/shard_map/ppermute | solution.py:20
  19.7 6.4 %collective-permute-start.6 = (f32[10,16,128]{2,1,0:T(8,128)S(1)}, f32[10,16,128]{2,1,0:T(8,128)S(1)}, u32[]{:S(2)}, u32[]{:S(2)}) collective-permute-start(f32[10,16,128]{2,1,0:T(8,128)S(1)} %get-tuple-element.64), channel_id=1, source_target_pairs={{0,32},{32,64},{64,96},{96,128},{128,160},{160,192},{192,224},{224... | collective-permute-start | bytes 245768 | tf_op jit(solution)/shard_map/ppermute | solution.py:20
  19.8 6.3 %collective-permute-start.7 = (f32[10,16,128]{2,1,0:T(8,128)S(1)}, f32[10,16,128]{2,1,0:T(8,128)S(1)}, u32[]{:S(2)}, u32[]{:S(2)}) collective-permute-start(f32[10,16,128]{2,1,0:T(8,128)S(1)} %get-tuple-element.65), channel_id=1, source_target_pairs={{0,224},{32,0},{64,32},{96,64},{128,96},{160,128},{192,160},{224,1... | collective-permute-start | bytes 245768 | tf_op jit(solution)/shard_map/ppermute | solution.py:20
  26.2 4.1 %collective-permute-start.8 = (f32[24,8,128]{2,1,0:T(8,128)S(1)}, f32[24,8,128]{2,1,0:T(8,128)S(1)}, u32[]{:S(2)}, u32[]{:S(2)}) collective-permute-start(f32[24,8,128]{2,1,0:T(8,128)S(1)} %get-tuple-element.67), channel_id=1, source_target_pairs={{0,1},{1,2},{2,3},{3,4},{4,5},{5,6},{6,7},{7,8},{8,9},{9,10},{10,1... | collective-permute-start | bytes 294920 | tf_op jit(solution)/shard_map/ppermute | solution.py:20
  26.3 4.0 %collective-permute-start.9 = (f32[24,8,128]{2,1,0:T(8,128)S(1)}, f32[24,8,128]{2,1,0:T(8,128)S(1)}, u32[]{:S(2)}, u32[]{:S(2)}) collective-permute-start(f32[24,8,128]{2,1,0:T(8,128)S(1)} %get-tuple-element.68), channel_id=1, source_target_pairs={{0,31},{1,0},{2,1},{3,2},{4,3},{5,4},{6,5},{7,6},{8,7},{9,8},{10,9... | collective-permute-start | bytes 294920 | tf_op jit(solution)/shard_map/ppermute | solution.py:20
  31.6 16.1 %all-to-all-start = ((f32[8,3,8,128]{3,2,1,0:T(8,128)}), f32[8,3,8,128]{3,2,1,0:T(8,128)S(1)}, u32[]{:S(2)}, u32[]{:S(2)}) async-start(f32[8,3,8,128]{3,2,1,0:T(8,128)} %get-tuple-element.69), calls=%async_computation | async-start | bytes 196608 | tf_op jit(solution)/shard_map/all_to_all | solution.py:742
  37.7 10.0 %collective-permute-start.10 = (f32[36,8,128]{2,1,0:T(8,128)S(1)}, f32[36,8,128]{2,1,0:T(8,128)S(1)}, u32[]{:S(2)}, u32[]{:S(2)}) collective-permute-start(f32[36,8,128]{2,1,0:T(8,128)S(1)} %get-tuple-element.71), channel_id=1, source_target_pairs={{0,32},{32,64},{64,96},{96,128},{128,160},{160,192},{192,224},{224... | collective-permute-start | bytes 442376 | tf_op jit(solution)/shard_map/ppermute | solution.py:20
  39.8 7.9 %collective-permute-start.11 = (f32[36,8,128]{2,1,0:T(8,128)S(1)}, f32[36,8,128]{2,1,0:T(8,128)S(1)}, u32[]{:S(2)}, u32[]{:S(2)}) collective-permute-start(f32[36,8,128]{2,1,0:T(8,128)S(1)} %get-tuple-element.72), channel_id=1, source_target_pairs={{0,224},{32,0},{64,32},{96,64},{128,96},{160,128},{192,160},{224,1... | collective-permute-start | bytes 442376 | tf_op jit(solution)/shard_map/ppermute | solution.py:20
  47.7 4.6 %collective-permute-start.12 = (f32[30,8,128]{2,1,0:T(8,128)S(1)}, f32[30,8,128]{2,1,0:T(8,128)S(1)}, u32[]{:S(2)}, u32[]{:S(2)}) collective-permute-start(f32[30,8,128]{2,1,0:T(8,128)S(1)} %get-tuple-element.73), channel_id=1, source_target_pairs={{0,1},{1,2},{2,3},{3,4},{4,5},{5,6},{6,7},{7,8},{8,9},{9,10},{10,1... | collective-permute-start | bytes 368648 | tf_op jit(solution)/shard_map/ppermute | solution.py:20
  48.1 4.2 %collective-permute-start.13 = (f32[30,8,128]{2,1,0:T(8,128)S(1)}, f32[30,8,128]{2,1,0:T(8,128)S(1)}, u32[]{:S(2)}, u32[]{:S(2)}) collective-permute-start(f32[30,8,128]{2,1,0:T(8,128)S(1)} %get-tuple-element.74), channel_id=1, source_target_pairs={{0,31},{1,0},{2,1},{3,2},{4,3},{5,4},{6,5},{7,6},{8,7},{9,8},{10,9... | collective-permute-start | bytes 368648 | tf_op jit(solution)/shard_map/ppermute | solution.py:20
  53.3 10.8 %collective-permute-start.14 = (f32[6,8,128]{2,1,0:T(8,128)S(1)}, f32[6,8,128]{2,1,0:T(8,128)S(1)}, u32[]{:S(2)}, u32[]{:S(2)}) collective-permute-start(f32[6,8,128]{2,1,0:T(8,128)S(1)} %get-tuple-element.75.own3), channel_id=1, source_target_pairs={{0,2},{1,3},{4,6},{5,7},{8,10},{9,11},{12,14},{13,15},{16,18},{17,... | collective-permute-start | bytes 73736 | tf_op jit(solution)/shard_map/ppermute | solution.py:32
  62.2 3.8 %collective-permute-start.15 = (f32[6,8,128]{2,1,0:T(8,128)S(1)}, f32[6,8,128]{2,1,0:T(8,128)S(1)}, u32[]{:S(2)}, u32[]{:S(2)}) collective-permute-start(f32[6,8,128]{2,1,0:T(8,128)S(1)} %get-tuple-element.75.own3), channel_id=1, source_target_pairs={{0,1},{2,4},{3,5},{6,8},{7,9},{10,12},{11,13},{14,16},{15,17},{18,... | collective-permute-start | bytes 73736 | tf_op jit(solution)/shard_map/ppermute | solution.py:32

commit v5 on v4

--- a/solution.py
+++ b/solution.py
@@ -72,14 +72,14 @@
         parts.append(
             jnp.concatenate(
                 [
-                    tmp[x, h, pl.ds(0, 16, stride=2), :] + tmp[x, h, pl.ds(1, 16, stride=2), :]
+                    tmp[x, h, pl.ds(0, 24, stride=2), :] + tmp[x, h, pl.ds(1, 24, stride=2), :]
                     for x in range(4)
                 ],
                 axis=0,
             )
         )
     w = jnp.where(iota((256, 128), 0) // 2 == iota((256, 128), 1), F32(0.125), F32(0.0))
-    return pick(jnp.concatenate(parts, axis=1), w)
+    return pick(jnp.concatenate(parts, axis=1), w).reshape(4, 24, 128)
 
 
 def fold_level1(tmp):
@@ -180,6 +180,9 @@
     return jnp.where(inside, value, F32(0.0))
 
 
+STRIPS = 54
+
+
 def k_load0(m, f, g, left, right, b0, c0, g0, mv, fv, sems):
     copies = [
         pltpu.make_async_copy(m, mv, sems.at[0]),
@@ -188,21 +191,34 @@
     ]
     for copy in copies:
         copy.start()
+
+    def strips(a, own):
+        for x in range(8):
+            for out, at, ninth, tenth, inside in (
+                (left, 0, 8, 9, place("gy") > 0),
+                (right, 24, 23, 22, place("gy") < lax.axis_size("gy") - 1),
+            ):
+                near = own[x, at : at + 8, :]
+                far = own[x, ninth : ninth + 1, :]
+                if a == 0:
+                    near, far = gate(inside, near), gate(inside, far)
+                if a == 1:
+                    far = far + harmonic(b0[x, ninth : ninth + 1, :], b0[x, tenth : tenth + 1, :])
+                for h in range(2):
+                    cut = slice(128 * h, 128 * h + 128)
+                    out[16 * a + 2 * x + h] = near[:, cut]
+                    out[48 + 2 * a + h, x : x + 1, :] = far[:, cut]
+
     copies[0].wait()
     for x in range(8):
         b0[x] = inverse_density(mv[x])
-        strip_tiles(left, x, gate(place("gy") > 0, b0[x, 0:4, :]))
-        inside = place("gy") < lax.axis_size("gy") - 1
-        strip_tiles(right, x, gate(inside, b0[x, 28:32, :]))
+    strips(0, b0)
     copies[1].wait()
     for x in range(8):
         c0[x] = reaction_of(fv[x])
-        strip_tiles(left, 8 + x, c0[x, 0:4, :])
-        strip_tiles(right, 8 + x, c0[x, 28:32, :])
+    strips(1, c0)
     copies[2].wait()
-    for x in range(8):
-        strip_tiles(left, 16 + x, g0[x, 0:4, :])
-        strip_tiles(right, 16 + x, g0[x, 28:32, :])
+    strips(2, g0)
 
 
 def k_edge0(b0, c0, g0, low, high):
@@ -220,69 +236,97 @@
         tmp[k, h] = value[:, 128 * h : 128 * h + 128]
 
 
-def k_coefs(b0, c0, b1, c1, bc2, tmp0, tmp1):
+def k_coefs(b0, c0, left, right, b1, c1, bc2, tmp0, tmp1):
     for k, (src, out) in enumerate(((b0, b1), (c0, c1))):
         for x in range(4):
-            split_pair(tmp0, x, src[2 * x] + src[2 * x + 1])
+            pair = src[2 * x] + src[2 * x + 1]
+            for h in range(2):
+                t = 16 * k + 4 * x + h
+                tmp0[x, h, 0:8, :] = left[t] + left[t + 2]
+                tmp0[x, h, 8:40, :] = pair[:, 128 * h : 128 * h + 128]
+                tmp0[x, h, 40:48, :] = right[t] + right[t + 2]
         t = fold_level0(tmp0)
         for x in range(4):
-            out[x] = t[16 * x : 16 * x + 16]
+            out[x] = t[x]
         for x in range(2):
-            tmp1[x] = t[32 * x : 32 * x + 16] + t[32 * x + 16 : 32 * x + 32]
+            tmp1[x] = (t[2 * x] + t[2 * x + 1])[4:20, :]
         bc2[k] = fold_level1(tmp1)
 
 
-def strip_tiles(out, t, value):
-    out[t, 0:4, :] = value[:, 0:128]
-    out[t, 4:8, :] = value[:, 128:256]
-
-
-CORNER = 7
+CORNERS = 37
 
 
 def k_corner0(left, right, low, high):
-    for side, strips in enumerate((left, right)):
-        at = CORNER * side
-        for k in range(3):
-            low[at + k] = gate(place("gx") > 0, strips[k])
-            high[at + k] = gate(place("gx") < lax.axis_size("gx") - 1, strips[5 + k])
-        for k in range(2):
-            low[at + 3 + k] = strips[8 + k]
-            high[at + 3 + k] = strips[14 + k]
-            low[at + 5 + k] = strips[16 + k]
-            high[at + 5 + k] = strips[22 + k]
-
-
-def put_strip0(ext, row, tile, high):
-    at = 36 if high else 0
-    ext[row, at : at + 4, 0:128] = tile[0:4, :]
-    ext[row, at : at + 4, 128:256] = tile[4:8, :]
-
-
-def assemble0(b0, c0, g0, below, above, left, right, under, over, be, ce, ge):
-    zero = jnp.zeros((8, 128), F32)
-    for which, (ext, own, corner, reach) in enumerate(
-        ((be, b0, 0, 3), (ce, c0, 3, 2), (ge, g0, 5, 2))
+    for out, first, edge, third, fourth, inside in (
+        (low, 0, 0, 2, 3, place("gx") > 0),
+        (high, 5, 7, 5, 4, place("gx") < lax.axis_size("gx") - 1),
     ):
+        out[36] = jnp.zeros((8, 128), F32)
+        for side, strips in enumerate((left, right)):
+            for h in range(2):
+                for k in range(3):
+                    x = first + k
+                    at = 18 * side + 2 * k + h
+                    out[at] = gate(inside, strips[2 * x + h])
+                    c = strips[16 + 2 * x + h]
+                    if x == third:
+                        c = c + harmonic(strips[2 * x + h], strips[2 * fourth + h])
+                    out[at + 6] = c
+                    out[at + 12] = strips[32 + 2 * x + h]
+                at = 2 * side + h
+                out[36, at : at + 1, :] = gate(inside, strips[48 + h, edge : edge + 1, :])
+
+
+def blocks0(b0, c0, g0, below, above, left, right, under, over):
+    for a, own in enumerate((b0, c0, g0)):
         for x in range(-3, 11):
-            if x < 0:
-                val = below[3 * which + x + 3]
-                k = corner + x + reach
-                near = x >= -reach
-                strips = (under[k], under[CORNER + k]) if near else (zero, zero)
-            elif x < 8:
-                val = own[x]
-                strips = left[8 * which + x], right[8 * which + x]
+            if 0 <= x < 8:
+                tiles = [[s[16 * a + 2 * x + h] for h in range(2)] for s in (left, right)]
+                ninth = [[s[48 + 2 * a + h, x : x + 1, :] for h in range(2)] for s in (left, right)]
+                yield a, x, own[x], tiles, ninth
             else:
-                val = above[3 * which + x - 8]
-                k = corner + x - 8
-                near = x - 8 < reach
-                strips = (over[k], over[CORNER + k]) if near else (zero, zero)
-            ext[4 + x, 4:36, :] = val
-            put_strip0(ext, 4 + x, strips[0], False)
-            put_strip0(ext, 4 + x, strips[1], True)
+                k = x + 3 if x < 0 else x - 8
+                main, far = (below, under) if x < 0 else (above, over)
+                tiles = [[far[18 * side + 6 * a + 2 * k + h] for h in range(2)] for side in range(2)]
+                ninth = None
+                if a == 0 and x in (-1, 8):
+                    ninth = [
+                        [far[36, 2 * side + h : 2 * side + h + 1, :] for h in range(2)]
+                        for side in range(2)
+                    ]
+                yield a, x, main[3 * a + k], tiles, ninth
+
+
+def assemble_deep(args, exts):
+    zero = jnp.zeros((4, 256), F32)
+    for a, x, own, tiles, ninth in blocks0(*args):
+        ext = exts[a]
+        r = 4 + x
+        ext[r, 0:4, :] = zero
+        ext[r, 12:44, :] = own
+        ext[r, 52:56, :] = zero
+        for h in range(2):
+            cut = pl.ds(128 * h, 128)
+            ext[r, 4:12, cut] = tiles[0][h]
+            ext[r, 44:52, cut] = tiles[1][h]
+            if ninth is not None:
+                ext[r, 3:4, cut] = ninth[0][h]
+                ext[r, 52:53, cut] = ninth[1][h]
     for x in (0, 15):
-        be[x] = jnp.zeros(be.shape[1:], F32)
+        exts[0][x] = jnp.zeros(exts[0].shape[1:], F32)
+
+
+def assemble0(args, exts):
+    for a, x, own, tiles, _ in blocks0(*args):
+        ext = exts[a]
+        r = 4 + x
+        ext[r, 4:36, :] = own
+        for h in range(2):
+            cut = pl.ds(128 * h, 128)
+            ext[r, 0:4, cut] = tiles[0][h][4:8, :]
+            ext[r, 36:40, cut] = tiles[1][h][0:4, :]
+    for x in (0, 15):
+        exts[0][x] = jnp.zeros(exts[0].shape[1:], F32)
 
 
 def k_descend0(
@@ -290,61 +334,38 @@
     v0, g1, low, high,
     be, ce, ge, wx, wy, wz, wl, rd, va, vb, tmp,
 ):
-    assemble0(b0, c0, g0, below, above, left, right, under, over, be, ce, ge)
+    assemble_deep((b0, c0, g0, below, above, left, right, under, over), (be, ce, ge))
     s = (wx, wy, wz, wl, rd, ce, ge)
     weights(be, s, va, 1.0, 1, 15, 7)
     sweep(va, vb, s, 2, 14, 6)
     sweep(vb, va, s, 3, 13, 5)
     for x in range(8):
-        v0[x] = va[4 + x, 4:36, :]
+        v0[x] = va[4 + x, 8:48, :]
     kept = None
     for x, here, res in residual_rows(va, s, 4, 12):
         if x % 2 == 0:
             kept = res
         else:
-            split_pair(tmp, (x - 4) // 2, (kept + res)[4:36, :])
+            split_pair(tmp, (x - 4) // 2, (kept + res)[4:52, :])
     t = fold_level0(tmp)
     for x in range(4):
-        g1[x] = t[16 * x : 16 * x + 16]
+        g1[x] = t[x]
         low[x] = gate(place("gx") > 0, b1[x])
         high[x] = gate(place("gx") < lax.axis_size("gx") - 1, b1[x])
     for k in range(3):
         low[4 + k] = c1[k]
         high[4 + k] = c1[1 + k]
-        low[7 + k] = t[16 * k : 16 * k + 16]
-        high[7 + k] = t[16 * k + 16 : 16 * k + 32]
-
-
-def k_pack_y1(g1, b1, c1, v0, below, above, low, high):
-    for out, at, inside in ((low, 0, place("gy") > 0), (high, 12, place("gy") < lax.axis_size("gy") - 1)):
-        cut = pl.ds(at, 4)
-        t = 0
-        for own, base, reach in ((b1, 0, 4), (c1, 4, 3), (g1, 7, 3)):
-            for x in range(-reach, 4 + reach):
-                if x < 0:
-                    val = below[base + x + reach, cut, :]
-                elif x < 4:
-                    val = own[x, cut, :]
-                else:
-                    val = above[base + x - 4, cut, :]
-                half = 4 * (t % 2)
-                out[t // 2, half : half + 4, :] = gate(inside, val) if base == 0 else val
-                t += 1
-        for x in range(8):
-            strip_tiles(out, 16 + x, v0[x, pl.ds(0 if at == 0 else 28, 4), :])
+        low[7 + k] = t[k]
+        high[7 + k] = t[1 + k]
 
 
 def k_descend1(
-    g1, b1, c1, bc2, below, above, left, right,
+    g1, b1, c1, bc2, below, above,
     v1, pay, be, ce, ge,
     wx, wy, wz, wl, rd, va, vb, tmp,
 ):
-    zeros = jnp.zeros((8, 128), F32)
-    t = 0
+    zeros = jnp.zeros((4, 128), F32)
     for ext, own, base, reach in ((be, b1, 0, 4), (ce, c1, 4, 3), (ge, g1, 7, 3)):
-        for x in range(12):
-            ext[x, 0:8, :] = zeros
-            ext[x, 24:32, :] = zeros
         for x in range(-reach, 4 + reach):
             if x < 0:
                 val = below[base + x + reach]
@@ -352,11 +373,9 @@
                 val = own[x]
             else:
                 val = above[base + x - 4]
-            ext[4 + x, 8:24, :] = val
-            half = 4 * (t % 2)
-            ext[4 + x, 4:8, :] = left[t // 2, half : half + 4, :]
-            ext[4 + x, 24:28, :] = right[t // 2, half : half + 4, :]
-            t += 1
+            ext[4 + x, 0:4, :] = zeros
+            ext[4 + x, 4:28, :] = val
+            ext[4 + x, 28:32, :] = zeros
 
     s = (wx, wy, wz, wl, rd, ce, ge)
     weights(be, s, va, 0.25, 1, 11, 10)
@@ -377,20 +396,17 @@
         pay[k, 2] = bc2[1]
 
 
-def k_pack_v(v0, v1, left, right, low, high):
-    for out, first, edge in ((low, 0, 0), (high, 5, 6)):
+def k_pack_v(v0, v1, low, high):
+    for out, first in ((low, 0), (high, 5)):
         for k in range(3):
-            for q in range(4):
+            for q in range(5):
                 for h in range(2):
-                    out[8 * k + 2 * q + h] = v0[
+                    out[10 * k + 2 * q + h] = v0[
                         first + k, 8 * q : 8 * q + 8, 128 * h : 128 * h + 128
                     ]
-        for k in range(2):
-            out[24 + k] = left[16 + edge + k]
-            out[26 + k] = right[16 + edge + k]
         for k in range(4):
             for q in range(2):
-                out[28 + 2 * k + q] = v1[k, 8 * q : 8 * q + 8, :]
+                out[30 + 2 * k + q] = v1[k, 8 * q : 8 * q + 8, :]
 
 
 def k_pack_y2(v1, below, above, gathered, low, high):
@@ -404,11 +420,11 @@
         cut = pl.ds(4 * q, 4)
         for t, x in enumerate(range(-4, 8)):
             if x < 0:
-                val = below[28 + 2 * (x + 4) + q, cut, :]
+                val = below[30 + 2 * (x + 4) + q, cut, :]
             elif x < 4:
                 val = v1[x, pl.ds(12 * q, 4), :]
             else:
-                val = above[28 + 2 * (x - 4) + q, cut, :]
+                val = above[30 + 2 * (x - 4) + q, cut, :]
             half = 4 * (t % 2)
             out[24 + t // 2, half : half + 4, :] = val
 
@@ -546,11 +562,11 @@
 
 def k_prepare(
     b0, c0, g0, below0, above0, left0, right0, under0, over0, be1, ce1, ge1,
-    v0, v1, left, right, below, above, left1, right1,
+    v0, v1, below, above, left1, right1,
     p0, ce, ge, wx, wy, wz, wl, rd, p1, wx1, wy1, wz1, wl1, rd1,
     be, va, va1,
 ):
-    assemble0(b0, c0, g0, below0, above0, left0, right0, under0, over0, be, ce, ge)
+    assemble0((b0, c0, g0, below0, above0, left0, right0, under0, over0), (be, ce, ge))
     weights(be, (wx, wy, wz, wl, rd, ce, ge), va, 1.0, 2, 14, 6)
     weights(be1, (wx1, wy1, wz1, wl1, rd1, ce1, ge1), va1, 0.25, 1, 11, 10)
     zero = jnp.zeros((8, 128), F32)
@@ -562,25 +578,20 @@
         else:
             src, k = (below, x + 4) if x < 0 else (above, x - 4)
             for q in range(2):
-                p1[t, 8 + 8 * q : 16 + 8 * q, :] = src[28 + 2 * k + q]
+                p1[t, 8 + 8 * q : 16 + 8 * q, :] = src[30 + 2 * k + q]
         half = 4 * (t % 2)
         p1[t, 4:8, :] = left1[24 + t // 2, half : half + 4, :]
         p1[t, 24:28, :] = right1[24 + t // 2, half : half + 4, :]
     for x in range(-3, 11):
         if 0 <= x < 8:
-            p0[4 + x, 4:36, :] = v0[x]
-            strips = left[16 + x], right[16 + x]
+            p0[4 + x] = v0[x]
         else:
             src, k = (below, x + 3) if x < 0 else (above, x - 8)
-            for q in range(4):
+            for q in range(5):
                 for h in range(2):
-                    p0[4 + x, 4 + 8 * q : 12 + 8 * q, 128 * h : 128 * h + 128] = (
-                        src[8 * k + 2 * q + h]
+                    p0[4 + x, 8 * q : 8 * q + 8, 128 * h : 128 * h + 128] = (
+                        src[10 * k + 2 * q + h]
                     )
-            e = x + 2 if x < 0 else x - 8
-            strips = (src[24 + e], src[26 + e]) if 0 <= e < 2 else (zero, zero)
-        put_strip0(p0, 4 + x, strips[0], False)
-        put_strip0(p0, 4 + x, strips[1], True)
 
 
 def k_ascend(
@@ -708,39 +719,34 @@
         pltpu.with_memory_space_constraint(a, pltpu.HBM) for a in (source, material, flags)
     )
     left, right, b0, c0, g0 = call(
-        k_load0, "load0", [(24, 8, 128)] * 2 + [B0] * 3,
+        k_load0, "load0", [(STRIPS, 8, 128)] * 2 + [B0] * 3,
         [pltpu.VMEM(B0, jnp.int32), pltpu.VMEM(B0, jnp.int32), pltpu.SemaphoreType.DMA((3,))],
         4, material, flags, source, anywhere=(0, 1, 2),
     )
     left0, right0 = exchange(left, right, "gy")
     low, high = call(k_edge0, "edge0", [(9, 32, 256)] * 2, [], 4, b0, c0, g0)
     below0, above0 = exchange(low, high, "gx")
-    low, high = call(k_corner0, "corner0", [(14, 8, 128)] * 2, [], 4, left0, right0)
+    low, high = call(k_corner0, "corner0", [(CORNERS, 8, 128)] * 2, [], 4, left0, right0)
     under0, over0 = exchange(low, high, "gx")
     b1, c1, bc2 = call(
-        k_coefs, "coefs", [(4, 16, 128), (4, 16, 128), (2, 8, 128)],
-        [(4, 2, 32, 128), (2, 16, 128)], 4, b0, c0,
-    )
-    blocks0 = (b0, c0, g0, below0, above0, left0, right0, under0, over0)
+        k_coefs, "coefs", [(4, 24, 128), (4, 24, 128), (2, 8, 128)],
+        [(4, 2, 48, 128), (2, 16, 128)], 4, b0, c0, left0, right0,
+    )
+    own0 = (b0, c0, g0, below0, above0, left0, right0, under0, over0)
     v0, g1, low, high = call(
         k_descend0, "descend0",
-        [B0, (4, 16, 128), (10, 16, 128), (10, 16, 128)],
-        [E0] * 10 + [(4, 2, 32, 128)], 12,
-        *blocks0, b1, c1,
+        [(8, 40, 256), (4, 24, 128), (10, 24, 128), (10, 24, 128)],
+        [(16, 56, 256)] * 10 + [(4, 2, 48, 128)], 16, *own0, b1, c1,
     )
     below, above = exchange(low, high, "gx")
-    low, high = call(
-        k_pack_y1, "pack_y1", [(24, 8, 128)] * 2, [], 4, g1, b1, c1, v0, below, above
-    )
-    left, right = exchange(low, high, "gy")
     v1, pay, be1, ce1, ge1 = call(
         k_descend1, "descend1",
         [(4, 16, 128), (8, 3, 8, 128)] + [E1] * 3,
         [E1] * 7 + [(2, 16, 128)], 4,
-        g1, b1, c1, bc2, below, above, left, right,
+        g1, b1, c1, bc2, below, above,
     )
     gathered = lax.all_to_all(pay, "gx", 0, 0)
-    low, high = call(k_pack_v, "pack_v", [(36, 8, 128)] * 2, [], 4, v0, v1, left, right)
+    low, high = call(k_pack_v, "pack_v", [(38, 8, 128)] * 2, [], 4, v0, v1)
     below, above = exchange(low, high, "gx")
     low, high = call(
         k_pack_y2, "pack_y2", [(30, 8, 128)] * 2, [], 4, v1, below, above, gathered
@@ -753,7 +759,7 @@
     r0, r1 = swap_chips(own3, "gy", 0), swap_chips(own3, "gy", 1)
     p0, ce0, ge0, wx0, wy0, wz0, wl0, rd0, p1, *w1 = call(
         k_prepare, "prepare", [E0] * 8 + [E1] * 6, [E0, E0, E1], 8,
-        *blocks0, be1, ce1, ge1, v0, v1, left, right, below, above, left1, right1,
+        *own0, be1, ce1, ge1, v0, v1, below, above, left1, right1,
     )
     pressure, residual = call(
         k_ascend, "ascend", [B0] * 2,

time: 70.4 us -> 64.5 us (0.916)
  starting transfers between devices: 36.8 us -> 31.4 us
  waiting for transfers between devices: 21.1 us -> 19.4 us
  Pallas kernels: 11.4 us -> 12.6 us
    ppermute x2, starting transfers between devices: 8.97 us -> 5.41 us  [swap_chips(): return lax.ppermute(block, axis, pairs + [(b, a) for a, b in pairs])]
    ppermute x14 -> x12, waiting for transfers between devices: 18.3 us -> 15.7 us  [shift(): lax.ppermute(block, axis, [(i, (i + step) % count) for i in range(count)])]
    ppermute x14 -> x12, starting transfers between devices: 21.7 us -> 19.9 us  [shift(): lax.ppermute(block, axis, [(i, (i + step) % count) for i in range(count)])]
    pallas_call x12 -> x11, Pallas kernels: 11.4 us -> 12.6 us  [call(): pl.pallas_call(kernel, name=name, out_shape=[jax.ShapeDtypeStruct(s, F32)...]
    all_to_all x1, waiting for transfers between devices: 0.01 us -> 0.92 us  [per_device(): gathered = lax.all_to_all(pay, 'gx', 0, 0)]
  transfers between devices with their start and end apart: 17 -> 15, of which waited for: 8 -> 8; matrix products, arithmetic and copies ran while one was open for 0% -> 0% of each run, Pallas kernels for 2% -> 3%
where the time goes in v5:
time: 64.5 us; the launch traced here: 64.3 us
  starting transfers between devices  31.4 us (49%)
  waiting for transfers between devices  19.4 us (30%)
  Pallas kernels  12.6 us (20%)
  between operations  0.88 us (1%)
    ppermute x12, starting transfers between devices, shift(): lax.ppermute(block, axis, [(i, (i + step) % count) for i in range(count)])  19.9 us
    ppermute x12, waiting for transfers between devices, shift(): lax.ppermute(block, axis, [(i, (i + step) % count) for i in range(count)])  15.7 us
    pallas_call x11, Pallas kernels, call(): pl.pallas_call(kernel, name=name, out_shape=[jax.ShapeDtypeStruct(s, F32)...  12.6 us
    all_to_all x1, starting transfers between devices, per_device(): gathered = lax.all_to_all(pay, 'gx', 0, 0)  6.12 us
    ppermute x2, starting transfers between devices, swap_chips(): return lax.ppermute(block, axis, pairs + [(b, a) for a, b in pairs])  5.41 us
    ppermute x2, waiting for transfers between devices, swap_chips(): return lax.ppermute(block, axis, pairs + [(b, a) for a, b in pairs])  2.74 us
  transfers between devices with their start and end apart: 15, of which 8 were waited for; matrix products, arithmetic and copies ran while one was open for 0% of the time, Pallas kernels for 3%

profile of v5, /device:TPU:2, one launch (start us, length us, event | category | flops | bytes accessed | tf_op | source)
XLA Modules:
  0.0 64.3 jit_solution(9813274504706148360)
XLA Ops:
  0.6 1.2 %load0.1 = (f32[54,8,128]{2,1,0:T(8,128)S(1)}, f32[54,8,128]{2,1,0:T(8,128)S(1)}, f32[8,32,256]{2,1,0:T(8,128)S(1)}, f32[8,32,256]{2,1,0:T(8,128)S(1)}, f32[8,32,256]{2,1,0:T(8,128)S(1)}) custom-call(s32[8,32,256]{2,1,0:T(8,128)} %m.1, s32[8,32,256]{2,1,0:T(8,128)} %f.1, f32[8,32,256]{2,1,0:T(8,128)} %g.1), custom_call_target="tpu_custom_call" | custom-call | tf_op jit(solution)/shard_map/load0/pallas_call | solution.py:700
  1.9 1.7 %collective-permute-start.3 = (f32[54,8,128]{2,1,0:T(8,128)S(1)}, f32[54,8,128]{2,1,0:T(8,128)S(1)}, u32[]{:S(2)}, u32[]{:S(2)}) collective-permute-start(f32[54,8,128]{2,1,0:T(8,128)S(1)} %get-tuple-element.55), channel_id=1, source_target_pairs={{0,31},{1,0},{2,1},{3,2},{4,3},{5,4},{6,5},{7,6},{8,7},{9,8},{10,9... | collective-permute-start | bytes 663560 | tf_op jit(solution)/shard_map/ppermute | solution.py:20
  3.7 2.0 %collective-permute-start = (f32[9,32,256]{2,1,0:T(8,128)S(1)}, f32[9,32,256]{2,1,0:T(8,128)S(1)}, u32[]{:S(2)}, u32[]{:S(2)}) collective-permute-start(f32[9,32,256]{2,1,0:T(8,128)S(1)} %get-tuple-element.52), channel_id=1, source_target_pairs={{0,32},{32,64},{64,96},{96,128},{128,160},{160,192},{192,224},{224... | collective-permute-start | bytes 884744 | tf_op jit(solution)/shard_map/ppermute | solution.py:20
  5.7 4.0 %collective-permute-start.1 = (f32[9,32,256]{2,1,0:T(8,128)S(1)}, f32[9,32,256]{2,1,0:T(8,128)S(1)}, u32[]{:S(2)}, u32[]{:S(2)}) collective-permute-start(f32[9,32,256]{2,1,0:T(8,128)S(1)} %get-tuple-element.53), channel_id=1, source_target_pairs={{0,224},{32,0},{64,32},{96,64},{128,96},{160,128},{192,160},{224,1... | collective-permute-start | bytes 884744 | tf_op jit(solution)/shard_map/ppermute | solution.py:20
  9.8 3.5 %collective-permute-start.5 = (f32[37,8,128]{2,1,0:T(8,128)S(1)}, f32[37,8,128]{2,1,0:T(8,128)S(1)}, u32[]{:S(2)}, u32[]{:S(2)}) collective-permute-start(f32[37,8,128]{2,1,0:T(8,128)S(1)} %get-tuple-element.57), channel_id=1, source_target_pairs={{0,224},{32,0},{64,32},{96,64},{128,96},{160,128},{192,160},{224,1... | collective-permute-start | bytes 454664 | tf_op jit(solution)/shard_map/ppermute | solution.py:20
  13.9 3.4 %collective-permute-done.below.below0 = f32[9,32,256]{2,1,0:T(8,128)S(1)} collective-permute-done((f32[9,32,256]{2,1,0:T(8,128)S(1)}, f32[9,32,256]{2,1,0:T(8,128)S(1)}, u32[]{:S(2)}, u32[]{:S(2)}) %collective-permute-start) | collective-permute-done | bytes 294944 | tf_op jit(solution)/shard_map/ppermute | solution.py:20
  17.3 2.6 %collective-permute-done.4.under.under0 = f32[37,8,128]{2,1,0:T(8,128)S(1)} collective-permute-done((f32[37,8,128]{2,1,0:T(8,128)S(1)}, f32[37,8,128]{2,1,0:T(8,128)S(1)}, u32[]{:S(2)}, u32[]{:S(2)}) %collective-permute-start.4) | collective-permute-done | bytes 151584 | tf_op jit(solution)/shard_map/ppermute | solution.py:20
  19.9 3.2 %descend0.1 = (f32[8,40,256]{2,1,0:T(8,128)S(1)}, f32[4,24,128]{2,1,0:T(8,128)S(1)}, f32[10,24,128]{2,1,0:T(8,128)S(1)}, f32[10,24,128]{2,1,0:T(8,128)S(1)}) custom-call(f32[8,32,256]{2,1,0:T(8,128)S(1)} %get-tuple-element.49.b0, f32[8,32,256]{2,1,0:T(8,128)S(1)} %get-tuple-element.50.c0, f32[8,32,256]{2,1,0:T(8,128)S(1)} %get-tuple-element.51.g0, ...), custom_call_target="tpu_custom_call" | custom-call | tf_op jit(solution)/shard_map/descend0/pallas_call | solution.py:700
  23.2 3.2 %collective-permute-start.7 = (f32[10,24,128]{2,1,0:T(8,128)S(1)}, f32[10,24,128]{2,1,0:T(8,128)S(1)}, u32[]{:S(2)}, u32[]{:S(2)}) collective-permute-start(f32[10,24,128]{2,1,0:T(8,128)S(1)} %get-tuple-element.63), channel_id=1, source_target_pairs={{0,224},{32,0},{64,32},{96,64},{128,96},{160,128},{192,160},{224,1... | collective-permute-start | bytes 368648 | tf_op jit(solution)/shard_map/ppermute | solution.py:20
  26.4 2.9 %collective-permute-done.6.below = f32[10,24,128]{2,1,0:T(8,128)S(1)} collective-permute-done((f32[10,24,128]{2,1,0:T(8,128)S(1)}, f32[10,24,128]{2,1,0:T(8,128)S(1)}, u32[]{:S(2)}, u32[]{:S(2)}) %collective-permute-start.6) | collective-permute-done | bytes 122912 | tf_op jit(solution)/shard_map/ppermute | solution.py:20
  29.3 1.3 %descend1.1 = (f32[4,16,128]{2,1,0:T(8,128)S(1)}, f32[8,3,8,128]{3,2,1,0:T(8,128)}, f32[12,32,128]{2,1,0:T(8,128)S(1)}, f32[12,32,128]{2,1,0:T(8,128)S(1)}, f32[12,32,128]{2,1,0:T(8,128)S(1)}) custom-call(f32[4,24,128]{2,1,0:T(8,128)S(1)} %get-tuple-element.60.g1, f32[4,24,128]{2,1,0:T(8,128)S(1)} %get-tuple-element.58.b1, ...), custom_call_target="tpu_custom_call" | custom-call | tf_op jit(solution)/shard_map/descend1/pallas_call | solution.py:700
  30.6 6.1 %all-to-all-start = ((f32[8,3,8,128]{3,2,1,0:T(8,128)}), f32[8,3,8,128]{3,2,1,0:T(8,128)S(1)}, u32[]{:S(2)}, u32[]{:S(2)}) async-start(f32[8,3,8,128]{3,2,1,0:T(8,128)} %get-tuple-element.64), calls=%async_computation | async-start | bytes 196608 | tf_op jit(solution)/shard_map/all_to_all | solution.py:748
  36.7 2.1 %collective-permute-start.8 = (f32[38,8,128]{2,1,0:T(8,128)S(1)}, f32[38,8,128]{2,1,0:T(8,128)S(1)}, u32[]{:S(2)}, u32[]{:S(2)}) collective-permute-start(f32[38,8,128]{2,1,0:T(8,128)S(1)} %get-tuple-element.67), channel_id=1, source_target_pairs={{0,32},{32,64},{64,96},{96,128},{128,160},{160,192},{192,224},{224... | collective-permute-start | bytes 466952 | tf_op jit(solution)/shard_map/ppermute | solution.py:20
  38.8 1.3 %collective-permute-start.9 = (f32[38,8,128]{2,1,0:T(8,128)S(1)}, f32[38,8,128]{2,1,0:T(8,128)S(1)}, u32[]{:S(2)}, u32[]{:S(2)}) collective-permute-start(f32[38,8,128]{2,1,0:T(8,128)S(1)} %get-tuple-element.68), channel_id=1, source_target_pairs={{0,224},{32,0},{64,32},{96,64},{128,96},{160,128},{192,160},{224,1... | collective-permute-start | bytes 466952 | tf_op jit(solution)/shard_map/ppermute | solution.py:20
  40.1 4.3 %collective-permute-done.8.below = f32[38,8,128]{2,1,0:T(8,128)S(1)} collective-permute-done((f32[38,8,128]{2,1,0:T(8,128)S(1)}, f32[38,8,128]{2,1,0:T(8,128)S(1)}, u32[]{:S(2)}, u32[]{:S(2)}) %collective-permute-start.8) | collective-permute-done | bytes 155680 | tf_op jit(solution)/shard_map/ppermute | solution.py:20
  44.4 0.9 %all-to-all-done.gathered = f32[8,3,8,128]{3,2,1,0:T(8,128)S(1)} async-done(((f32[8,3,8,128]{3,2,1,0:T(8,128)}), f32[8,3,8,128]{3,2,1,0:T(8,128)S(1)}, u32[]{:S(2)}, u32[]{:S(2)}) %all-to-all-start) | async-done | bytes 98336 | tf_op jit(solution)/shard_map/all_to_all | solution.py:748
  45.4 1.7 %collective-permute-start.11 = (f32[30,8,128]{2,1,0:T(8,128)S(1)}, f32[30,8,128]{2,1,0:T(8,128)S(1)}, u32[]{:S(2)}, u32[]{:S(2)}) collective-permute-start(f32[30,8,128]{2,1,0:T(8,128)S(1)} %get-tuple-element.70), channel_id=1, source_target_pairs={{0,31},{1,0},{2,1},{3,2},{4,3},{5,4},{6,5},{7,6},{8,7},{9,8},{10,9... | collective-permute-start | bytes 368648 | tf_op jit(solution)/shard_map/ppermute | solution.py:20
  47.2 2.6 %collective-permute-done.10.left.left1 = f32[30,8,128]{2,1,0:T(8,128)S(1)} collective-permute-done((f32[30,8,128]{2,1,0:T(8,128)S(1)}, f32[30,8,128]{2,1,0:T(8,128)S(1)}, u32[]{:S(2)}, u32[]{:S(2)}) %collective-permute-start.10) | collective-permute-done | bytes 122912 | tf_op jit(solution)/shard_map/ppermute | solution.py:20
  49.7 1.0 %descend2.1 = (f32[8,24,128]{2,1,0:T(8,128)S(1)}, f32[6,8,128]{2,1,0:T(8,128)S(1)}, f32[8,24,128]{2,1,0:T(8,128)S(1)}, f32[8,24,128]{2,1,0:T(8,128)S(1)}, f32[8,...) custom-call(f32[8,3,8,128]{3,2,1,0:T(8,128)S(1)} %all-to-all-done.gather, ...), custom_call_target="tpu_custom_call" | custom-call | tf_op jit(solution)/shard_map/descend2/pallas_call | solution.py:700
  50.7 5.4 %collective-permute-start.12 = (f32[6,8,128]{2,1,0:T(8,128)S(1)}, f32[6,8,128]{2,1,0:T(8,128)S(1)}, u32[]{:S(2)}, u32[]{:S(2)}) collective-permute-start(f32[6,8,128]{2,1,0:T(8,128)S(1)} %get-tuple-element.71.own3), channel_id=1, source_target_pairs={{0,2},{1,3},{4,6},{5,7},{8,10},{9,11},{12,14},{13,15},{16,18},{17,... | collective-permute-start | bytes 73736 | tf_op jit(solution)/shard_map/ppermute | solution.py:32
  56.1 1.1 %prepare.1 = (f32[16,40,256]{2,1,0:T(8,128)S(1)}, f32[16,40,256]{2,1,0:T(8,128)S(1)}, f32[16,40,256]{2,1,0:T(8,128)S(1)}, f32[16,40,256]{2,1,0:T(8,128)S(1)}, f3...) custom-call(f32[8,32,256]{2,1,0:T(8,128)S(1)} %get-tuple-element.49., ...), custom_call_target="tpu_custom_call" | custom-call | tf_op jit(solution)/shard_map/prepare/pallas_call | solution.py:700
  57.2 0.7 %collective-permute-done.12.r0 = f32[6,8,128]{2,1,0:T(8,128)S(1)} collective-permute-done((f32[6,8,128]{2,1,0:T(8,128)S(1)}, f32[6,8,128]{2,1,0:T(8,128)S(1)}, u32[]{:S(2)}, u32[]{:S(2)}) %collective-permute-start.12) | collective-permute-done | bytes 24608 | tf_op jit(solution)/shard_map/ppermute | solution.py:32
  57.9 2.0 %collective-permute-done.13.r1 = f32[6,8,128]{2,1,0:T(8,128)S(1)} collective-permute-done((f32[6,8,128]{2,1,0:T(8,128)S(1)}, f32[6,8,128]{2,1,0:T(8,128)S(1)}, u32[]{:S(2)}, u32[]{:S(2)}) %collective-permute-start.13) | collective-permute-done | bytes 24608 | tf_op jit(solution)/shard_map/ppermute | solution.py:32
  60.0 4.1 %ascend.1 = (f32[8,32,256]{2,1,0:T(8,128)}, f32[8,32,256]{2,1,0:T(8,128)}) custom-call(f32[6,8,128]{2,1,0:T(8,128)S(1)} %get-tuple-element.71.own3, f32[6,8,128]{2,1,0:T(8,128)S(1)} %collective-permute-done.12.r0, f32[6,8,128]{2,1,0:T(8,128)S(1)} %collective-permute-done.13.r1, f32[8,24,128]{2,1,0:T(8,128)S(1)} %get-tuple-element.72.v2, ...), custom_call_target="tpu_custom_call" | custom-call | tf_op jit(solution)/shard_map/ascend/pallas_call | solution.py:700
  (17 shorter events, 1.1 us)
Async XLA Ops:
  1.8 7.9 %collective-permute-start.2 = (f32[54,8,128]{2,1,0:T(8,128)S(1)}, f32[54,8,128]{2,1,0:T(8,128)S(1)}, u32[]{:S(2)}, u32[]{:S(2)}) collective-permute-start(f32[54,8,128]{2,1,0:T(8,128)S(1)} %get-tuple-element.54), channel_id=1, source_target_pairs={{0,1},{1,2},{2,3},{3,4},{4,5},{5,6},{6,7},{7,8},{8,9},{9,10},{10,1... | collective-permute-start | bytes 663560 | tf_op jit(solution)/shard_map/ppermute | solution.py:20
  1.9 7.8 %collective-permute-start.3 = (f32[54,8,128]{2,1,0:T(8,128)S(1)}, f32[54,8,128]{2,1,0:T(8,128)S(1)}, u32[]{:S(2)}, u32[]{:S(2)}) collective-permute-start(f32[54,8,128]{2,1,0:T(8,128)S(1)} %get-tuple-element.55), channel_id=1, source_target_pairs={{0,31},{1,0},{2,1},{3,2},{4,3},{5,4},{6,5},{7,6},{8,7},{9,8},{10,9... | collective-permute-start | bytes 663560 | tf_op jit(solution)/shard_map/ppermute | solution.py:20
  3.7 13.6 %collective-permute-start = (f32[9,32,256]{2,1,0:T(8,128)S(1)}, f32[9,32,256]{2,1,0:T(8,128)S(1)}, u32[]{:S(2)}, u32[]{:S(2)}) collective-permute-start(f32[9,32,256]{2,1,0:T(8,128)S(1)} %get-tuple-element.52), channel_id=1, source_target_pairs={{0,32},{32,64},{64,96},{96,128},{128,160},{160,192},{192,224},{224... | collective-permute-start | bytes 884744 | tf_op jit(solution)/shard_map/ppermute | solution.py:20
  5.7 11.6 %collective-permute-start.1 = (f32[9,32,256]{2,1,0:T(8,128)S(1)}, f32[9,32,256]{2,1,0:T(8,128)S(1)}, u32[]{:S(2)}, u32[]{:S(2)}) collective-permute-start(f32[9,32,256]{2,1,0:T(8,128)S(1)} %get-tuple-element.53), channel_id=1, source_target_pairs={{0,224},{32,0},{64,32},{96,64},{128,96},{160,128},{192,160},{224,1... | collective-permute-start | bytes 884744 | tf_op jit(solution)/shard_map/ppermute | solution.py:20
  9.7 10.2 %collective-permute-start.4 = (f32[37,8,128]{2,1,0:T(8,128)S(1)}, f32[37,8,128]{2,1,0:T(8,128)S(1)}, u32[]{:S(2)}, u32[]{:S(2)}) collective-permute-start(f32[37,8,128]{2,1,0:T(8,128)S(1)} %get-tuple-element.56), channel_id=1, source_target_pairs={{0,32},{32,64},{64,96},{96,128},{128,160},{160,192},{192,224},{224... | collective-permute-start | bytes 454664 | tf_op jit(solution)/shard_map/ppermute | solution.py:20
  9.8 10.1 %collective-permute-start.5 = (f32[37,8,128]{2,1,0:T(8,128)S(1)}, f32[37,8,128]{2,1,0:T(8,128)S(1)}, u32[]{:S(2)}, u32[]{:S(2)}) collective-permute-start(f32[37,8,128]{2,1,0:T(8,128)S(1)} %get-tuple-element.57), channel_id=1, source_target_pairs={{0,224},{32,0},{64,32},{96,64},{128,96},{160,128},{192,160},{224,1... | collective-permute-start | bytes 454664 | tf_op jit(solution)/shard_map/ppermute | solution.py:20
  23.1 6.2 %collective-permute-start.6 = (f32[10,24,128]{2,1,0:T(8,128)S(1)}, f32[10,24,128]{2,1,0:T(8,128)S(1)}, u32[]{:S(2)}, u32[]{:S(2)}) collective-permute-start(f32[10,24,128]{2,1,0:T(8,128)S(1)} %get-tuple-element.62), channel_id=1, source_target_pairs={{0,32},{32,64},{64,96},{96,128},{128,160},{160,192},{192,224},{224... | collective-permute-start | bytes 368648 | tf_op jit(solution)/shard_map/ppermute | solution.py:20
  23.2 6.1 %collective-permute-start.7 = (f32[10,24,128]{2,1,0:T(8,128)S(1)}, f32[10,24,128]{2,1,0:T(8,128)S(1)}, u32[]{:S(2)}, u32[]{:S(2)}) collective-permute-start(f32[10,24,128]{2,1,0:T(8,128)S(1)} %get-tuple-element.63), channel_id=1, source_target_pairs={{0,224},{32,0},{64,32},{96,64},{128,96},{160,128},{192,160},{224,1... | collective-permute-start | bytes 368648 | tf_op jit(solution)/shard_map/ppermute | solution.py:20
  30.6 14.8 %all-to-all-start = ((f32[8,3,8,128]{3,2,1,0:T(8,128)}), f32[8,3,8,128]{3,2,1,0:T(8,128)S(1)}, u32[]{:S(2)}, u32[]{:S(2)}) async-start(f32[8,3,8,128]{3,2,1,0:T(8,128)} %get-tuple-element.64), calls=%async_computation | async-start | bytes 196608 | tf_op jit(solution)/shard_map/all_to_all | solution.py:748
  36.7 7.7 %collective-permute-start.8 = (f32[38,8,128]{2,1,0:T(8,128)S(1)}, f32[38,8,128]{2,1,0:T(8,128)S(1)}, u32[]{:S(2)}, u32[]{:S(2)}) collective-permute-start(f32[38,8,128]{2,1,0:T(8,128)S(1)} %get-tuple-element.67), channel_id=1, source_target_pairs={{0,32},{32,64},{64,96},{96,128},{128,160},{160,192},{192,224},{224... | collective-permute-start | bytes 466952 | tf_op jit(solution)/shard_map/ppermute | solution.py:20
  38.8 5.6 %collective-permute-start.9 = (f32[38,8,128]{2,1,0:T(8,128)S(1)}, f32[38,8,128]{2,1,0:T(8,128)S(1)}, u32[]{:S(2)}, u32[]{:S(2)}) collective-permute-start(f32[38,8,128]{2,1,0:T(8,128)S(1)} %get-tuple-element.68), channel_id=1, source_target_pairs={{0,224},{32,0},{64,32},{96,64},{128,96},{160,128},{192,160},{224,1... | collective-permute-start | bytes 466952 | tf_op jit(solution)/shard_map/ppermute | solution.py:20
  45.3 4.4 %collective-permute-start.10 = (f32[30,8,128]{2,1,0:T(8,128)S(1)}, f32[30,8,128]{2,1,0:T(8,128)S(1)}, u32[]{:S(2)}, u32[]{:S(2)}) collective-permute-start(f32[30,8,128]{2,1,0:T(8,128)S(1)} %get-tuple-element.69), channel_id=1, source_target_pairs={{0,1},{1,2},{2,3},{3,4},{4,5},{5,6},{6,7},{7,8},{8,9},{9,10},{10,1... | collective-permute-start | bytes 368648 | tf_op jit(solution)/shard_map/ppermute | solution.py:20
  45.4 4.3 %collective-permute-start.11 = (f32[30,8,128]{2,1,0:T(8,128)S(1)}, f32[30,8,128]{2,1,0:T(8,128)S(1)}, u32[]{:S(2)}, u32[]{:S(2)}) collective-permute-start(f32[30,8,128]{2,1,0:T(8,128)S(1)} %get-tuple-element.70), channel_id=1, source_target_pairs={{0,31},{1,0},{2,1},{3,2},{4,3},{5,4},{6,5},{7,6},{8,7},{9,8},{10,9... | collective-permute-start | bytes 368648 | tf_op jit(solution)/shard_map/ppermute | solution.py:20
  50.7 7.2 %collective-permute-start.12 = (f32[6,8,128]{2,1,0:T(8,128)S(1)}, f32[6,8,128]{2,1,0:T(8,128)S(1)}, u32[]{:S(2)}, u32[]{:S(2)}) collective-permute-start(f32[6,8,128]{2,1,0:T(8,128)S(1)} %get-tuple-element.71.own3), channel_id=1, source_target_pairs={{0,2},{1,3},{4,6},{5,7},{8,10},{9,11},{12,14},{13,15},{16,18},{17,... | collective-permute-start | bytes 73736 | tf_op jit(solution)/shard_map/ppermute | solution.py:32
  56.1 3.8 %collective-permute-start.13 = (f32[6,8,128]{2,1,0:T(8,128)S(1)}, f32[6,8,128]{2,1,0:T(8,128)S(1)}, u32[]{:S(2)}, u32[]{:S(2)}) collective-permute-start(f32[6,8,128]{2,1,0:T(8,128)S(1)} %get-tuple-element.71.own3), channel_id=1, source_target_pairs={{0,1},{2,4},{3,5},{6,8},{7,9},{10,12},{11,13},{14,16},{15,17},{18,... | collective-permute-start | bytes 73736 | tf_op jit(solution)/shard_map/ppermute | solution.py:32

commit v6 on v5

--- a/solution.py
+++ b/solution.py
@@ -38,14 +38,14 @@
 
 def pick(a, w):
     count = a.shape[0]
-    a1 = a.astype(BF16)
-    rest = a - a1.astype(F32)
-    a2 = rest.astype(BF16)
-    a3 = (rest - a2.astype(F32)).astype(BF16)
-    out = jnp.dot(
-        jnp.concatenate([a1, a2, a3], axis=0), w.astype(BF16), preferred_element_type=F32
-    )
-    return out[:count] + out[count : 2 * count] + out[2 * count :]
+    a1 = a.astype(BF16).astype(F32)
+    a2 = (a - a1).astype(BF16).astype(F32)
+    parts = [a1, a2, (a - a1) - a2]
+    if 3 * count % 16:
+        parts.append(jnp.zeros((16 - 3 * count % 16, a.shape[1]), F32))
+    stacked = jnp.concatenate(parts, axis=0).astype(BF16)
+    out = jnp.dot(stacked, w.astype(BF16), preferred_element_type=F32)
+    return out[:count] + out[count : 2 * count] + out[2 * count : 3 * count]
 
 
 def inverse_density(material):
@@ -337,8 +337,8 @@
     assemble_deep((b0, c0, g0, below, above, left, right, under, over), (be, ce, ge))
     s = (wx, wy, wz, wl, rd, ce, ge)
     weights(be, s, va, 1.0, 1, 15, 7)
-    sweep(va, vb, s, 2, 14, 6)
-    sweep(vb, va, s, 3, 13, 5)
+    sweep(va, vb, s, 2, 14, 12)
+    sweep(vb, va, s, 3, 13, 10)
     for x in range(8):
         v0[x] = va[4 + x, 8:48, :]
     kept = None
@@ -675,8 +675,8 @@
             cut = pl.ds(128 * h, 128)
             p0a[x, :, cut] = p0[x, :, cut] + f0[x // 2, h]
     s0 = (wx0, wy0, wz0, wl0, rd0, ce0, ge0)
-    sweep(p0a, p0b, s0, 2, 14, 6)
-    sweep(p0b, p0a, s0, 3, 13, 5)
+    sweep(p0a, p0b, s0, 2, 14, 12)
+    sweep(p0b, p0a, s0, 3, 13, 10)
     for x in range(8):
         own[x] = p0a[4 + x, 4:36, :]
     copies = [pltpu.make_async_copy(own, pressure, sems.at[0])]

time: 64.5 us -> 64.4 us (level)
  no operation moved by 1% of the time
where the time goes in v6:
time: 64.4 us; the launch traced here: 64.2 us
  starting transfers between devices  31.6 us (49%)
  waiting for transfers between devices  19.4 us (30%)
  Pallas kernels  12.3 us (19%)
  between operations  0.88 us (1%)
    ppermute x12, starting transfers between devices, shift(): lax.ppermute(block, axis, [(i, (i + step) % count) for i in range(count)])  20.1 us
    ppermute x12, waiting for transfers between devices, shift(): lax.ppermute(block, axis, [(i, (i + step) % count) for i in range(count)])  15.7 us
    pallas_call x11, Pallas kernels, call(): pl.pallas_call(kernel, name=name, out_shape=[jax.ShapeDtypeStruct(s, F32)...  12.3 us
    all_to_all x1, starting transfers between devices, per_device(): gathered = lax.all_to_all(pay, 'gx', 0, 0)  6.12 us
    ppermute x2, starting transfers between devices, swap_chips(): return lax.ppermute(block, axis, pairs + [(b, a) for a, b in pairs])  5.41 us
    ppermute x2, waiting for transfers between devices, swap_chips(): return lax.ppermute(block, axis, pairs + [(b, a) for a, b in pairs])  2.74 us
  transfers between devices with their start and end apart: 15, of which 8 were waited for; matrix products, arithmetic and copies ran while one was open for 0% of the time, Pallas kernels for 3%

profile of v6, /device:TPU:2, one launch (start us, length us, event | category | flops | bytes accessed | tf_op | source)
XLA Modules:
  0.0 64.2 jit_solution(2558356168031196314)
XLA Ops:
  0.6 1.2 %load0.1 = (f32[54,8,128]{2,1,0:T(8,128)S(1)}, f32[54,8,128]{2,1,0:T(8,128)S(1)}, f32[8,32,256]{2,1,0:T(8,128)S(1)}, f32[8,32,256]{2,1,0:T(8,128)S(1)}, f32[8,32,256]{2,1,0:T(8,128)S(1)}) custom-call(s32[8,32,256]{2,1,0:T(8,128)} %m.1, s32[8,32,256]{2,1,0:T(8,128)} %f.1, f32[8,32,256]{2,1,0:T(8,128)} %g.1), custom_call_target="tpu_custom_call" | custom-call | tf_op jit(solution)/shard_map/load0/pallas_call | solution.py:700
  1.9 1.7 %collective-permute-start.3 = (f32[54,8,128]{2,1,0:T(8,128)S(1)}, f32[54,8,128]{2,1,0:T(8,128)S(1)}, u32[]{:S(2)}, u32[]{:S(2)}) collective-permute-start(f32[54,8,128]{2,1,0:T(8,128)S(1)} %get-tuple-element.55), channel_id=1, source_target_pairs={{0,31},{1,0},{2,1},{3,2},{4,3},{5,4},{6,5},{7,6},{8,7},{9,8},{10,9... | collective-permute-start | bytes 663560 | tf_op jit(solution)/shard_map/ppermute | solution.py:20
  3.7 2.0 %collective-permute-start = (f32[9,32,256]{2,1,0:T(8,128)S(1)}, f32[9,32,256]{2,1,0:T(8,128)S(1)}, u32[]{:S(2)}, u32[]{:S(2)}) collective-permute-start(f32[9,32,256]{2,1,0:T(8,128)S(1)} %get-tuple-element.52), channel_id=1, source_target_pairs={{0,32},{32,64},{64,96},{96,128},{128,160},{160,192},{192,224},{224... | collective-permute-start | bytes 884744 | tf_op jit(solution)/shard_map/ppermute | solution.py:20
  5.7 4.0 %collective-permute-start.1 = (f32[9,32,256]{2,1,0:T(8,128)S(1)}, f32[9,32,256]{2,1,0:T(8,128)S(1)}, u32[]{:S(2)}, u32[]{:S(2)}) collective-permute-start(f32[9,32,256]{2,1,0:T(8,128)S(1)} %get-tuple-element.53), channel_id=1, source_target_pairs={{0,224},{32,0},{64,32},{96,64},{128,96},{160,128},{192,160},{224,1... | collective-permute-start | bytes 884744 | tf_op jit(solution)/shard_map/ppermute | solution.py:20
  9.8 3.5 %collective-permute-start.5 = (f32[37,8,128]{2,1,0:T(8,128)S(1)}, f32[37,8,128]{2,1,0:T(8,128)S(1)}, u32[]{:S(2)}, u32[]{:S(2)}) collective-permute-start(f32[37,8,128]{2,1,0:T(8,128)S(1)} %get-tuple-element.57), channel_id=1, source_target_pairs={{0,224},{32,0},{64,32},{96,64},{128,96},{160,128},{192,160},{224,1... | collective-permute-start | bytes 454664 | tf_op jit(solution)/shard_map/ppermute | solution.py:20
  13.9 3.4 %collective-permute-done.below.below0 = f32[9,32,256]{2,1,0:T(8,128)S(1)} collective-permute-done((f32[9,32,256]{2,1,0:T(8,128)S(1)}, f32[9,32,256]{2,1,0:T(8,128)S(1)}, u32[]{:S(2)}, u32[]{:S(2)}) %collective-permute-start) | collective-permute-done | bytes 294944 | tf_op jit(solution)/shard_map/ppermute | solution.py:20
  17.3 2.6 %collective-permute-done.4.under.under0 = f32[37,8,128]{2,1,0:T(8,128)S(1)} collective-permute-done((f32[37,8,128]{2,1,0:T(8,128)S(1)}, f32[37,8,128]{2,1,0:T(8,128)S(1)}, u32[]{:S(2)}, u32[]{:S(2)}) %collective-permute-start.4) | collective-permute-done | bytes 151584 | tf_op jit(solution)/shard_map/ppermute | solution.py:20
  19.9 3.1 %descend0.1 = (f32[8,40,256]{2,1,0:T(8,128)S(1)}, f32[4,24,128]{2,1,0:T(8,128)S(1)}, f32[10,24,128]{2,1,0:T(8,128)S(1)}, f32[10,24,128]{2,1,0:T(8,128)S(1)}) custom-call(f32[8,32,256]{2,1,0:T(8,128)S(1)} %get-tuple-element.49.b0, f32[8,32,256]{2,1,0:T(8,128)S(1)} %get-tuple-element.50.c0, f32[8,32,256]{2,1,0:T(8,128)S(1)} %get-tuple-element.51.g0, ...), custom_call_target="tpu_custom_call" | custom-call | tf_op jit(solution)/shard_map/descend0/pallas_call | solution.py:700
  23.1 3.2 %collective-permute-start.7 = (f32[10,24,128]{2,1,0:T(8,128)S(1)}, f32[10,24,128]{2,1,0:T(8,128)S(1)}, u32[]{:S(2)}, u32[]{:S(2)}) collective-permute-start(f32[10,24,128]{2,1,0:T(8,128)S(1)} %get-tuple-element.63), channel_id=1, source_target_pairs={{0,224},{32,0},{64,32},{96,64},{128,96},{160,128},{192,160},{224,1... | collective-permute-start | bytes 368648 | tf_op jit(solution)/shard_map/ppermute | solution.py:20
  26.3 2.9 %collective-permute-done.6.below = f32[10,24,128]{2,1,0:T(8,128)S(1)} collective-permute-done((f32[10,24,128]{2,1,0:T(8,128)S(1)}, f32[10,24,128]{2,1,0:T(8,128)S(1)}, u32[]{:S(2)}, u32[]{:S(2)}) %collective-permute-start.6) | collective-permute-done | bytes 122912 | tf_op jit(solution)/shard_map/ppermute | solution.py:20
  29.2 1.3 %descend1.1 = (f32[4,16,128]{2,1,0:T(8,128)S(1)}, f32[8,3,8,128]{3,2,1,0:T(8,128)}, f32[12,32,128]{2,1,0:T(8,128)S(1)}, f32[12,32,128]{2,1,0:T(8,128)S(1)}, f32[12,32,128]{2,1,0:T(8,128)S(1)}) custom-call(f32[4,24,128]{2,1,0:T(8,128)S(1)} %get-tuple-element.60.g1, f32[4,24,128]{2,1,0:T(8,128)S(1)} %get-tuple-element.58.b1, ...), custom_call_target="tpu_custom_call" | custom-call | tf_op jit(solution)/shard_map/descend1/pallas_call | solution.py:700
  30.4 6.1 %all-to-all-start = ((f32[8,3,8,128]{3,2,1,0:T(8,128)}), f32[8,3,8,128]{3,2,1,0:T(8,128)S(1)}, u32[]{:S(2)}, u32[]{:S(2)}) async-start(f32[8,3,8,128]{3,2,1,0:T(8,128)} %get-tuple-element.64), calls=%async_computation | async-start | bytes 196608 | tf_op jit(solution)/shard_map/all_to_all | solution.py:748
  36.6 2.1 %collective-permute-start.8 = (f32[38,8,128]{2,1,0:T(8,128)S(1)}, f32[38,8,128]{2,1,0:T(8,128)S(1)}, u32[]{:S(2)}, u32[]{:S(2)}) collective-permute-start(f32[38,8,128]{2,1,0:T(8,128)S(1)} %get-tuple-element.67), channel_id=1, source_target_pairs={{0,32},{32,64},{64,96},{96,128},{128,160},{160,192},{192,224},{224... | collective-permute-start | bytes 466952 | tf_op jit(solution)/shard_map/ppermute | solution.py:20
  38.7 1.3 %collective-permute-start.9 = (f32[38,8,128]{2,1,0:T(8,128)S(1)}, f32[38,8,128]{2,1,0:T(8,128)S(1)}, u32[]{:S(2)}, u32[]{:S(2)}) collective-permute-start(f32[38,8,128]{2,1,0:T(8,128)S(1)} %get-tuple-element.68), channel_id=1, source_target_pairs={{0,224},{32,0},{64,32},{96,64},{128,96},{160,128},{192,160},{224,1... | collective-permute-start | bytes 466952 | tf_op jit(solution)/shard_map/ppermute | solution.py:20
  40.0 4.3 %collective-permute-done.8.below = f32[38,8,128]{2,1,0:T(8,128)S(1)} collective-permute-done((f32[38,8,128]{2,1,0:T(8,128)S(1)}, f32[38,8,128]{2,1,0:T(8,128)S(1)}, u32[]{:S(2)}, u32[]{:S(2)}) %collective-permute-start.8) | collective-permute-done | bytes 155680 | tf_op jit(solution)/shard_map/ppermute | solution.py:20
  44.2 0.9 %all-to-all-done.gathered = f32[8,3,8,128]{3,2,1,0:T(8,128)S(1)} async-done(((f32[8,3,8,128]{3,2,1,0:T(8,128)}), f32[8,3,8,128]{3,2,1,0:T(8,128)S(1)}, u32[]{:S(2)}, u32[]{:S(2)}) %all-to-all-start) | async-done | bytes 98336 | tf_op jit(solution)/shard_map/all_to_all | solution.py:748
  45.5 1.7 %collective-permute-start.11 = (f32[30,8,128]{2,1,0:T(8,128)S(1)}, f32[30,8,128]{2,1,0:T(8,128)S(1)}, u32[]{:S(2)}, u32[]{:S(2)}) collective-permute-start(f32[30,8,128]{2,1,0:T(8,128)S(1)} %get-tuple-element.70), channel_id=1, source_target_pairs={{0,31},{1,0},{2,1},{3,2},{4,3},{5,4},{6,5},{7,6},{8,7},{9,8},{10,9... | collective-permute-start | bytes 368648 | tf_op jit(solution)/shard_map/ppermute | solution.py:20
  47.2 2.6 %collective-permute-done.10.left.left1 = f32[30,8,128]{2,1,0:T(8,128)S(1)} collective-permute-done((f32[30,8,128]{2,1,0:T(8,128)S(1)}, f32[30,8,128]{2,1,0:T(8,128)S(1)}, u32[]{:S(2)}, u32[]{:S(2)}) %collective-permute-start.10) | collective-permute-done | bytes 122912 | tf_op jit(solution)/shard_map/ppermute | solution.py:20
  49.8 1.0 %descend2.1 = (f32[8,24,128]{2,1,0:T(8,128)S(1)}, f32[6,8,128]{2,1,0:T(8,128)S(1)}, f32[8,24,128]{2,1,0:T(8,128)S(1)}, f32[8,24,128]{2,1,0:T(8,128)S(1)}, f32[8,...) custom-call(f32[8,3,8,128]{3,2,1,0:T(8,128)S(1)} %all-to-all-done.gather, ...), custom_call_target="tpu_custom_call" | custom-call | tf_op jit(solution)/shard_map/descend2/pallas_call | solution.py:700
  50.8 5.4 %collective-permute-start.12 = (f32[6,8,128]{2,1,0:T(8,128)S(1)}, f32[6,8,128]{2,1,0:T(8,128)S(1)}, u32[]{:S(2)}, u32[]{:S(2)}) collective-permute-start(f32[6,8,128]{2,1,0:T(8,128)S(1)} %get-tuple-element.71.own3), channel_id=1, source_target_pairs={{0,2},{1,3},{4,6},{5,7},{8,10},{9,11},{12,14},{13,15},{16,18},{17,... | collective-permute-start | bytes 73736 | tf_op jit(solution)/shard_map/ppermute | solution.py:32
  56.2 1.1 %prepare.1 = (f32[16,40,256]{2,1,0:T(8,128)S(1)}, f32[16,40,256]{2,1,0:T(8,128)S(1)}, f32[16,40,256]{2,1,0:T(8,128)S(1)}, f32[16,40,256]{2,1,0:T(8,128)S(1)}, f3...) custom-call(f32[8,32,256]{2,1,0:T(8,128)S(1)} %get-tuple-element.49., ...), custom_call_target="tpu_custom_call" | custom-call | tf_op jit(solution)/shard_map/prepare/pallas_call | solution.py:700
  57.2 0.7 %collective-permute-done.12.r0 = f32[6,8,128]{2,1,0:T(8,128)S(1)} collective-permute-done((f32[6,8,128]{2,1,0:T(8,128)S(1)}, f32[6,8,128]{2,1,0:T(8,128)S(1)}, u32[]{:S(2)}, u32[]{:S(2)}) %collective-permute-start.12) | collective-permute-done | bytes 24608 | tf_op jit(solution)/shard_map/ppermute | solution.py:32
  58.0 2.0 %collective-permute-done.13.r1 = f32[6,8,128]{2,1,0:T(8,128)S(1)} collective-permute-done((f32[6,8,128]{2,1,0:T(8,128)S(1)}, f32[6,8,128]{2,1,0:T(8,128)S(1)}, u32[]{:S(2)}, u32[]{:S(2)}) %collective-permute-start.13) | collective-permute-done | bytes 24608 | tf_op jit(solution)/shard_map/ppermute | solution.py:32
  60.0 4.0 %ascend.1 = (f32[8,32,256]{2,1,0:T(8,128)}, f32[8,32,256]{2,1,0:T(8,128)}) custom-call(f32[6,8,128]{2,1,0:T(8,128)S(1)} %get-tuple-element.71.own3, f32[6,8,128]{2,1,0:T(8,128)S(1)} %collective-permute-done.12.r0, f32[6,8,128]{2,1,0:T(8,128)S(1)} %collective-permute-done.13.r1, f32[8,24,128]{2,1,0:T(8,128)S(1)} %get-tuple-element.72.v2, ...), custom_call_target="tpu_custom_call" | custom-call | tf_op jit(solution)/shard_map/ascend/pallas_call | solution.py:700
  (17 shorter events, 1.3 us)
Async XLA Ops:
  1.8 7.9 %collective-permute-start.2 = (f32[54,8,128]{2,1,0:T(8,128)S(1)}, f32[54,8,128]{2,1,0:T(8,128)S(1)}, u32[]{:S(2)}, u32[]{:S(2)}) collective-permute-start(f32[54,8,128]{2,1,0:T(8,128)S(1)} %get-tuple-element.54), channel_id=1, source_target_pairs={{0,1},{1,2},{2,3},{3,4},{4,5},{5,6},{6,7},{7,8},{8,9},{9,10},{10,1... | collective-permute-start | bytes 663560 | tf_op jit(solution)/shard_map/ppermute | solution.py:20
  1.9 7.8 %collective-permute-start.3 = (f32[54,8,128]{2,1,0:T(8,128)S(1)}, f32[54,8,128]{2,1,0:T(8,128)S(1)}, u32[]{:S(2)}, u32[]{:S(2)}) collective-permute-start(f32[54,8,128]{2,1,0:T(8,128)S(1)} %get-tuple-element.55), channel_id=1, source_target_pairs={{0,31},{1,0},{2,1},{3,2},{4,3},{5,4},{6,5},{7,6},{8,7},{9,8},{10,9... | collective-permute-start | bytes 663560 | tf_op jit(solution)/shard_map/ppermute | solution.py:20
  3.7 13.6 %collective-permute-start = (f32[9,32,256]{2,1,0:T(8,128)S(1)}, f32[9,32,256]{2,1,0:T(8,128)S(1)}, u32[]{:S(2)}, u32[]{:S(2)}) collective-permute-start(f32[9,32,256]{2,1,0:T(8,128)S(1)} %get-tuple-element.52), channel_id=1, source_target_pairs={{0,32},{32,64},{64,96},{96,128},{128,160},{160,192},{192,224},{224... | collective-permute-start | bytes 884744 | tf_op jit(solution)/shard_map/ppermute | solution.py:20
  5.7 11.6 %collective-permute-start.1 = (f32[9,32,256]{2,1,0:T(8,128)S(1)}, f32[9,32,256]{2,1,0:T(8,128)S(1)}, u32[]{:S(2)}, u32[]{:S(2)}) collective-permute-start(f32[9,32,256]{2,1,0:T(8,128)S(1)} %get-tuple-element.53), channel_id=1, source_target_pairs={{0,224},{32,0},{64,32},{96,64},{128,96},{160,128},{192,160},{224,1... | collective-permute-start | bytes 884744 | tf_op jit(solution)/shard_map/ppermute | solution.py:20
  9.7 10.2 %collective-permute-start.4 = (f32[37,8,128]{2,1,0:T(8,128)S(1)}, f32[37,8,128]{2,1,0:T(8,128)S(1)}, u32[]{:S(2)}, u32[]{:S(2)}) collective-permute-start(f32[37,8,128]{2,1,0:T(8,128)S(1)} %get-tuple-element.56), channel_id=1, source_target_pairs={{0,32},{32,64},{64,96},{96,128},{128,160},{160,192},{192,224},{224... | collective-permute-start | bytes 454664 | tf_op jit(solution)/shard_map/ppermute | solution.py:20
  9.8 10.1 %collective-permute-start.5 = (f32[37,8,128]{2,1,0:T(8,128)S(1)}, f32[37,8,128]{2,1,0:T(8,128)S(1)}, u32[]{:S(2)}, u32[]{:S(2)}) collective-permute-start(f32[37,8,128]{2,1,0:T(8,128)S(1)} %get-tuple-element.57), channel_id=1, source_target_pairs={{0,224},{32,0},{64,32},{96,64},{128,96},{160,128},{192,160},{224,1... | collective-permute-start | bytes 454664 | tf_op jit(solution)/shard_map/ppermute | solution.py:20
  23.0 6.2 %collective-permute-start.6 = (f32[10,24,128]{2,1,0:T(8,128)S(1)}, f32[10,24,128]{2,1,0:T(8,128)S(1)}, u32[]{:S(2)}, u32[]{:S(2)}) collective-permute-start(f32[10,24,128]{2,1,0:T(8,128)S(1)} %get-tuple-element.62), channel_id=1, source_target_pairs={{0,32},{32,64},{64,96},{96,128},{128,160},{160,192},{192,224},{224... | collective-permute-start | bytes 368648 | tf_op jit(solution)/shard_map/ppermute | solution.py:20
  23.1 6.1 %collective-permute-start.7 = (f32[10,24,128]{2,1,0:T(8,128)S(1)}, f32[10,24,128]{2,1,0:T(8,128)S(1)}, u32[]{:S(2)}, u32[]{:S(2)}) collective-permute-start(f32[10,24,128]{2,1,0:T(8,128)S(1)} %get-tuple-element.63), channel_id=1, source_target_pairs={{0,224},{32,0},{64,32},{96,64},{128,96},{160,128},{192,160},{224,1... | collective-permute-start | bytes 368648 | tf_op jit(solution)/shard_map/ppermute | solution.py:20
  30.4 14.8 %all-to-all-start = ((f32[8,3,8,128]{3,2,1,0:T(8,128)}), f32[8,3,8,128]{3,2,1,0:T(8,128)S(1)}, u32[]{:S(2)}, u32[]{:S(2)}) async-start(f32[8,3,8,128]{3,2,1,0:T(8,128)} %get-tuple-element.64), calls=%async_computation | async-start | bytes 196608 | tf_op jit(solution)/shard_map/all_to_all | solution.py:748
  36.6 7.7 %collective-permute-start.8 = (f32[38,8,128]{2,1,0:T(8,128)S(1)}, f32[38,8,128]{2,1,0:T(8,128)S(1)}, u32[]{:S(2)}, u32[]{:S(2)}) collective-permute-start(f32[38,8,128]{2,1,0:T(8,128)S(1)} %get-tuple-element.67), channel_id=1, source_target_pairs={{0,32},{32,64},{64,96},{96,128},{128,160},{160,192},{192,224},{224... | collective-permute-start | bytes 466952 | tf_op jit(solution)/shard_map/ppermute | solution.py:20
  38.7 5.6 %collective-permute-start.9 = (f32[38,8,128]{2,1,0:T(8,128)S(1)}, f32[38,8,128]{2,1,0:T(8,128)S(1)}, u32[]{:S(2)}, u32[]{:S(2)}) collective-permute-start(f32[38,8,128]{2,1,0:T(8,128)S(1)} %get-tuple-element.68), channel_id=1, source_target_pairs={{0,224},{32,0},{64,32},{96,64},{128,96},{160,128},{192,160},{224,1... | collective-permute-start | bytes 466952 | tf_op jit(solution)/shard_map/ppermute | solution.py:20
  45.2 4.6 %collective-permute-start.10 = (f32[30,8,128]{2,1,0:T(8,128)S(1)}, f32[30,8,128]{2,1,0:T(8,128)S(1)}, u32[]{:S(2)}, u32[]{:S(2)}) collective-permute-start(f32[30,8,128]{2,1,0:T(8,128)S(1)} %get-tuple-element.69), channel_id=1, source_target_pairs={{0,1},{1,2},{2,3},{3,4},{4,5},{5,6},{6,7},{7,8},{8,9},{9,10},{10,1... | collective-permute-start | bytes 368648 | tf_op jit(solution)/shard_map/ppermute | solution.py:20
  45.5 4.3 %collective-permute-start.11 = (f32[30,8,128]{2,1,0:T(8,128)S(1)}, f32[30,8,128]{2,1,0:T(8,128)S(1)}, u32[]{:S(2)}, u32[]{:S(2)}) collective-permute-start(f32[30,8,128]{2,1,0:T(8,128)S(1)} %get-tuple-element.70), channel_id=1, source_target_pairs={{0,31},{1,0},{2,1},{3,2},{4,3},{5,4},{6,5},{7,6},{8,7},{9,8},{10,9... | collective-permute-start | bytes 368648 | tf_op jit(solution)/shard_map/ppermute | solution.py:20
  50.8 7.2 %collective-permute-start.12 = (f32[6,8,128]{2,1,0:T(8,128)S(1)}, f32[6,8,128]{2,1,0:T(8,128)S(1)}, u32[]{:S(2)}, u32[]{:S(2)}) collective-permute-start(f32[6,8,128]{2,1,0:T(8,128)S(1)} %get-tuple-element.71.own3), channel_id=1, source_target_pairs={{0,2},{1,3},{4,6},{5,7},{8,10},{9,11},{12,14},{13,15},{16,18},{17,... | collective-permute-start | bytes 73736 | tf_op jit(solution)/shard_map/ppermute | solution.py:32
  56.2 3.8 %collective-permute-start.13 = (f32[6,8,128]{2,1,0:T(8,128)S(1)}, f32[6,8,128]{2,1,0:T(8,128)S(1)}, u32[]{:S(2)}, u32[]{:S(2)}) collective-permute-start(f32[6,8,128]{2,1,0:T(8,128)S(1)} %get-tuple-element.71.own3), channel_id=1, source_target_pairs={{0,1},{2,4},{3,5},{6,8},{7,9},{10,12},{11,13},{14,16},{15,17},{18,... | collective-permute-start | bytes 73736 | tf_op jit(solution)/shard_map/ppermute | solution.py:32

commit v7 on v6

--- a/solution.py
+++ b/solution.py
@@ -397,16 +397,25 @@
 
 
 def k_pack_v(v0, v1, low, high):
-    for out, first in ((low, 0), (high, 5)):
+    for out, first, edge, second in ((low, 0, 0, 1), (high, 5, 7, 6)):
         for k in range(3):
-            for q in range(5):
+            for q in range(4):
                 for h in range(2):
-                    out[10 * k + 2 * q + h] = v0[
-                        first + k, 8 * q : 8 * q + 8, 128 * h : 128 * h + 128
+                    out[8 * k + 2 * q + h] = v0[
+                        first + k, 4 + 8 * q : 12 + 8 * q, 128 * h : 128 * h + 128
                     ]
+        out[25] = jnp.zeros((8, 128), F32)
+        for h in range(2):
+            cut = slice(128 * h, 128 * h + 128)
+            for side, at in ((0, 2), (1, 36)):
+                t = 4 * side + 2 * h
+                out[24, t : t + 2, :] = v0[edge, at : at + 2, cut]
+                near = 3 if side == 0 else 36
+                t = 2 * side + h
+                out[25, t : t + 1, :] = v0[second, near : near + 1, cut]
         for k in range(4):
             for q in range(2):
-                out[30 + 2 * k + q] = v1[k, 8 * q : 8 * q + 8, :]
+                out[26 + 2 * k + q] = v1[k, 8 * q : 8 * q + 8, :]
 
 
 def k_pack_y2(v1, below, above, gathered, low, high):
@@ -420,11 +429,11 @@
         cut = pl.ds(4 * q, 4)
         for t, x in enumerate(range(-4, 8)):
             if x < 0:
-                val = below[30 + 2 * (x + 4) + q, cut, :]
+                val = below[26 + 2 * (x + 4) + q, cut, :]
             elif x < 4:
                 val = v1[x, pl.ds(12 * q, 4), :]
             else:
-                val = above[30 + 2 * (x - 4) + q, cut, :]
+                val = above[26 + 2 * (x - 4) + q, cut, :]
             half = 4 * (t % 2)
             out[24 + t // 2, half : half + 4, :] = val
 
@@ -541,21 +550,26 @@
     xl = [last_y(p) for p in wx]
     yl = block_last(wy)
     zl = [last_z(p) for p in wz]
-    rd = []
+    keep, add, sides = [], [], []
     for t in range(TILES):
+        faces = (wx[t], xl[t], wy[t], yl[t], wz[t], zl[t])
         d = (wx[t] + xl[t]) + (wy[t] + yl[t]) + (wz[t] + zl[t]) + c[t]
-        rd.append(step_of(d))
-    e = [p * q for p, q in zip(rd, g)]
-    for _ in range(7):
+        rd = step_of(d)
+        keep.append(1.0 - rd * d)
+        add.append(rd * g[t])
+        sides.append([rd * w for w in faces])
+    e = add
+    for first in (0, 0, 1, 1, 1, 1, 2):
         up = block_next(e)
         down = block_last(e)
-        new = []
-        for t in range(TILES):
+        new = list(e)
+        for t in range(first, TILES - first):
             h = e[t]
-            flux = wx[t] * (h - next_y(h)) + xl[t] * (h - last_y(h))
-            flux = flux + (wy[t] * (h - up[t]) + yl[t] * (h - down[t]))
-            flux = flux + (wz[t] * (h - next_z(h)) + zl[t] * (h - last_z(h)))
-            new.append(h + rd[t] * (g[t] - (flux + c[t] * h)))
+            w = sides[t]
+            x = w[0] * next_y(h) + w[1] * last_y(h)
+            y = w[2] * up[t] + w[3] * down[t]
+            z = w[4] * next_z(h) + w[5] * last_z(h)
+            new[t] = (add[t] + keep[t] * h) + (x + y) + z
         e = new
     return e
 
@@ -578,7 +592,7 @@
         else:
             src, k = (below, x + 4) if x < 0 else (above, x - 4)
             for q in range(2):
-                p1[t, 8 + 8 * q : 16 + 8 * q, :] = src[30 + 2 * k + q]
+                p1[t, 8 + 8 * q : 16 + 8 * q, :] = src[26 + 2 * k + q]
         half = 4 * (t % 2)
         p1[t, 4:8, :] = left1[24 + t // 2, half : half + 4, :]
         p1[t, 24:28, :] = right1[24 + t // 2, half : half + 4, :]
@@ -587,11 +601,18 @@
             p0[4 + x] = v0[x]
         else:
             src, k = (below, x + 3) if x < 0 else (above, x - 8)
-            for q in range(5):
-                for h in range(2):
-                    p0[4 + x, 8 * q : 8 * q + 8, 128 * h : 128 * h + 128] = (
-                        src[10 * k + 2 * q + h]
-                    )
+            p0[4 + x, 0:4, :] = jnp.zeros((4, 256), F32)
+            p0[4 + x, 36:40, :] = jnp.zeros((4, 256), F32)
+            for h in range(2):
+                cut = slice(128 * h, 128 * h + 128)
+                for q in range(4):
+                    p0[4 + x, 4 + 8 * q : 12 + 8 * q, cut] = src[8 * k + 2 * q + h]
+                if x in (-1, 8):
+                    p0[4 + x, 2:4, cut] = src[24, 2 * h : 2 * h + 2, :]
+                    p0[4 + x, 36:38, cut] = src[24, 4 + 2 * h : 6 + 2 * h, :]
+                if x in (-2, 9):
+                    p0[4 + x, 3:4, cut] = src[25, h : h + 1, :]
+                    p0[4 + x, 36:37, cut] = src[25, 2 + h : 3 + h, :]
 
 
 def k_ascend(
@@ -746,7 +767,7 @@
         g1, b1, c1, bc2, below, above,
     )
     gathered = lax.all_to_all(pay, "gx", 0, 0)
-    low, high = call(k_pack_v, "pack_v", [(38, 8, 128)] * 2, [], 4, v0, v1)
+    low, high = call(k_pack_v, "pack_v", [(34, 8, 128)] * 2, [], 4, v0, v1)
     below, above = exchange(low, high, "gx")
     low, high = call(
         k_pack_y2, "pack_y2", [(30, 8, 128)] * 2, [], 4, v1, below, above, gathered

time: 64.4 us -> 64.3 us (level)
  no operation moved by 1% of the time
where the time goes in v7:
time: 64.3 us; the launch traced here: 64.1 us
  starting transfers between devices  31.6 us (49%)
  waiting for transfers between devices  19.3 us (30%)
  Pallas kernels  12.3 us (19%)
  between operations  0.88 us (1%)
    ppermute x12, starting transfers between devices, shift(): lax.ppermute(block, axis, [(i, (i + step) % count) for i in range(count)])  20.1 us
    ppermute x12, waiting for transfers between devices, shift(): lax.ppermute(block, axis, [(i, (i + step) % count) for i in range(count)])  15.5 us
    pallas_call x11, Pallas kernels, call(): pl.pallas_call(kernel, name=name, out_shape=[jax.ShapeDtypeStruct(s, F32)...  12.3 us
    all_to_all x1, starting transfers between devices, per_device(): gathered = lax.all_to_all(pay, 'gx', 0, 0)  6.12 us
    ppermute x2, starting transfers between devices, swap_chips(): return lax.ppermute(block, axis, pairs + [(b, a) for a, b in pairs])  5.4 us
    ppermute x2, waiting for transfers between devices, swap_chips(): return lax.ppermute(block, axis, pairs + [(b, a) for a, b in pairs])  2.75 us
  transfers between devices with their start and end apart: 15, of which 8 were waited for; matrix products, arithmetic and copies ran while one was open for 0% of the time, Pallas kernels for 3%

profile of v7, /device:TPU:2, one launch (start us, length us, event | category | flops | bytes accessed | tf_op | source)
XLA Modules:
  0.0 64.1 jit_solution(9638917707842959126)
XLA Ops:
  0.6 1.2 %load0.1 = (f32[54,8,128]{2,1,0:T(8,128)S(1)}, f32[54,8,128]{2,1,0:T(8,128)S(1)}, f32[8,32,256]{2,1,0:T(8,128)S(1)}, f32[8,32,256]{2,1,0:T(8,128)S(1)}, f32[8,32,256]{2,1,0:T(8,128)S(1)}) custom-call(s32[8,32,256]{2,1,0:T(8,128)} %m.1, s32[8,32,256]{2,1,0:T(8,128)} %f.1, f32[8,32,256]{2,1,0:T(8,128)} %g.1), custom_call_target="tpu_custom_call" | custom-call | tf_op jit(solution)/shard_map/load0/pallas_call | solution.py:721
  1.9 1.7 %collective-permute-start.3 = (f32[54,8,128]{2,1,0:T(8,128)S(1)}, f32[54,8,128]{2,1,0:T(8,128)S(1)}, u32[]{:S(2)}, u32[]{:S(2)}) collective-permute-start(f32[54,8,128]{2,1,0:T(8,128)S(1)} %get-tuple-element.55), channel_id=1, source_target_pairs={{0,31},{1,0},{2,1},{3,2},{4,3},{5,4},{6,5},{7,6},{8,7},{9,8},{10,9... | collective-permute-start | bytes 663560 | tf_op jit(solution)/shard_map/ppermute | solution.py:20
  3.7 2.0 %collective-permute-start = (f32[9,32,256]{2,1,0:T(8,128)S(1)}, f32[9,32,256]{2,1,0:T(8,128)S(1)}, u32[]{:S(2)}, u32[]{:S(2)}) collective-permute-start(f32[9,32,256]{2,1,0:T(8,128)S(1)} %get-tuple-element.52), channel_id=1, source_target_pairs={{0,32},{32,64},{64,96},{96,128},{128,160},{160,192},{192,224},{224... | collective-permute-start | bytes 884744 | tf_op jit(solution)/shard_map/ppermute | solution.py:20
  5.7 4.0 %collective-permute-start.1 = (f32[9,32,256]{2,1,0:T(8,128)S(1)}, f32[9,32,256]{2,1,0:T(8,128)S(1)}, u32[]{:S(2)}, u32[]{:S(2)}) collective-permute-start(f32[9,32,256]{2,1,0:T(8,128)S(1)} %get-tuple-element.53), channel_id=1, source_target_pairs={{0,224},{32,0},{64,32},{96,64},{128,96},{160,128},{192,160},{224,1... | collective-permute-start | bytes 884744 | tf_op jit(solution)/shard_map/ppermute | solution.py:20
  9.8 3.5 %collective-permute-start.5 = (f32[37,8,128]{2,1,0:T(8,128)S(1)}, f32[37,8,128]{2,1,0:T(8,128)S(1)}, u32[]{:S(2)}, u32[]{:S(2)}) collective-permute-start(f32[37,8,128]{2,1,0:T(8,128)S(1)} %get-tuple-element.57), channel_id=1, source_target_pairs={{0,224},{32,0},{64,32},{96,64},{128,96},{160,128},{192,160},{224,1... | collective-permute-start | bytes 454664 | tf_op jit(solution)/shard_map/ppermute | solution.py:20
  13.9 3.4 %collective-permute-done.below.below0 = f32[9,32,256]{2,1,0:T(8,128)S(1)} collective-permute-done((f32[9,32,256]{2,1,0:T(8,128)S(1)}, f32[9,32,256]{2,1,0:T(8,128)S(1)}, u32[]{:S(2)}, u32[]{:S(2)}) %collective-permute-start) | collective-permute-done | bytes 294944 | tf_op jit(solution)/shard_map/ppermute | solution.py:20
  17.3 2.6 %collective-permute-done.4.under.under0 = f32[37,8,128]{2,1,0:T(8,128)S(1)} collective-permute-done((f32[37,8,128]{2,1,0:T(8,128)S(1)}, f32[37,8,128]{2,1,0:T(8,128)S(1)}, u32[]{:S(2)}, u32[]{:S(2)}) %collective-permute-start.4) | collective-permute-done | bytes 151584 | tf_op jit(solution)/shard_map/ppermute | solution.py:20
  19.9 3.1 %descend0.1 = (f32[8,40,256]{2,1,0:T(8,128)S(1)}, f32[4,24,128]{2,1,0:T(8,128)S(1)}, f32[10,24,128]{2,1,0:T(8,128)S(1)}, f32[10,24,128]{2,1,0:T(8,128)S(1)}) custom-call(f32[8,32,256]{2,1,0:T(8,128)S(1)} %get-tuple-element.49.b0, f32[8,32,256]{2,1,0:T(8,128)S(1)} %get-tuple-element.50.c0, f32[8,32,256]{2,1,0:T(8,128)S(1)} %get-tuple-element.51.g0, ...), custom_call_target="tpu_custom_call" | custom-call | tf_op jit(solution)/shard_map/descend0/pallas_call | solution.py:721
  23.1 3.2 %collective-permute-start.7 = (f32[10,24,128]{2,1,0:T(8,128)S(1)}, f32[10,24,128]{2,1,0:T(8,128)S(1)}, u32[]{:S(2)}, u32[]{:S(2)}) collective-permute-start(f32[10,24,128]{2,1,0:T(8,128)S(1)} %get-tuple-element.63), channel_id=1, source_target_pairs={{0,224},{32,0},{64,32},{96,64},{128,96},{160,128},{192,160},{224,1... | collective-permute-start | bytes 368648 | tf_op jit(solution)/shard_map/ppermute | solution.py:20
  26.3 2.9 %collective-permute-done.6.below = f32[10,24,128]{2,1,0:T(8,128)S(1)} collective-permute-done((f32[10,24,128]{2,1,0:T(8,128)S(1)}, f32[10,24,128]{2,1,0:T(8,128)S(1)}, u32[]{:S(2)}, u32[]{:S(2)}) %collective-permute-start.6) | collective-permute-done | bytes 122912 | tf_op jit(solution)/shard_map/ppermute | solution.py:20
  29.2 1.3 %descend1.1 = (f32[4,16,128]{2,1,0:T(8,128)S(1)}, f32[8,3,8,128]{3,2,1,0:T(8,128)}, f32[12,32,128]{2,1,0:T(8,128)S(1)}, f32[12,32,128]{2,1,0:T(8,128)S(1)}, f32[12,32,128]{2,1,0:T(8,128)S(1)}) custom-call(f32[4,24,128]{2,1,0:T(8,128)S(1)} %get-tuple-element.60.g1, f32[4,24,128]{2,1,0:T(8,128)S(1)} %get-tuple-element.58.b1, ...), custom_call_target="tpu_custom_call" | custom-call | tf_op jit(solution)/shard_map/descend1/pallas_call | solution.py:721
  30.4 6.1 %all-to-all-start = ((f32[8,3,8,128]{3,2,1,0:T(8,128)}), f32[8,3,8,128]{3,2,1,0:T(8,128)S(1)}, u32[]{:S(2)}, u32[]{:S(2)}) async-start(f32[8,3,8,128]{3,2,1,0:T(8,128)} %get-tuple-element.64), calls=%async_computation | async-start | bytes 196608 | tf_op jit(solution)/shard_map/all_to_all | solution.py:769
  36.6 2.1 %collective-permute-start.8 = (f32[34,8,128]{2,1,0:T(8,128)S(1)}, f32[34,8,128]{2,1,0:T(8,128)S(1)}, u32[]{:S(2)}, u32[]{:S(2)}) collective-permute-start(f32[34,8,128]{2,1,0:T(8,128)S(1)} %get-tuple-element.67), channel_id=1, source_target_pairs={{0,32},{32,64},{64,96},{96,128},{128,160},{160,192},{192,224},{224... | collective-permute-start | bytes 417800 | tf_op jit(solution)/shard_map/ppermute | solution.py:20
  38.7 1.3 %collective-permute-start.9 = (f32[34,8,128]{2,1,0:T(8,128)S(1)}, f32[34,8,128]{2,1,0:T(8,128)S(1)}, u32[]{:S(2)}, u32[]{:S(2)}) collective-permute-start(f32[34,8,128]{2,1,0:T(8,128)S(1)} %get-tuple-element.68), channel_id=1, source_target_pairs={{0,224},{32,0},{64,32},{96,64},{128,96},{160,128},{192,160},{224,1... | collective-permute-start | bytes 417800 | tf_op jit(solution)/shard_map/ppermute | solution.py:20
  40.0 4.1 %collective-permute-done.8.below = f32[34,8,128]{2,1,0:T(8,128)S(1)} collective-permute-done((f32[34,8,128]{2,1,0:T(8,128)S(1)}, f32[34,8,128]{2,1,0:T(8,128)S(1)}, u32[]{:S(2)}, u32[]{:S(2)}) %collective-permute-start.8) | collective-permute-done | bytes 139296 | tf_op jit(solution)/shard_map/ppermute | solution.py:20
  44.1 1.1 %all-to-all-done.gathered = f32[8,3,8,128]{3,2,1,0:T(8,128)S(1)} async-done(((f32[8,3,8,128]{3,2,1,0:T(8,128)}), f32[8,3,8,128]{3,2,1,0:T(8,128)S(1)}, u32[]{:S(2)}, u32[]{:S(2)}) %all-to-all-start) | async-done | bytes 98336 | tf_op jit(solution)/shard_map/all_to_all | solution.py:769
  45.5 1.7 %collective-permute-start.11 = (f32[30,8,128]{2,1,0:T(8,128)S(1)}, f32[30,8,128]{2,1,0:T(8,128)S(1)}, u32[]{:S(2)}, u32[]{:S(2)}) collective-permute-start(f32[30,8,128]{2,1,0:T(8,128)S(1)} %get-tuple-element.70), channel_id=1, source_target_pairs={{0,31},{1,0},{2,1},{3,2},{4,3},{5,4},{6,5},{7,6},{8,7},{9,8},{10,9... | collective-permute-start | bytes 368648 | tf_op jit(solution)/shard_map/ppermute | solution.py:20
  47.2 2.6 %collective-permute-done.10.left.left1 = f32[30,8,128]{2,1,0:T(8,128)S(1)} collective-permute-done((f32[30,8,128]{2,1,0:T(8,128)S(1)}, f32[30,8,128]{2,1,0:T(8,128)S(1)}, u32[]{:S(2)}, u32[]{:S(2)}) %collective-permute-start.10) | collective-permute-done | bytes 122912 | tf_op jit(solution)/shard_map/ppermute | solution.py:20
  49.8 1.0 %descend2.1 = (f32[8,24,128]{2,1,0:T(8,128)S(1)}, f32[6,8,128]{2,1,0:T(8,128)S(1)}, f32[8,24,128]{2,1,0:T(8,128)S(1)}, f32[8,24,128]{2,1,0:T(8,128)S(1)}, f32[8,...) custom-call(f32[8,3,8,128]{3,2,1,0:T(8,128)S(1)} %all-to-all-done.gather, ...), custom_call_target="tpu_custom_call" | custom-call | tf_op jit(solution)/shard_map/descend2/pallas_call | solution.py:721
  50.8 5.4 %collective-permute-start.12 = (f32[6,8,128]{2,1,0:T(8,128)S(1)}, f32[6,8,128]{2,1,0:T(8,128)S(1)}, u32[]{:S(2)}, u32[]{:S(2)}) collective-permute-start(f32[6,8,128]{2,1,0:T(8,128)S(1)} %get-tuple-element.71.own3), channel_id=1, source_target_pairs={{0,2},{1,3},{4,6},{5,7},{8,10},{9,11},{12,14},{13,15},{16,18},{17,... | collective-permute-start | bytes 73736 | tf_op jit(solution)/shard_map/ppermute | solution.py:32
  56.2 1.1 %prepare.1 = (f32[16,40,256]{2,1,0:T(8,128)S(1)}, f32[16,40,256]{2,1,0:T(8,128)S(1)}, f32[16,40,256]{2,1,0:T(8,128)S(1)}, f32[16,40,256]{2,1,0:T(8,128)S(1)}, f3...) custom-call(f32[8,32,256]{2,1,0:T(8,128)S(1)} %get-tuple-element.49., ...), custom_call_target="tpu_custom_call" | custom-call | tf_op jit(solution)/shard_map/prepare/pallas_call | solution.py:721
  57.2 0.7 %collective-permute-done.12.r0 = f32[6,8,128]{2,1,0:T(8,128)S(1)} collective-permute-done((f32[6,8,128]{2,1,0:T(8,128)S(1)}, f32[6,8,128]{2,1,0:T(8,128)S(1)}, u32[]{:S(2)}, u32[]{:S(2)}) %collective-permute-start.12) | collective-permute-done | bytes 24608 | tf_op jit(solution)/shard_map/ppermute | solution.py:32
  58.0 2.0 %collective-permute-done.13.r1 = f32[6,8,128]{2,1,0:T(8,128)S(1)} collective-permute-done((f32[6,8,128]{2,1,0:T(8,128)S(1)}, f32[6,8,128]{2,1,0:T(8,128)S(1)}, u32[]{:S(2)}, u32[]{:S(2)}) %collective-permute-start.13) | collective-permute-done | bytes 24608 | tf_op jit(solution)/shard_map/ppermute | solution.py:32
  60.0 4.0 %ascend.1 = (f32[8,32,256]{2,1,0:T(8,128)}, f32[8,32,256]{2,1,0:T(8,128)}) custom-call(f32[6,8,128]{2,1,0:T(8,128)S(1)} %get-tuple-element.71.own3, f32[6,8,128]{2,1,0:T(8,128)S(1)} %collective-permute-done.12.r0, f32[6,8,128]{2,1,0:T(8,128)S(1)} %collective-permute-done.13.r1, f32[8,24,128]{2,1,0:T(8,128)S(1)} %get-tuple-element.72.v2, ...), custom_call_target="tpu_custom_call" | custom-call | tf_op jit(solution)/shard_map/ascend/pallas_call | solution.py:721
  (17 shorter events, 1.3 us)
Async XLA Ops:
  1.8 7.9 %collective-permute-start.2 = (f32[54,8,128]{2,1,0:T(8,128)S(1)}, f32[54,8,128]{2,1,0:T(8,128)S(1)}, u32[]{:S(2)}, u32[]{:S(2)}) collective-permute-start(f32[54,8,128]{2,1,0:T(8,128)S(1)} %get-tuple-element.54), channel_id=1, source_target_pairs={{0,1},{1,2},{2,3},{3,4},{4,5},{5,6},{6,7},{7,8},{8,9},{9,10},{10,1... | collective-permute-start | bytes 663560 | tf_op jit(solution)/shard_map/ppermute | solution.py:20
  1.9 7.8 %collective-permute-start.3 = (f32[54,8,128]{2,1,0:T(8,128)S(1)}, f32[54,8,128]{2,1,0:T(8,128)S(1)}, u32[]{:S(2)}, u32[]{:S(2)}) collective-permute-start(f32[54,8,128]{2,1,0:T(8,128)S(1)} %get-tuple-element.55), channel_id=1, source_target_pairs={{0,31},{1,0},{2,1},{3,2},{4,3},{5,4},{6,5},{7,6},{8,7},{9,8},{10,9... | collective-permute-start | bytes 663560 | tf_op jit(solution)/shard_map/ppermute | solution.py:20
  3.7 13.6 %collective-permute-start = (f32[9,32,256]{2,1,0:T(8,128)S(1)}, f32[9,32,256]{2,1,0:T(8,128)S(1)}, u32[]{:S(2)}, u32[]{:S(2)}) collective-permute-start(f32[9,32,256]{2,1,0:T(8,128)S(1)} %get-tuple-element.52), channel_id=1, source_target_pairs={{0,32},{32,64},{64,96},{96,128},{128,160},{160,192},{192,224},{224... | collective-permute-start | bytes 884744 | tf_op jit(solution)/shard_map/ppermute | solution.py:20
  5.7 11.6 %collective-permute-start.1 = (f32[9,32,256]{2,1,0:T(8,128)S(1)}, f32[9,32,256]{2,1,0:T(8,128)S(1)}, u32[]{:S(2)}, u32[]{:S(2)}) collective-permute-start(f32[9,32,256]{2,1,0:T(8,128)S(1)} %get-tuple-element.53), channel_id=1, source_target_pairs={{0,224},{32,0},{64,32},{96,64},{128,96},{160,128},{192,160},{224,1... | collective-permute-start | bytes 884744 | tf_op jit(solution)/shard_map/ppermute | solution.py:20
  9.7 10.2 %collective-permute-start.4 = (f32[37,8,128]{2,1,0:T(8,128)S(1)}, f32[37,8,128]{2,1,0:T(8,128)S(1)}, u32[]{:S(2)}, u32[]{:S(2)}) collective-permute-start(f32[37,8,128]{2,1,0:T(8,128)S(1)} %get-tuple-element.56), channel_id=1, source_target_pairs={{0,32},{32,64},{64,96},{96,128},{128,160},{160,192},{192,224},{224... | collective-permute-start | bytes 454664 | tf_op jit(solution)/shard_map/ppermute | solution.py:20
  9.8 10.1 %collective-permute-start.5 = (f32[37,8,128]{2,1,0:T(8,128)S(1)}, f32[37,8,128]{2,1,0:T(8,128)S(1)}, u32[]{:S(2)}, u32[]{:S(2)}) collective-permute-start(f32[37,8,128]{2,1,0:T(8,128)S(1)} %get-tuple-element.57), channel_id=1, source_target_pairs={{0,224},{32,0},{64,32},{96,64},{128,96},{160,128},{192,160},{224,1... | collective-permute-start | bytes 454664 | tf_op jit(solution)/shard_map/ppermute | solution.py:20
  23.0 6.2 %collective-permute-start.6 = (f32[10,24,128]{2,1,0:T(8,128)S(1)}, f32[10,24,128]{2,1,0:T(8,128)S(1)}, u32[]{:S(2)}, u32[]{:S(2)}) collective-permute-start(f32[10,24,128]{2,1,0:T(8,128)S(1)} %get-tuple-element.62), channel_id=1, source_target_pairs={{0,32},{32,64},{64,96},{96,128},{128,160},{160,192},{192,224},{224... | collective-permute-start | bytes 368648 | tf_op jit(solution)/shard_map/ppermute | solution.py:20
  23.1 6.1 %collective-permute-start.7 = (f32[10,24,128]{2,1,0:T(8,128)S(1)}, f32[10,24,128]{2,1,0:T(8,128)S(1)}, u32[]{:S(2)}, u32[]{:S(2)}) collective-permute-start(f32[10,24,128]{2,1,0:T(8,128)S(1)} %get-tuple-element.63), channel_id=1, source_target_pairs={{0,224},{32,0},{64,32},{96,64},{128,96},{160,128},{192,160},{224,1... | collective-permute-start | bytes 368648 | tf_op jit(solution)/shard_map/ppermute | solution.py:20
  30.4 14.8 %all-to-all-start = ((f32[8,3,8,128]{3,2,1,0:T(8,128)}), f32[8,3,8,128]{3,2,1,0:T(8,128)S(1)}, u32[]{:S(2)}, u32[]{:S(2)}) async-start(f32[8,3,8,128]{3,2,1,0:T(8,128)} %get-tuple-element.64), calls=%async_computation | async-start | bytes 196608 | tf_op jit(solution)/shard_map/all_to_all | solution.py:769
  36.6 7.5 %collective-permute-start.8 = (f32[34,8,128]{2,1,0:T(8,128)S(1)}, f32[34,8,128]{2,1,0:T(8,128)S(1)}, u32[]{:S(2)}, u32[]{:S(2)}) collective-permute-start(f32[34,8,128]{2,1,0:T(8,128)S(1)} %get-tuple-element.67), channel_id=1, source_target_pairs={{0,32},{32,64},{64,96},{96,128},{128,160},{160,192},{192,224},{224... | collective-permute-start | bytes 417800 | tf_op jit(solution)/shard_map/ppermute | solution.py:20
  38.7 5.4 %collective-permute-start.9 = (f32[34,8,128]{2,1,0:T(8,128)S(1)}, f32[34,8,128]{2,1,0:T(8,128)S(1)}, u32[]{:S(2)}, u32[]{:S(2)}) collective-permute-start(f32[34,8,128]{2,1,0:T(8,128)S(1)} %get-tuple-element.68), channel_id=1, source_target_pairs={{0,224},{32,0},{64,32},{96,64},{128,96},{160,128},{192,160},{224,1... | collective-permute-start | bytes 417800 | tf_op jit(solution)/shard_map/ppermute | solution.py:20
  45.2 4.6 %collective-permute-start.10 = (f32[30,8,128]{2,1,0:T(8,128)S(1)}, f32[30,8,128]{2,1,0:T(8,128)S(1)}, u32[]{:S(2)}, u32[]{:S(2)}) collective-permute-start(f32[30,8,128]{2,1,0:T(8,128)S(1)} %get-tuple-element.69), channel_id=1, source_target_pairs={{0,1},{1,2},{2,3},{3,4},{4,5},{5,6},{6,7},{7,8},{8,9},{9,10},{10,1... | collective-permute-start | bytes 368648 | tf_op jit(solution)/shard_map/ppermute | solution.py:20
  45.5 4.3 %collective-permute-start.11 = (f32[30,8,128]{2,1,0:T(8,128)S(1)}, f32[30,8,128]{2,1,0:T(8,128)S(1)}, u32[]{:S(2)}, u32[]{:S(2)}) collective-permute-start(f32[30,8,128]{2,1,0:T(8,128)S(1)} %get-tuple-element.70), channel_id=1, source_target_pairs={{0,31},{1,0},{2,1},{3,2},{4,3},{5,4},{6,5},{7,6},{8,7},{9,8},{10,9... | collective-permute-start | bytes 368648 | tf_op jit(solution)/shard_map/ppermute | solution.py:20
  50.8 7.2 %collective-permute-start.12 = (f32[6,8,128]{2,1,0:T(8,128)S(1)}, f32[6,8,128]{2,1,0:T(8,128)S(1)}, u32[]{:S(2)}, u32[]{:S(2)}) collective-permute-start(f32[6,8,128]{2,1,0:T(8,128)S(1)} %get-tuple-element.71.own3), channel_id=1, source_target_pairs={{0,2},{1,3},{4,6},{5,7},{8,10},{9,11},{12,14},{13,15},{16,18},{17,... | collective-permute-start | bytes 73736 | tf_op jit(solution)/shard_map/ppermute | solution.py:32
  56.2 3.8 %collective-permute-start.13 = (f32[6,8,128]{2,1,0:T(8,128)S(1)}, f32[6,8,128]{2,1,0:T(8,128)S(1)}, u32[]{:S(2)}, u32[]{:S(2)}) collective-permute-start(f32[6,8,128]{2,1,0:T(8,128)S(1)} %get-tuple-element.71.own3), channel_id=1, source_target_pairs={{0,1},{2,4},{3,5},{6,8},{7,9},{10,12},{11,13},{14,16},{15,17},{18,... | collective-permute-start | bytes 73736 | tf_op jit(solution)/shard_map/ppermute | solution.py:32

commit v8 on v6

--- a/solution.py
+++ b/solution.py
@@ -756,7 +756,8 @@
         k_descend2, "descend2", [E2, (6, 8, 128)] + [E2] * 6, [E2, (384, 128)], 4,
         gathered, left1, right1,
     )
-    r0, r1 = swap_chips(own3, "gy", 0), swap_chips(own3, "gy", 1)
+    r1 = swap_chips(own3, "gy", 1)
+    r0 = swap_chips(own3, "gy", 0)
     p0, ce0, ge0, wx0, wy0, wz0, wl0, rd0, p1, *w1 = call(
         k_prepare, "prepare", [E0] * 8 + [E1] * 6, [E0, E0, E1], 8,
         *own0, be1, ce1, ge1, v0, v1, below, above, left1, right1,

time: 64.4 us -> 64.4 us (level)
  no operation moved by 1% of the time
where the time goes in v8:
time: 64.4 us; the launch traced here: 64.2 us
  starting transfers between devices  31.6 us (49%)
  waiting for transfers between devices  19.4 us (30%)
  Pallas kernels  12.3 us (19%)
  between operations  0.88 us (1%)
    ppermute x12, starting transfers between devices, shift(): lax.ppermute(block, axis, [(i, (i + step) % count) for i in range(count)])  20.1 us
    ppermute x12, waiting for transfers between devices, shift(): lax.ppermute(block, axis, [(i, (i + step) % count) for i in range(count)])  15.7 us
    pallas_call x11, Pallas kernels, call(): pl.pallas_call(kernel, name=name, out_shape=[jax.ShapeDtypeStruct(s, F32)...  12.3 us
    all_to_all x1, starting transfers between devices, per_device(): gathered = lax.all_to_all(pay, 'gx', 0, 0)  6.12 us
    ppermute x2, starting transfers between devices, swap_chips(): return lax.ppermute(block, axis, pairs + [(b, a) for a, b in pairs])  5.41 us
    ppermute x2, waiting for transfers between devices, swap_chips(): return lax.ppermute(block, axis, pairs + [(b, a) for a, b in pairs])  2.74 us
  transfers between devices with their start and end apart: 15, of which 8 were waited for; matrix products, arithmetic and copies ran while one was open for 0% of the time, Pallas kernels for 3%

profile of v8, /device:TPU:2, one launch (start us, length us, event | category | flops | bytes accessed | tf_op | source)
XLA Modules:
  0.0 64.2 jit_solution(2558356168031196314)
XLA Ops:
  0.6 1.2 %load0.1 = (f32[54,8,128]{2,1,0:T(8,128)S(1)}, f32[54,8,128]{2,1,0:T(8,128)S(1)}, f32[8,32,256]{2,1,0:T(8,128)S(1)}, f32[8,32,256]{2,1,0:T(8,128)S(1)}, f32[8,32,256]{2,1,0:T(8,128)S(1)}) custom-call(s32[8,32,256]{2,1,0:T(8,128)} %m.1, s32[8,32,256]{2,1,0:T(8,128)} %f.1, f32[8,32,256]{2,1,0:T(8,128)} %g.1), custom_call_target="tpu_custom_call" | custom-call | tf_op jit(solution)/shard_map/load0/pallas_call | solution.py:700
  1.9 1.7 %collective-permute-start.3 = (f32[54,8,128]{2,1,0:T(8,128)S(1)}, f32[54,8,128]{2,1,0:T(8,128)S(1)}, u32[]{:S(2)}, u32[]{:S(2)}) collective-permute-start(f32[54,8,128]{2,1,0:T(8,128)S(1)} %get-tuple-element.55), channel_id=1, source_target_pairs={{0,31},{1,0},{2,1},{3,2},{4,3},{5,4},{6,5},{7,6},{8,7},{9,8},{10,9... | collective-permute-start | bytes 663560 | tf_op jit(solution)/shard_map/ppermute | solution.py:20
  3.7 2.0 %collective-permute-start = (f32[9,32,256]{2,1,0:T(8,128)S(1)}, f32[9,32,256]{2,1,0:T(8,128)S(1)}, u32[]{:S(2)}, u32[]{:S(2)}) collective-permute-start(f32[9,32,256]{2,1,0:T(8,128)S(1)} %get-tuple-element.52), channel_id=1, source_target_pairs={{0,32},{32,64},{64,96},{96,128},{128,160},{160,192},{192,224},{224... | collective-permute-start | bytes 884744 | tf_op jit(solution)/shard_map/ppermute | solution.py:20
  5.7 4.0 %collective-permute-start.1 = (f32[9,32,256]{2,1,0:T(8,128)S(1)}, f32[9,32,256]{2,1,0:T(8,128)S(1)}, u32[]{:S(2)}, u32[]{:S(2)}) collective-permute-start(f32[9,32,256]{2,1,0:T(8,128)S(1)} %get-tuple-element.53), channel_id=1, source_target_pairs={{0,224},{32,0},{64,32},{96,64},{128,96},{160,128},{192,160},{224,1... | collective-permute-start | bytes 884744 | tf_op jit(solution)/shard_map/ppermute | solution.py:20
  9.8 3.5 %collective-permute-start.5 = (f32[37,8,128]{2,1,0:T(8,128)S(1)}, f32[37,8,128]{2,1,0:T(8,128)S(1)}, u32[]{:S(2)}, u32[]{:S(2)}) collective-permute-start(f32[37,8,128]{2,1,0:T(8,128)S(1)} %get-tuple-element.57), channel_id=1, source_target_pairs={{0,224},{32,0},{64,32},{96,64},{128,96},{160,128},{192,160},{224,1... | collective-permute-start | bytes 454664 | tf_op jit(solution)/shard_map/ppermute | solution.py:20
  13.9 3.4 %collective-permute-done.below.below0 = f32[9,32,256]{2,1,0:T(8,128)S(1)} collective-permute-done((f32[9,32,256]{2,1,0:T(8,128)S(1)}, f32[9,32,256]{2,1,0:T(8,128)S(1)}, u32[]{:S(2)}, u32[]{:S(2)}) %collective-permute-start) | collective-permute-done | bytes 294944 | tf_op jit(solution)/shard_map/ppermute | solution.py:20
  17.3 2.6 %collective-permute-done.4.under.under0 = f32[37,8,128]{2,1,0:T(8,128)S(1)} collective-permute-done((f32[37,8,128]{2,1,0:T(8,128)S(1)}, f32[37,8,128]{2,1,0:T(8,128)S(1)}, u32[]{:S(2)}, u32[]{:S(2)}) %collective-permute-start.4) | collective-permute-done | bytes 151584 | tf_op jit(solution)/shard_map/ppermute | solution.py:20
  19.9 3.1 %descend0.1 = (f32[8,40,256]{2,1,0:T(8,128)S(1)}, f32[4,24,128]{2,1,0:T(8,128)S(1)}, f32[10,24,128]{2,1,0:T(8,128)S(1)}, f32[10,24,128]{2,1,0:T(8,128)S(1)}) custom-call(f32[8,32,256]{2,1,0:T(8,128)S(1)} %get-tuple-element.49.b0, f32[8,32,256]{2,1,0:T(8,128)S(1)} %get-tuple-element.50.c0, f32[8,32,256]{2,1,0:T(8,128)S(1)} %get-tuple-element.51.g0, ...), custom_call_target="tpu_custom_call" | custom-call | tf_op jit(solution)/shard_map/descend0/pallas_call | solution.py:700
  23.1 3.2 %collective-permute-start.7 = (f32[10,24,128]{2,1,0:T(8,128)S(1)}, f32[10,24,128]{2,1,0:T(8,128)S(1)}, u32[]{:S(2)}, u32[]{:S(2)}) collective-permute-start(f32[10,24,128]{2,1,0:T(8,128)S(1)} %get-tuple-element.63), channel_id=1, source_target_pairs={{0,224},{32,0},{64,32},{96,64},{128,96},{160,128},{192,160},{224,1... | collective-permute-start | bytes 368648 | tf_op jit(solution)/shard_map/ppermute | solution.py:20
  26.3 2.9 %collective-permute-done.6.below = f32[10,24,128]{2,1,0:T(8,128)S(1)} collective-permute-done((f32[10,24,128]{2,1,0:T(8,128)S(1)}, f32[10,24,128]{2,1,0:T(8,128)S(1)}, u32[]{:S(2)}, u32[]{:S(2)}) %collective-permute-start.6) | collective-permute-done | bytes 122912 | tf_op jit(solution)/shard_map/ppermute | solution.py:20
  29.2 1.3 %descend1.1 = (f32[4,16,128]{2,1,0:T(8,128)S(1)}, f32[8,3,8,128]{3,2,1,0:T(8,128)}, f32[12,32,128]{2,1,0:T(8,128)S(1)}, f32[12,32,128]{2,1,0:T(8,128)S(1)}, f32[12,32,128]{2,1,0:T(8,128)S(1)}) custom-call(f32[4,24,128]{2,1,0:T(8,128)S(1)} %get-tuple-element.60.g1, f32[4,24,128]{2,1,0:T(8,128)S(1)} %get-tuple-element.58.b1, ...), custom_call_target="tpu_custom_call" | custom-call | tf_op jit(solution)/shard_map/descend1/pallas_call | solution.py:700
  30.4 6.1 %all-to-all-start = ((f32[8,3,8,128]{3,2,1,0:T(8,128)}), f32[8,3,8,128]{3,2,1,0:T(8,128)S(1)}, u32[]{:S(2)}, u32[]{:S(2)}) async-start(f32[8,3,8,128]{3,2,1,0:T(8,128)} %get-tuple-element.64), calls=%async_computation | async-start | bytes 196608 | tf_op jit(solution)/shard_map/all_to_all | solution.py:748
  36.6 2.1 %collective-permute-start.8 = (f32[38,8,128]{2,1,0:T(8,128)S(1)}, f32[38,8,128]{2,1,0:T(8,128)S(1)}, u32[]{:S(2)}, u32[]{:S(2)}) collective-permute-start(f32[38,8,128]{2,1,0:T(8,128)S(1)} %get-tuple-element.67), channel_id=1, source_target_pairs={{0,32},{32,64},{64,96},{96,128},{128,160},{160,192},{192,224},{224... | collective-permute-start | bytes 466952 | tf_op jit(solution)/shard_map/ppermute | solution.py:20
  38.7 1.3 %collective-permute-start.9 = (f32[38,8,128]{2,1,0:T(8,128)S(1)}, f32[38,8,128]{2,1,0:T(8,128)S(1)}, u32[]{:S(2)}, u32[]{:S(2)}) collective-permute-start(f32[38,8,128]{2,1,0:T(8,128)S(1)} %get-tuple-element.68), channel_id=1, source_target_pairs={{0,224},{32,0},{64,32},{96,64},{128,96},{160,128},{192,160},{224,1... | collective-permute-start | bytes 466952 | tf_op jit(solution)/shard_map/ppermute | solution.py:20
  40.0 4.3 %collective-permute-done.8.below = f32[38,8,128]{2,1,0:T(8,128)S(1)} collective-permute-done((f32[38,8,128]{2,1,0:T(8,128)S(1)}, f32[38,8,128]{2,1,0:T(8,128)S(1)}, u32[]{:S(2)}, u32[]{:S(2)}) %collective-permute-start.8) | collective-permute-done | bytes 155680 | tf_op jit(solution)/shard_map/ppermute | solution.py:20
  44.2 0.9 %all-to-all-done.gathered = f32[8,3,8,128]{3,2,1,0:T(8,128)S(1)} async-done(((f32[8,3,8,128]{3,2,1,0:T(8,128)}), f32[8,3,8,128]{3,2,1,0:T(8,128)S(1)}, u32[]{:S(2)}, u32[]{:S(2)}) %all-to-all-start) | async-done | bytes 98336 | tf_op jit(solution)/shard_map/all_to_all | solution.py:748
  45.5 1.7 %collective-permute-start.11 = (f32[30,8,128]{2,1,0:T(8,128)S(1)}, f32[30,8,128]{2,1,0:T(8,128)S(1)}, u32[]{:S(2)}, u32[]{:S(2)}) collective-permute-start(f32[30,8,128]{2,1,0:T(8,128)S(1)} %get-tuple-element.70), channel_id=1, source_target_pairs={{0,31},{1,0},{2,1},{3,2},{4,3},{5,4},{6,5},{7,6},{8,7},{9,8},{10,9... | collective-permute-start | bytes 368648 | tf_op jit(solution)/shard_map/ppermute | solution.py:20
  47.2 2.6 %collective-permute-done.10.left.left1 = f32[30,8,128]{2,1,0:T(8,128)S(1)} collective-permute-done((f32[30,8,128]{2,1,0:T(8,128)S(1)}, f32[30,8,128]{2,1,0:T(8,128)S(1)}, u32[]{:S(2)}, u32[]{:S(2)}) %collective-permute-start.10) | collective-permute-done | bytes 122912 | tf_op jit(solution)/shard_map/ppermute | solution.py:20
  49.8 1.0 %descend2.1 = (f32[8,24,128]{2,1,0:T(8,128)S(1)}, f32[6,8,128]{2,1,0:T(8,128)S(1)}, f32[8,24,128]{2,1,0:T(8,128)S(1)}, f32[8,24,128]{2,1,0:T(8,128)S(1)}, f32[8,...) custom-call(f32[8,3,8,128]{3,2,1,0:T(8,128)S(1)} %all-to-all-done.gather, ...), custom_call_target="tpu_custom_call" | custom-call | tf_op jit(solution)/shard_map/descend2/pallas_call | solution.py:700
  50.8 5.4 %collective-permute-start.12 = (f32[6,8,128]{2,1,0:T(8,128)S(1)}, f32[6,8,128]{2,1,0:T(8,128)S(1)}, u32[]{:S(2)}, u32[]{:S(2)}) collective-permute-start(f32[6,8,128]{2,1,0:T(8,128)S(1)} %get-tuple-element.71.own3), channel_id=1, source_target_pairs={{0,2},{1,3},{4,6},{5,7},{8,10},{9,11},{12,14},{13,15},{16,18},{17,... | collective-permute-start | bytes 73736 | tf_op jit(solution)/shard_map/ppermute | solution.py:32
  56.2 1.1 %prepare.1 = (f32[16,40,256]{2,1,0:T(8,128)S(1)}, f32[16,40,256]{2,1,0:T(8,128)S(1)}, f32[16,40,256]{2,1,0:T(8,128)S(1)}, f32[16,40,256]{2,1,0:T(8,128)S(1)}, f3...) custom-call(f32[8,32,256]{2,1,0:T(8,128)S(1)} %get-tuple-element.49., ...), custom_call_target="tpu_custom_call" | custom-call | tf_op jit(solution)/shard_map/prepare/pallas_call | solution.py:700
  57.2 0.7 %collective-permute-done.12.r0 = f32[6,8,128]{2,1,0:T(8,128)S(1)} collective-permute-done((f32[6,8,128]{2,1,0:T(8,128)S(1)}, f32[6,8,128]{2,1,0:T(8,128)S(1)}, u32[]{:S(2)}, u32[]{:S(2)}) %collective-permute-start.12) | collective-permute-done | bytes 24608 | tf_op jit(solution)/shard_map/ppermute | solution.py:32
  58.0 2.0 %collective-permute-done.13.r1 = f32[6,8,128]{2,1,0:T(8,128)S(1)} collective-permute-done((f32[6,8,128]{2,1,0:T(8,128)S(1)}, f32[6,8,128]{2,1,0:T(8,128)S(1)}, u32[]{:S(2)}, u32[]{:S(2)}) %collective-permute-start.13) | collective-permute-done | bytes 24608 | tf_op jit(solution)/shard_map/ppermute | solution.py:32
  60.0 4.0 %ascend.1 = (f32[8,32,256]{2,1,0:T(8,128)}, f32[8,32,256]{2,1,0:T(8,128)}) custom-call(f32[6,8,128]{2,1,0:T(8,128)S(1)} %get-tuple-element.71.own3, f32[6,8,128]{2,1,0:T(8,128)S(1)} %collective-permute-done.12.r0, f32[6,8,128]{2,1,0:T(8,128)S(1)} %collective-permute-done.13.r1, f32[8,24,128]{2,1,0:T(8,128)S(1)} %get-tuple-element.72.v2, ...), custom_call_target="tpu_custom_call" | custom-call | tf_op jit(solution)/shard_map/ascend/pallas_call | solution.py:700
  (17 shorter events, 1.3 us)
Async XLA Ops:
  1.8 7.9 %collective-permute-start.2 = (f32[54,8,128]{2,1,0:T(8,128)S(1)}, f32[54,8,128]{2,1,0:T(8,128)S(1)}, u32[]{:S(2)}, u32[]{:S(2)}) collective-permute-start(f32[54,8,128]{2,1,0:T(8,128)S(1)} %get-tuple-element.54), channel_id=1, source_target_pairs={{0,1},{1,2},{2,3},{3,4},{4,5},{5,6},{6,7},{7,8},{8,9},{9,10},{10,1... | collective-permute-start | bytes 663560 | tf_op jit(solution)/shard_map/ppermute | solution.py:20
  1.9 7.8 %collective-permute-start.3 = (f32[54,8,128]{2,1,0:T(8,128)S(1)}, f32[54,8,128]{2,1,0:T(8,128)S(1)}, u32[]{:S(2)}, u32[]{:S(2)}) collective-permute-start(f32[54,8,128]{2,1,0:T(8,128)S(1)} %get-tuple-element.55), channel_id=1, source_target_pairs={{0,31},{1,0},{2,1},{3,2},{4,3},{5,4},{6,5},{7,6},{8,7},{9,8},{10,9... | collective-permute-start | bytes 663560 | tf_op jit(solution)/shard_map/ppermute | solution.py:20
  3.7 13.6 %collective-permute-start = (f32[9,32,256]{2,1,0:T(8,128)S(1)}, f32[9,32,256]{2,1,0:T(8,128)S(1)}, u32[]{:S(2)}, u32[]{:S(2)}) collective-permute-start(f32[9,32,256]{2,1,0:T(8,128)S(1)} %get-tuple-element.52), channel_id=1, source_target_pairs={{0,32},{32,64},{64,96},{96,128},{128,160},{160,192},{192,224},{224... | collective-permute-start | bytes 884744 | tf_op jit(solution)/shard_map/ppermute | solution.py:20
  5.7 11.6 %collective-permute-start.1 = (f32[9,32,256]{2,1,0:T(8,128)S(1)}, f32[9,32,256]{2,1,0:T(8,128)S(1)}, u32[]{:S(2)}, u32[]{:S(2)}) collective-permute-start(f32[9,32,256]{2,1,0:T(8,128)S(1)} %get-tuple-element.53), channel_id=1, source_target_pairs={{0,224},{32,0},{64,32},{96,64},{128,96},{160,128},{192,160},{224,1... | collective-permute-start | bytes 884744 | tf_op jit(solution)/shard_map/ppermute | solution.py:20
  9.7 10.2 %collective-permute-start.4 = (f32[37,8,128]{2,1,0:T(8,128)S(1)}, f32[37,8,128]{2,1,0:T(8,128)S(1)}, u32[]{:S(2)}, u32[]{:S(2)}) collective-permute-start(f32[37,8,128]{2,1,0:T(8,128)S(1)} %get-tuple-element.56), channel_id=1, source_target_pairs={{0,32},{32,64},{64,96},{96,128},{128,160},{160,192},{192,224},{224... | collective-permute-start | bytes 454664 | tf_op jit(solution)/shard_map/ppermute | solution.py:20
  9.8 10.1 %collective-permute-start.5 = (f32[37,8,128]{2,1,0:T(8,128)S(1)}, f32[37,8,128]{2,1,0:T(8,128)S(1)}, u32[]{:S(2)}, u32[]{:S(2)}) collective-permute-start(f32[37,8,128]{2,1,0:T(8,128)S(1)} %get-tuple-element.57), channel_id=1, source_target_pairs={{0,224},{32,0},{64,32},{96,64},{128,96},{160,128},{192,160},{224,1... | collective-permute-start | bytes 454664 | tf_op jit(solution)/shard_map/ppermute | solution.py:20
  23.0 6.2 %collective-permute-start.6 = (f32[10,24,128]{2,1,0:T(8,128)S(1)}, f32[10,24,128]{2,1,0:T(8,128)S(1)}, u32[]{:S(2)}, u32[]{:S(2)}) collective-permute-start(f32[10,24,128]{2,1,0:T(8,128)S(1)} %get-tuple-element.62), channel_id=1, source_target_pairs={{0,32},{32,64},{64,96},{96,128},{128,160},{160,192},{192,224},{224... | collective-permute-start | bytes 368648 | tf_op jit(solution)/shard_map/ppermute | solution.py:20
  23.1 6.1 %collective-permute-start.7 = (f32[10,24,128]{2,1,0:T(8,128)S(1)}, f32[10,24,128]{2,1,0:T(8,128)S(1)}, u32[]{:S(2)}, u32[]{:S(2)}) collective-permute-start(f32[10,24,128]{2,1,0:T(8,128)S(1)} %get-tuple-element.63), channel_id=1, source_target_pairs={{0,224},{32,0},{64,32},{96,64},{128,96},{160,128},{192,160},{224,1... | collective-permute-start | bytes 368648 | tf_op jit(solution)/shard_map/ppermute | solution.py:20
  30.4 14.8 %all-to-all-start = ((f32[8,3,8,128]{3,2,1,0:T(8,128)}), f32[8,3,8,128]{3,2,1,0:T(8,128)S(1)}, u32[]{:S(2)}, u32[]{:S(2)}) async-start(f32[8,3,8,128]{3,2,1,0:T(8,128)} %get-tuple-element.64), calls=%async_computation | async-start | bytes 196608 | tf_op jit(solution)/shard_map/all_to_all | solution.py:748
  36.6 7.7 %collective-permute-start.8 = (f32[38,8,128]{2,1,0:T(8,128)S(1)}, f32[38,8,128]{2,1,0:T(8,128)S(1)}, u32[]{:S(2)}, u32[]{:S(2)}) collective-permute-start(f32[38,8,128]{2,1,0:T(8,128)S(1)} %get-tuple-element.67), channel_id=1, source_target_pairs={{0,32},{32,64},{64,96},{96,128},{128,160},{160,192},{192,224},{224... | collective-permute-start | bytes 466952 | tf_op jit(solution)/shard_map/ppermute | solution.py:20
  38.7 5.6 %collective-permute-start.9 = (f32[38,8,128]{2,1,0:T(8,128)S(1)}, f32[38,8,128]{2,1,0:T(8,128)S(1)}, u32[]{:S(2)}, u32[]{:S(2)}) collective-permute-start(f32[38,8,128]{2,1,0:T(8,128)S(1)} %get-tuple-element.68), channel_id=1, source_target_pairs={{0,224},{32,0},{64,32},{96,64},{128,96},{160,128},{192,160},{224,1... | collective-permute-start | bytes 466952 | tf_op jit(solution)/shard_map/ppermute | solution.py:20
  45.2 4.6 %collective-permute-start.10 = (f32[30,8,128]{2,1,0:T(8,128)S(1)}, f32[30,8,128]{2,1,0:T(8,128)S(1)}, u32[]{:S(2)}, u32[]{:S(2)}) collective-permute-start(f32[30,8,128]{2,1,0:T(8,128)S(1)} %get-tuple-element.69), channel_id=1, source_target_pairs={{0,1},{1,2},{2,3},{3,4},{4,5},{5,6},{6,7},{7,8},{8,9},{9,10},{10,1... | collective-permute-start | bytes 368648 | tf_op jit(solution)/shard_map/ppermute | solution.py:20
  45.5 4.3 %collective-permute-start.11 = (f32[30,8,128]{2,1,0:T(8,128)S(1)}, f32[30,8,128]{2,1,0:T(8,128)S(1)}, u32[]{:S(2)}, u32[]{:S(2)}) collective-permute-start(f32[30,8,128]{2,1,0:T(8,128)S(1)} %get-tuple-element.70), channel_id=1, source_target_pairs={{0,31},{1,0},{2,1},{3,2},{4,3},{5,4},{6,5},{7,6},{8,7},{9,8},{10,9... | collective-permute-start | bytes 368648 | tf_op jit(solution)/shard_map/ppermute | solution.py:20
  50.8 7.2 %collective-permute-start.12 = (f32[6,8,128]{2,1,0:T(8,128)S(1)}, f32[6,8,128]{2,1,0:T(8,128)S(1)}, u32[]{:S(2)}, u32[]{:S(2)}) collective-permute-start(f32[6,8,128]{2,1,0:T(8,128)S(1)} %get-tuple-element.71.own3), channel_id=1, source_target_pairs={{0,2},{1,3},{4,6},{5,7},{8,10},{9,11},{12,14},{13,15},{16,18},{17,... | collective-permute-start | bytes 73736 | tf_op jit(solution)/shard_map/ppermute | solution.py:32
  56.2 3.8 %collective-permute-start.13 = (f32[6,8,128]{2,1,0:T(8,128)S(1)}, f32[6,8,128]{2,1,0:T(8,128)S(1)}, u32[]{:S(2)}, u32[]{:S(2)}) collective-permute-start(f32[6,8,128]{2,1,0:T(8,128)S(1)} %get-tuple-element.71.own3), channel_id=1, source_target_pairs={{0,1},{2,4},{3,5},{6,8},{7,9},{10,12},{11,13},{14,16},{15,17},{18,... | collective-permute-start | bytes 73736 | tf_op jit(solution)/shard_map/ppermute | solution.py:32
